TPU v7x, 32 devices: a whole 2x2x4 slice. The times are simulated.
32 devices in a mesh: dp: 16 (over z, y, x), tensor: 2 (over core).
Axes of the slice: x: 2, y: 2, z: 4, core: 2. Of those that a mesh axis runs over, the one named last changes fastest.
Arguments:
- images: bfloat16 [16, 16, 16, 1024], P('dp'), may hold values from -4 to 4
- t_index: int32 [16], P('dp'), may hold values from 0 to 999
- cotangent: bfloat16 [16, 64, 2048], P('dp'), may hold values from -4 to 4
- norm_params: float32 [2, 1024], P(None, 'dp'), may hold values from -1 to 1.6
- norm_params_avg: float32 [2, 1024], P(None, 'dp'), may hold values from -0.0004272461 to 0.0004272461
- norm_params_sq: float32 [2, 1024], P(None, 'dp'), may hold values from 5.615713e-09 to 2.2462851e-08
- first_conv: float32 [3, 3, 1024, 1024], P(None, None, 'dp', 'tensor'), may hold values from -0.0625 to 0.0625
- first_conv_avg: float32 [3, 3, 1024, 1024], P(None, None, 'dp', 'tensor'), may hold values from -0.00061035156 to 0.00061035156
- first_conv_sq: float32 [3, 3, 1024, 1024], P(None, None, 'dp', 'tensor'), may hold values from 1.0766219e-08 to 4.3064876e-08
- resnet_mod: float32 [256, 2, 1024], P('dp', None, 'tensor'), may hold values from -0.1875 to 0.1875
- resnet_mod_avg: float32 [256, 2, 1024], P('dp', None, 'tensor'), may hold values from -0.0004272461 to 0.0004272461
- resnet_mod_sq: float32 [256, 2, 1024], P('dp', None, 'tensor'), may hold values from 5.615713e-09 to 2.2462851e-08
- second_conv: float32 [3, 3, 1024, 1024], P(None, None, 'tensor', 'dp'), may hold values from -0.0625 to 0.0625
- second_kernel_first_moment: float32 [3, 3, 1024, 1024], P(None, None, 'tensor', 'dp'), may hold values from -0.0008544922 to 0.0008544922
- second_conv_sq: float32 [3, 3, 1024, 1024], P(None, None, 'tensor', 'dp'), may hold values from 1.7578179e-08 to 7.0312716e-08
- down_conv: float32 [3, 3, 1024, 2048], P(None, None, 'dp', 'tensor'), may hold values from -0.0625 to 0.0625
- down_conv_avg: float32 [3, 3, 1024, 2048], P(None, None, 'dp', 'tensor'), may hold values from -0.0009765625 to 0.0009765625
- down_conv_sq: float32 [3, 3, 1024, 2048], P(None, None, 'dp', 'tensor'), may hold values from 2.9906165e-08 to 1.1962466e-07
- ada_proj: float32 [256, 6, 2048], P('dp'), may hold values from -0.1875 to 0.1875
- ada_proj_avg: float32 [256, 6, 2048], P('dp'), may hold values from -0.0004272461 to 0.0004272461
- ada_proj_sq: float32 [256, 6, 2048], P('dp'), may hold values from 4.784986e-09 to 1.9139945e-08
- qkv_proj: float32 [2048, 3, 16, 128], P('dp', None, 'tensor'), may hold values from -0.125 to 0.125
- qkv_proj_avg: float32 [2048, 3, 16, 128], P('dp', None, 'tensor'), may hold values from -0.00048828125 to 0.00048828125
- qkv_proj_sq: float32 [2048, 3, 16, 128], P('dp', None, 'tensor'), may hold values from 7.476541e-09 to 2.9906165e-08
- out_proj: float32 [16, 128, 2048], P('tensor', None, 'dp'), may hold values from -0.75 to 0.75
- out_proj_avg: float32 [16, 128, 2048], P('tensor', None, 'dp'), may hold values from -7.6293945e-05 to 7.6293945e-05
- out_proj_sq: float32 [16, 128, 2048], P('tensor', None, 'dp'), may hold values from 1.9139944e-10 to 7.6559775e-10
- hidden_in: float32 [2048, 8192], P('dp', 'tensor'), may hold values from -0.125 to 0.125
- hidden_in_avg: float32 [2048, 8192], P('dp', 'tensor'), may hold values from -0.00018310547 to 0.00018310547
- hidden_in_sq: float32 [2048, 8192], P('dp', 'tensor'), may hold values from 8.3072677e-10 to 3.322907e-09
- hidden_out: float32 [8192, 2048], P('tensor', 'dp'), may hold values from -0.0625 to 0.0625
- hidden_out_avg: float32 [8192, 2048], P('tensor', 'dp'), may hold values from -0.00024414062 to 0.00024414062
- hidden_out_sq: float32 [8192, 2048], P('tensor', 'dp'), may hold values from 1.9701516e-09 to 7.880606e-09
Outputs:
- block_out: bfloat16 [16, 64, 2048], P('dp')
- images_grad: float32 [16, 16, 16, 1024], P('dp')
- grad_norm: float32 [1], replicated
- new_norm_params: float32 [2, 1024], P(None, 'dp')
- new_norm_params_avg: float32 [2, 1024], P(None, 'dp')
- new_norm_params_sq: float32 [2, 1024], P(None, 'dp')
- new_first_conv: float32 [3, 3, 1024, 1024], P(None, None, 'dp', 'tensor')
- new_first_conv_avg: float32 [3, 3, 1024, 1024], P(None, None, 'dp', 'tensor')
- new_first_conv_sq: float32 [3, 3, 1024, 1024], P(None, None, 'dp', 'tensor')
- new_resnet_mod: float32 [256, 2, 1024], P('dp', None, 'tensor')
- new_resnet_mod_avg: float32 [256, 2, 1024], P('dp', None, 'tensor')
- new_resnet_mod_sq: float32 [256, 2, 1024], P('dp', None, 'tensor')
- new_second_conv: float32 [3, 3, 1024, 1024], P(None, None, 'tensor', 'dp')
- new_second_conv_avg: float32 [3, 3, 1024, 1024], P(None, None, 'tensor', 'dp')
- new_second_conv_sq: float32 [3, 3, 1024, 1024], P(None, None, 'tensor', 'dp')
- new_down_conv: float32 [3, 3, 1024, 2048], P(None, None, 'dp', 'tensor')
- new_down_conv_avg: float32 [3, 3, 1024, 2048], P(None, None, 'dp', 'tensor')
- new_down_conv_sq: float32 [3, 3, 1024, 2048], P(None, None, 'dp', 'tensor')
- new_ada_proj: float32 [256, 6, 2048], P('dp')
- new_ada_proj_avg: float32 [256, 6, 2048], P('dp')
- new_ada_proj_sq: float32 [256, 6, 2048], P('dp')
- new_qkv_proj: float32 [2048, 3, 16, 128], P('dp', None, 'tensor')
- new_qkv_proj_avg: float32 [2048, 3, 16, 128], P('dp', None, 'tensor')
- new_qkv_proj_sq: float32 [2048, 3, 16, 128], P('dp', None, 'tensor')
- new_out_proj: float32 [16, 128, 2048], P('tensor', None, 'dp')
- new_out_proj_avg: float32 [16, 128, 2048], P('tensor', None, 'dp')
- new_out_proj_sq: float32 [16, 128, 2048], P('tensor', None, 'dp')
- new_hidden_in: float32 [2048, 8192], P('dp', 'tensor')
- new_hidden_in_avg: float32 [2048, 8192], P('dp', 'tensor')
- new_hidden_in_sq: float32 [2048, 8192], P('dp', 'tensor')
- new_hidden_out: float32 [8192, 2048], P('tensor', 'dp')
- new_hidden_out_avg: float32 [8192, 2048], P('tensor', 'dp')
- new_hidden_out_sq: float32 [8192, 2048], P('tensor', 'dp')
All inputs are finite; a program needn't handle non-finite values.
Results may differ from a plain program's by a relative error of at most 0.035.
Values may be sent and summed in bfloat16 or wider, within the bound.
A program may use at most 448 MiB of HBM per device.

v0:
```python
import math

import jax
import jax.numpy as jnp
from jax import lax
from jax.sharding import PartitionSpec as P

C = 1024
D = 2048
HEADS = 16
HDIM = 128
FF = 8192
GROUPS = 32
FREQ = 256
STEP = 5


GN_EPS = 1e-05
LN_EPS = 1e-06
CLIP = 1.0
BETA_ONE = 0.5
BETA_TWO = 0.5
ADAM_EPS = 1e-08
DECAY = 0.1
LR_SCALE = 2.0
LR_NORM = 0.5
PLAN = 1000.0
HIGHEST = lax.Precision.HIGHEST


def embed_noise(t_index, emb_width):
    fraction = (t_index.astype(jnp.float32) + 0.5) / PLAN
    logsnr = -2.0 * jnp.log(jnp.tan(0.5 * math.pi * fraction)) + 2.0 * math.log(64.0 / 512.0)
    half_width = emb_width // 2
    frequencies = jnp.exp(
        -math.log(10000.0) * jnp.arange(half_width, dtype=jnp.float32) / half_width
    )
    angles = logsnr[:, None] * frequencies[None, :]
    return jnp.concatenate([jnp.sin(angles), jnp.cos(angles)], axis=1)


def group_norm(values, group_size):
    dims_of = values.shape
    grouped = values.reshape(dims_of[:-1] + (dims_of[-1] // group_size, group_size))
    center = jnp.mean(grouped, axis=(1, 2, 4), keepdims=True)
    shifted = grouped - center
    spread = jnp.mean(shifted * shifted, axis=(1, 2, 4), keepdims=True)
    return (shifted * lax.rsqrt(spread + GN_EPS)).reshape(dims_of)


def layer_norm(values):
    center = jnp.mean(values, axis=-1, keepdims=True)
    shifted = values - center
    spread = jnp.mean(shifted * shifted, axis=-1, keepdims=True)
    return shifted * lax.rsqrt(spread + LN_EPS)


def leading_segment(picture, gain_bias):
    return jax.nn.silu(group_norm(picture, C // GROUPS) * gain_bias[0] + gain_bias[1])


def second_piece(middle, res_mods):
    return jax.nn.silu(
        group_norm(middle, C // GROUPS) * (1.0 + res_mods[:, None, None, 0])
        + res_mods[:, None, None, 1]
    )


def modulate(tokens, shift_scale):
    return layer_norm(tokens) * (1.0 + shift_scale[:, None, 1]) + shift_scale[:, None, 0]


def gelu_tanh(values):
    return jax.nn.gelu(values, approximate=True)


def conv_same(inputs, kernel):
    height, breadth = (inputs.shape[1], inputs.shape[2])
    padded = jnp.pad(inputs, ((0, 0), (1, 1), (1, 1), (0, 0)))
    summed_taps = jnp.zeros(inputs.shape[:3] + (kernel.shape[3],), jnp.float32)
    for row_tap in range(3):
        for col_tap in range(3):
            window = padded[:, row_tap : row_tap + height, col_tap : col_tap + breadth]
            summed_taps = summed_taps + jnp.einsum(
                "bhwc,cd->bhwd",
                window,
                kernel[row_tap, col_tap],
                preferred_element_type=jnp.float32,
            )
    return summed_taps


def conv_same_input(upstream, kernel):
    height, breadth = (upstream.shape[1], upstream.shape[2])
    padded = jnp.pad(upstream, ((0, 0), (1, 1), (1, 1), (0, 0)))
    summed_taps = jnp.zeros(upstream.shape[:3] + (kernel.shape[2],), jnp.float32)
    for row_tap in range(3):
        for col_tap in range(3):
            window = padded[
                :, 2 - row_tap : 2 - row_tap + height, 2 - col_tap : 2 - col_tap + breadth
            ]
            summed_taps = summed_taps + jnp.einsum(
                "bhwd,cd->bhwc",
                window,
                kernel[row_tap, col_tap],
                preferred_element_type=jnp.float32,
            )
    return summed_taps


def conv_same_kernel(inputs, upstream):
    height, breadth = (inputs.shape[1], inputs.shape[2])
    padded = jnp.pad(inputs, ((0, 0), (1, 1), (1, 1), (0, 0)))
    tap_list = []
    for row_tap in range(3):
        for col_tap in range(3):
            window = padded[:, row_tap : row_tap + height, col_tap : col_tap + breadth]
            tap_list.append(
                jnp.einsum("bhwc,bhwd->cd", window, upstream, preferred_element_type=jnp.float32)
            )
    return jnp.stack(tap_list).reshape(3, 3, inputs.shape[3], upstream.shape[3])


def conv_down(inputs, kernel):
    height, breadth = (inputs.shape[1], inputs.shape[2])
    padded = jnp.pad(inputs, ((0, 0), (1, 1), (1, 1), (0, 0)))
    summed_taps = jnp.zeros(
        (inputs.shape[0], height // 2, breadth // 2, kernel.shape[3]), jnp.float32
    )
    for row_tap in range(3):
        for col_tap in range(3):
            window = padded[:, row_tap : row_tap + height : 2, col_tap : col_tap + breadth : 2]
            summed_taps = summed_taps + jnp.einsum(
                "bhwc,cd->bhwd",
                window,
                kernel[row_tap, col_tap],
                preferred_element_type=jnp.float32,
            )
    return summed_taps


def conv_down_input(upstream, kernel, height, breadth):
    summed_taps = jnp.zeros(
        (upstream.shape[0], height + 2, breadth + 2, kernel.shape[2]), jnp.float32
    )
    for row_tap in range(3):
        for col_tap in range(3):
            spread_out = jnp.einsum(
                "bhwd,cd->bhwc",
                upstream,
                kernel[row_tap, col_tap],
                preferred_element_type=jnp.float32,
            )
            placed = lax.pad(
                spread_out,
                jnp.float32(0.0),
                ((0, 0, 0), (row_tap, 3 - row_tap, 1), (col_tap, 3 - col_tap, 1), (0, 0, 0)),
            )
            summed_taps = summed_taps + placed
    return summed_taps[:, 1 : height + 1, 1 : breadth + 1]


def conv_down_kernel(inputs, upstream):
    height, breadth = (inputs.shape[1], inputs.shape[2])
    padded = jnp.pad(inputs, ((0, 0), (1, 1), (1, 1), (0, 0)))
    tap_list = []
    for row_tap in range(3):
        for col_tap in range(3):
            window = padded[:, row_tap : row_tap + height : 2, col_tap : col_tap + breadth : 2]
            tap_list.append(
                jnp.einsum("bhwc,bhwd->cd", window, upstream, preferred_element_type=jnp.float32)
            )
    return jnp.stack(tap_list).reshape(3, 3, inputs.shape[3], upstream.shape[3])


def per_device(
    images,
    t_index,
    cotangent,
    norm_params,
    norm_params_avg,
    norm_params_sq,
    first_conv,
    first_conv_avg,
    first_conv_sq,
    resnet_mod,
    resnet_mod_avg,
    resnet_mod_sq,
    second_conv,
    second_kernel_first_moment,
    second_conv_sq,
    down_conv,
    down_conv_avg,
    down_conv_sq,
    ada_proj,
    ada_proj_avg,
    ada_proj_sq,
    qkv_proj,
    qkv_proj_avg,
    qkv_proj_sq,
    out_proj,
    out_proj_avg,
    out_proj_sq,
    hidden_in,
    hidden_in_avg,
    hidden_in_sq,
    hidden_out,
    hidden_out_avg,
    hidden_out_sq,
):
    masters = (
        norm_params,
        first_conv,
        resnet_mod,
        second_conv,
        down_conv,
        ada_proj,
        qkv_proj,
        out_proj,
        hidden_in,
        hidden_out,
    )
    averages = (
        norm_params_avg,
        first_conv_avg,
        resnet_mod_avg,
        second_kernel_first_moment,
        down_conv_avg,
        ada_proj_avg,
        qkv_proj_avg,
        out_proj_avg,
        hidden_in_avg,
        hidden_out_avg,
    )
    squares = (
        norm_params_sq,
        first_conv_sq,
        resnet_mod_sq,
        second_conv_sq,
        down_conv_sq,
        ada_proj_sq,
        qkv_proj_sq,
        out_proj_sq,
        hidden_in_sq,
        hidden_out_sq,
    )
    lowered = tuple((master.astype(jnp.bfloat16) for master in masters))
    gathered = (
        lax.all_gather(lowered[0], "dp", axis=1, tiled=True),
        lax.all_gather(lowered[1], "dp", axis=2, tiled=True),
        lax.all_gather(lowered[2], "dp", axis=0, tiled=True),
        lax.all_gather(lowered[3], "dp", axis=3, tiled=True),
        lax.all_gather(lowered[4], "dp", axis=2, tiled=True),
        lax.all_gather(lowered[5], "dp", axis=0, tiled=True),
        lax.all_gather(lowered[6], "dp", axis=0, tiled=True),
        lax.all_gather(lowered[7], "dp", axis=2, tiled=True),
        lax.all_gather(lowered[8], "dp", axis=0, tiled=True),
        lax.all_gather(lowered[9], "dp", axis=1, tiled=True),
    )
    (
        gain_bias,
        conv_one,
        res_table,
        conv_two,
        conv_half,
        ada_table,
        qkv_full,
        out_full,
        up_full,
        down_full,
    ) = gathered
    batch_size = images.shape[0]
    height, breadth = (images.shape[1], images.shape[2])
    local_c = conv_one.shape[3]
    local_d = conv_half.shape[3]
    heads_here = qkv_full.shape[2]
    tokens_len = height // 2 * (breadth // 2)
    tensor_pos = lax.axis_index("tensor")
    n_tensor = lax.axis_size("tensor")
    score_scale = HDIM ** (-0.5)
    noise_emb = embed_noise(t_index, FREQ)
    emb_low = noise_emb.astype(jnp.bfloat16)
    emb_back = emb_low.astype(jnp.float32)
    res_mods = jnp.dot(
        emb_low, res_table.reshape(FREQ, 2 * local_c), preferred_element_type=jnp.float32
    ).reshape(batch_size, 2, local_c)
    ada_mods = jnp.dot(
        emb_low, ada_table.reshape(FREQ, 6 * D), preferred_element_type=jnp.float32
    ).reshape(batch_size, 6, D)
    image_float = images.astype(jnp.float32)
    gain_float = gain_bias.astype(jnp.float32)
    act_one, first_back = jax.vjp(leading_segment, image_float, gain_float)
    act_one = act_one.astype(jnp.bfloat16)
    middle = conv_same(act_one, conv_one)
    act_two, second_back = jax.vjp(second_piece, middle, res_mods)
    act_two = act_two.astype(jnp.bfloat16)
    branch = lax.psum(conv_same(act_two, conv_two).astype(jnp.bfloat16), "tensor").astype(
        jnp.float32
    )
    residual = image_float + branch
    resid_low = residual.astype(jnp.bfloat16)
    shrunk = conv_down(resid_low, conv_half)
    pieces = lax.all_gather(shrunk.astype(jnp.bfloat16), "tensor", axis=3, tiled=True).astype(
        shrunk.dtype
    )
    tokens = pieces.reshape(batch_size, tokens_len, D)
    attn_in, attn_back = jax.vjp(modulate, tokens, ada_mods[:, 0:2])
    attn_low = attn_in.astype(jnp.bfloat16).reshape(batch_size * tokens_len, D)
    qkv_low = jnp.dot(
        attn_low, qkv_full.reshape(D, 3 * heads_here * HDIM), preferred_element_type=jnp.float32
    ).astype(jnp.bfloat16)
    qkv_low = qkv_low.reshape(batch_size, tokens_len, 3, heads_here, HDIM)
    query_low, key_low, value_low = (qkv_low[:, :, 0], qkv_low[:, :, 1], qkv_low[:, :, 2])
    scores = (
        jnp.einsum("bqhd,bkhd->bhqk", query_low, key_low, preferred_element_type=jnp.float32)
        * score_scale
    )
    row_max = jnp.max(scores, axis=-1, keepdims=True)
    log_total = row_max + jnp.log(jnp.sum(jnp.exp(scores - row_max), axis=-1, keepdims=True))
    attention_low = jnp.exp(scores - log_total).astype(jnp.bfloat16)
    mixed = jnp.einsum(
        "bhqk,bkhd->bqhd", attention_low, value_low, preferred_element_type=jnp.float32
    ).astype(jnp.bfloat16)
    mixed = mixed.reshape(batch_size * tokens_len, heads_here * HDIM)
    out_flat = out_full.reshape(heads_here * HDIM, D)
    attended = (
        lax.psum(
            jnp.dot(mixed, out_flat, preferred_element_type=jnp.float32).astype(jnp.bfloat16),
            "tensor",
        )
        .astype(jnp.float32)
        .reshape(batch_size, tokens_len, D)
    )
    gate_one = 1.0 + ada_mods[:, None, 2]
    after_attn = tokens + gate_one * attended
    mlp_in, mlp_back = jax.vjp(modulate, after_attn, ada_mods[:, 3:5])
    mlp_low = mlp_in.astype(jnp.bfloat16).reshape(batch_size * tokens_len, D)
    pre_act = jnp.dot(mlp_low, up_full, preferred_element_type=jnp.float32)
    hidden_act, gelu_back = jax.vjp(gelu_tanh, pre_act)
    hidden_low = hidden_act.astype(jnp.bfloat16)
    expanded = (
        lax.psum(
            jnp.dot(hidden_low, down_full, preferred_element_type=jnp.float32).astype(jnp.bfloat16),
            "tensor",
        )
        .astype(jnp.float32)
        .reshape(batch_size, tokens_len, D)
    )
    gate_two = 1.0 + ada_mods[:, None, 5]
    block_out = (after_attn + gate_two * expanded).astype(jnp.bfloat16)
    upstream = cotangent.astype(jnp.float32)
    grad_expanded = (gate_two * upstream).astype(jnp.bfloat16).reshape(batch_size * tokens_len, D)
    grad_gate_two = jnp.sum(upstream * expanded, axis=1)
    grad_down = jnp.einsum(
        "tf,td->fd", hidden_low, grad_expanded, preferred_element_type=jnp.float32
    )
    grad_hidden = jnp.einsum(
        "td,fd->tf", grad_expanded, down_full, preferred_element_type=jnp.float32
    )
    (grad_pre,) = gelu_back(grad_hidden)
    grad_pre_low = grad_pre.astype(jnp.bfloat16)
    grad_mlp_in = (
        lax.psum(
            jnp.einsum(
                "tf,df->td", grad_pre_low, up_full, preferred_element_type=jnp.float32
            ).astype(jnp.bfloat16),
            "tensor",
        )
        .astype(jnp.float32)
        .reshape(batch_size, tokens_len, D)
    )
    grad_after_norm, grad_mods_two = mlp_back(grad_mlp_in)
    grad_after = upstream + grad_after_norm
    grad_attended = (gate_one * grad_after).astype(jnp.bfloat16).reshape(batch_size * tokens_len, D)
    grad_gate_one = jnp.sum(grad_after * attended, axis=1)
    grad_out = jnp.einsum("tk,td->kd", mixed, grad_attended, preferred_element_type=jnp.float32)
    grad_mixed = jnp.einsum(
        "td,kd->tk", grad_attended, out_flat, preferred_element_type=jnp.float32
    ).astype(jnp.bfloat16)
    grad_mixed = grad_mixed.reshape(batch_size, tokens_len, heads_here, HDIM)
    scores = (
        jnp.einsum("bqhd,bkhd->bhqk", query_low, key_low, preferred_element_type=jnp.float32)
        * score_scale
    )
    attention = jnp.exp(scores - log_total)
    attention_low = attention.astype(jnp.bfloat16)
    grad_probs = jnp.einsum(
        "bqhd,bkhd->bhqk", grad_mixed, value_low, preferred_element_type=jnp.float32
    )
    grad_values = jnp.einsum(
        "bhqk,bqhd->bkhd", attention_low, grad_mixed, preferred_element_type=jnp.float32
    )
    grad_scores = (
        attention * (grad_probs - jnp.sum(grad_probs * attention, axis=-1, keepdims=True))
    ).astype(jnp.bfloat16)
    query_gradient = (
        jnp.einsum("bhqk,bkhd->bqhd", grad_scores, key_low, preferred_element_type=jnp.float32)
        * score_scale
    )
    grad_keys = (
        jnp.einsum("bhqk,bqhd->bkhd", grad_scores, query_low, preferred_element_type=jnp.float32)
        * score_scale
    )
    grad_qkv = (
        jnp.stack([query_gradient, grad_keys, grad_values], axis=2)
        .astype(jnp.bfloat16)
        .reshape(batch_size * tokens_len, 3 * heads_here * HDIM)
    )
    grad_qkv_w = jnp.einsum(
        "td,tk->dk", attn_low, grad_qkv, preferred_element_type=jnp.float32
    ).reshape(D, 3, heads_here, HDIM)
    grad_attn_in = (
        lax.psum(
            jnp.einsum(
                "tk,dk->td",
                grad_qkv,
                qkv_full.reshape(D, 3 * heads_here * HDIM),
                preferred_element_type=jnp.float32,
            ).astype(jnp.bfloat16),
            "tensor",
        )
        .astype(jnp.float32)
        .reshape(batch_size, tokens_len, D)
    )
    grad_tokens_norm, grad_mods_one = attn_back(grad_attn_in)
    grad_tokens = grad_after + grad_tokens_norm
    grad_mods = jnp.concatenate(
        [grad_mods_one, grad_gate_one[:, None], grad_mods_two, grad_gate_two[:, None]], axis=1
    )
    adaptive_gradient = jnp.einsum(
        "bf,bk->fk", emb_back, grad_mods.reshape(batch_size, 6 * D), precision=HIGHEST
    ).reshape(FREQ, 6, D)
    grad_out_w = grad_out.reshape(heads_here, HDIM, D)
    grad_up = jnp.einsum("td,tf->df", mlp_low, grad_pre_low, preferred_element_type=jnp.float32)
    transformer_gradient_total = (
        lax.psum_scatter(adaptive_gradient, "dp", scatter_dimension=0, tiled=True),
        lax.psum_scatter(grad_qkv_w, "dp", scatter_dimension=0, tiled=True),
        lax.psum_scatter(grad_out_w, "dp", scatter_dimension=2, tiled=True),
        lax.psum_scatter(grad_up, "dp", scatter_dimension=0, tiled=True),
        lax.psum_scatter(grad_down, "dp", scatter_dimension=1, tiled=True),
    )
    grad_shrunk = lax.dynamic_slice_in_dim(
        grad_tokens.reshape(batch_size, height // 2, breadth // 2, D),
        tensor_pos * local_d,
        local_d,
        axis=3,
    ).astype(jnp.bfloat16)
    grad_half = conv_down_kernel(resid_low, grad_shrunk)
    grad_resid = lax.psum(
        conv_down_input(grad_shrunk, conv_half, height, breadth).astype(jnp.bfloat16), "tensor"
    ).astype(jnp.float32)
    grad_branch = grad_resid.astype(jnp.bfloat16)
    grad_conv_two = conv_same_kernel(act_two, grad_branch)
    grad_act_two = conv_same_input(grad_branch, conv_two)
    grad_middle, grad_res_mods = second_back(grad_act_two)
    grad_middle_low = grad_middle.astype(jnp.bfloat16)
    grad_conv_one = conv_same_kernel(act_one, grad_middle_low)
    grad_act_one = lax.psum(
        conv_same_input(grad_middle_low, conv_one).astype(jnp.bfloat16), "tensor"
    ).astype(jnp.float32)
    grad_image_norm, grad_gain = first_back(grad_act_one)
    images_grad = grad_resid + grad_image_norm
    grad_res_table = jnp.einsum(
        "bf,bk->fk", emb_back, grad_res_mods.reshape(batch_size, 2 * local_c), precision=HIGHEST
    ).reshape(FREQ, 2, local_c)
    resnet_gradient_total = (
        lax.psum_scatter(grad_gain, "dp", scatter_dimension=1, tiled=True),
        lax.psum_scatter(grad_conv_one, "dp", scatter_dimension=2, tiled=True),
        lax.psum_scatter(grad_res_table, "dp", scatter_dimension=0, tiled=True),
        lax.psum_scatter(grad_conv_two, "dp", scatter_dimension=3, tiled=True),
        lax.psum_scatter(grad_half, "dp", scatter_dimension=2, tiled=True),
    )
    combined_total = tuple(resnet_gradient_total) + tuple(transformer_gradient_total)
    local_sq = jnp.zeros((), jnp.float32)
    for position, reduced in enumerate(combined_total):
        shard_sq = jnp.sum(reduced * reduced)
        if position == 0 or position == 5:
            shard_sq = shard_sq / n_tensor
        local_sq = local_sq + shard_sq
    square_sum = lax.psum(local_sq, ("dp", "tensor"))
    grad_norm = jnp.sqrt(square_sum)
    factor = jnp.minimum(1.0, CLIP / (grad_norm + 1e-06))
    conv_rate = LR_SCALE * (9 * C) ** (-0.5)
    mod_rate = LR_SCALE * (4 * FREQ) ** (-0.5)
    rates = (
        LR_NORM,
        conv_rate,
        mod_rate,
        conv_rate,
        conv_rate,
        mod_rate,
        LR_SCALE * D ** (-0.5),
        LR_SCALE * (HEADS * HDIM // 32) ** (-0.5),
        LR_SCALE * D ** (-0.5),
        LR_SCALE * FF ** (-0.5),
    )
    correct_one = 1.0 - BETA_ONE**STEP
    correct_two = 1.0 - BETA_TWO**STEP
    results = []
    for master, average, square, reduced, learn_rate in zip(
        masters, averages, squares, combined_total, rates
    ):
        clipped = reduced * factor
        new_avg = BETA_ONE * average + (1.0 - BETA_ONE) * clipped
        new_sq = BETA_TWO * square + (1.0 - BETA_TWO) * clipped * clipped
        step_dir = new_avg / correct_one / (jnp.sqrt(new_sq / correct_two) + ADAM_EPS)
        new_master = master - learn_rate * (step_dir + DECAY * master)
        results += [new_master, new_avg, new_sq]
    return (block_out, images_grad, grad_norm.reshape(1)) + tuple(results)


def solution(mesh):
    in_specs = (
        P("dp", None, None, None),
        P("dp"),
        P("dp", None, None),
        P(None, "dp"),
        P(None, "dp"),
        P(None, "dp"),
        P(None, None, "dp", "tensor"),
        P(None, None, "dp", "tensor"),
        P(None, None, "dp", "tensor"),
        P("dp", None, "tensor"),
        P("dp", None, "tensor"),
        P("dp", None, "tensor"),
        P(None, None, "tensor", "dp"),
        P(None, None, "tensor", "dp"),
        P(None, None, "tensor", "dp"),
        P(None, None, "dp", "tensor"),
        P(None, None, "dp", "tensor"),
        P(None, None, "dp", "tensor"),
        P("dp", None, None),
        P("dp", None, None),
        P("dp", None, None),
        P("dp", None, "tensor", None),
        P("dp", None, "tensor", None),
        P("dp", None, "tensor", None),
        P("tensor", None, "dp"),
        P("tensor", None, "dp"),
        P("tensor", None, "dp"),
        P("dp", "tensor"),
        P("dp", "tensor"),
        P("dp", "tensor"),
        P("tensor", "dp"),
        P("tensor", "dp"),
        P("tensor", "dp"),
    )
    out_specs = (
        P("dp", None, None),
        P("dp", None, None, None),
        P(),
        P(None, "dp"),
        P(None, "dp"),
        P(None, "dp"),
        P(None, None, "dp", "tensor"),
        P(None, None, "dp", "tensor"),
        P(None, None, "dp", "tensor"),
        P("dp", None, "tensor"),
        P("dp", None, "tensor"),
        P("dp", None, "tensor"),
        P(None, None, "tensor", "dp"),
        P(None, None, "tensor", "dp"),
        P(None, None, "tensor", "dp"),
        P(None, None, "dp", "tensor"),
        P(None, None, "dp", "tensor"),
        P(None, None, "dp", "tensor"),
        P("dp", None, None),
        P("dp", None, None),
        P("dp", None, None),
        P("dp", None, "tensor", None),
        P("dp", None, "tensor", None),
        P("dp", None, "tensor", None),
        P("tensor", None, "dp"),
        P("tensor", None, "dp"),
        P("tensor", None, "dp"),
        P("dp", "tensor"),
        P("dp", "tensor"),
        P("dp", "tensor"),
        P("tensor", "dp"),
        P("tensor", "dp"),
        P("tensor", "dp"),
    )
    return jax.shard_map(
        per_device, mesh=mesh, in_specs=in_specs, out_specs=out_specs, check_vma=False
    )
```

profile of v0, /device:TPU:0, one launch (start us, length us, event | category | flops | bytes accessed | tf_op | source)
XLA Modules:
  0.0 5549.9 jit_solution(12171616674595519980)
XLA Ops:
  12.9 42.5 all-gather.1
  56.6 42.1 all_gather.35
  99.3 44.0 all-gather.11.cloned.1.call-done
  154.3 112.8 %all-gather.13.cloned.1.call-done = bf16[3,3,512,1024]{2,3,1,0:T(8,128)(2,1)} async-done(((bf16[3,3,512,64]{2,3,1,0:T(8,128)(2,1)}), bf16[3,3,512,1024]{2,3,1,0:T(8,128)(2,1)}) %all-gather.13.cloned.1.call-update) | async-done | bytes 9437200 | tf_op jit(solution)/shard_map/all_gather | solution.py:252
  284.5 78.3 %all-gather.17.cloned.1.call-done = bf16[256,6,2048]{2,0,1:T(8,128)(2,1)} async-done(((bf16[16,6,2048]{2,0,1:T(8,128)(2,1)}), bf16[256,6,2048]{2,0,1:T(8,128)(2,1)}) %all-gather.17.cloned.1.call-update) | async-done | bytes 6291472 | tf_op jit(solution)/shard_map/all_gather | solution.py:254
  362.9 8.7 copy.174
  371.6 4.5 fusion.6
  377.4 5.4 all-reduce.32.cloned.1.call-done
  389.5 209.6 %all-gather.15.cloned.1.call-done = bf16[3,3,1024,1024]{3,2,1,0:T(8,128)(2,1)} async-done(((bf16[3,3,64,1024]{3,2,1,0:T(8,128)(2,1)}), bf16[3,3,1024,1024]{3,2,1,0:T(8,128)(2,1)}) %all-gather.15.cloned.1.call-update) | async-done | bytes 18874384 | tf_op jit(solution)/shard_map/all_gather | solution.py:253
  621.1 131.8 %all-gather.19.cloned.1.call-done = bf16[2048,3,8,128]{3,2,1,0:T(8,128)(2,1)} async-done(((bf16[128,3,8,128]{3,2,1,0:T(8,128)(2,1)}), bf16[2048,3,8,128]{3,2,1,0:T(8,128)(2,1)}) %all-gather.19.cloned.1.call-update) | async-done | bytes 12582928 | tf_op jit(solution)/shard_map/all_gather | solution.py:255
  752.9 7.0 fusion.44
  761.3 82.6 %all-gather.21.cloned.1.call-done = bf16[8,128,2048]{2,1,0:T(8,128)(2,1)} async-done(((bf16[8,128,128]{2,1,0:T(8,128)(2,1)}), bf16[8,128,2048]{2,1,0:T(8,128)(2,1)}) %all-gather.21.cloned.1.call-update) | async-done | bytes 4194320 | tf_op jit(solution)/shard_map/all_gather | solution.py:256
  853.7 10.6 all-reduce.34.cloned.1.call-done
  866.7 193.8 %all-gather.23.cloned.1.call-done = bf16[2048,4096]{1,0:T(8,128)(2,1)} async-done(((bf16[128,4096]{1,0:T(8,128)(2,1)}), bf16[2048,4096]{1,0:T(8,128)(2,1)}) %all-gather.23.cloned.1.call-update) | async-done | bytes 16777232 | tf_op jit(solution)/shard_map/all_gather | solution.py:257
  1060.5 9.1 fusion.343
  1069.6 241.9 %all-gather.25.cloned.1.call-done = bf16[4096,2048]{1,0:T(8,128)(2,1)} async-done(((bf16[4096,128]{1,0:T(8,128)(2,1)}), bf16[4096,2048]{1,0:T(8,128)(2,1)}) %all-gather.25.cloned.1.call-update) | async-done | bytes 16777232 | tf_op jit(solution)/shard_map/all_gather | solution.py:258
  1311.4 11.9 fusion.89
  1323.4 11.9 convolution_convert_fusion
  1335.5 16.4 all-reduce.36.cloned.1.call-done
  1364.6 9.4 fusion.12
  1374.3 19.4 all-reduce.38.cloned.1.call-done
  1443.1 3.8 pad.76
  1453.2 4.2 add_add_fusion
  1459.8 9.5 convolution_convert_fusion.1
  1469.3 10.3 all-reduce.40.cloned.1.call-done
  1515.7 19.9 all-reduce.44.cloned.1.call-done
  1550.3 4.6 fusion.222
  1556.1 6.2 broadcast_multiply_fusion
  1566.7 6.4 copy-done.7
  1578.1 6.4 copy-done.8
  1584.5 18.7 copy.184
  1604.3 10.2 fusion.176
  1615.7 13.3 fusion.342
  1630.2 13.4 fusion.226
  1674.6 66.1 %all-reduce.42.cloned.1.call-done = f32[256,2,512]{2,1,0:T(2,128)} async-done(((f32[256,2,512]{2,1,0:T(2,128)}), f32[256,2,512]{2,1,0:T(2,128)}) %all-reduce.42.cloned.1.call-update) | async-done | bytes 1048592
  1742.2 177.7 %reduce-scatter.22.cloned.1.call-done = f32[8,128,128]{2,1,0:T(8,128)} async-done(((f32[8,128,2048]{2,1,0:T(8,128)}), f32[8,128,128]{2,1,0:T(8,128)}) %reduce-scatter.22.cloned.1.call-update) | async-done | bytes 524304 | tf_op jit(solution)/shard_map/reduce_scatter | solution.py:438
  1921.7 211.8 %reduce-scatter.18.cloned.1.call-done = f32[16,6,2048]{2,0,1:T(8,128)} async-done(((f32[256,6,2048]{2,0,1:T(8,128)}), f32[16,6,2048]{2,0,1:T(8,128)}) %reduce-scatter.18.cloned.1.call-update) | async-done | bytes 786448 | tf_op jit(solution)/shard_map/reduce_scatter | solution.py:436
  2136.1 387.9 %reduce-scatter.12.cloned.1.call-done = f32[3,3,64,512]{3,2,1,0:T(8,128)} async-done(((f32[3,3,1024,512]{3,2,1,0:T(8,128)}), f32[3,3,64,512]{3,2,1,0:T(8,128)}) %reduce-scatter.12.cloned.1.call-update) | async-done | bytes 1179664 | tf_op jit(solution)/shard_map/reduce_scatter | solution.py:468
  2527.5 393.3 %reduce-scatter.14.cloned.1.call-done = f32[3,3,512,64]{2,3,1,0:T(8,128)} async-done(((f32[3,3,512,1024]{2,3,1,0:T(8,128)}), f32[3,3,512,64]{2,3,1,0:T(8,128)}) %reduce-scatter.14.cloned.1.call-update) | async-done | bytes 1179664 | tf_op jit(solution)/shard_map/reduce_scatter | solution.py:470
  2923.6 371.0 %reduce-scatter.20.cloned.1.call-done = f32[128,3,8,128]{3,0,2,1:T(8,128)} async-done(((f32[2048,3,8,128]{3,0,2,1:T(8,128)}), f32[128,3,8,128]{3,0,2,1:T(8,128)}) %reduce-scatter.20.cloned.1.call-update) | async-done | bytes 1572880 | tf_op jit(solution)/shard_map/reduce_scatter | solution.py:437
  3297.0 682.4 %reduce-scatter.24.cloned.1.call-done = f32[128,4096]{1,0:T(8,128)} async-done(((f32[2048,4096]{1,0:T(8,128)}), f32[128,4096]{1,0:T(8,128)}) %reduce-scatter.24.cloned.1.call-update) | async-done | bytes 2097168 | tf_op jit(solution)/shard_map/reduce_scatter | solution.py:439
  3982.1 688.7 %reduce-scatter.26.cloned.1.call-done = f32[4096,128]{1,0:T(8,128)} async-done(((f32[4096,2048]{1,0:T(8,128)}), f32[4096,128]{1,0:T(8,128)}) %reduce-scatter.26.cloned.1.call-update) | async-done | bytes 2097168 | tf_op jit(solution)/shard_map/reduce_scatter | solution.py:440
  4673.5 772.9 %reduce-scatter.16.cloned.1.call-done = f32[3,3,64,1024]{3,2,1,0:T(8,128)} async-done(((f32[3,3,1024,1024]{3,2,1,0:T(8,128)}), f32[3,3,64,1024]{3,2,1,0:T(8,128)}) %reduce-scatter.16.cloned.1.call-update) | async-done | bytes 2359312 | tf_op jit(solution)/shard_map/reduce_scatter | solution.py:471
  5454.0 45.0 psum.63
  5499.7 4.3 multiply_subtract_fusion.3
  5525.4 4.0 multiply_subtract_fusion.1
  5531.1 4.4 multiply_subtract_fusion.2
  5537.1 4.4 multiply_subtract_fusion
  (594 shorter events, 289.0 us)
Async XLA Ops:
  7.2 136.1 %all-gather.11.cloned.1.call-start = ((), (), s32[]{:S(2)}) async-start(), calls=%async_computation.9 | async-start | bytes 10027008 | tf_op jit(solution)/shard_map/all_gather | solution.py:250
  9.6 257.5 %all-gather.13.cloned.1.call-start = ((), (), s32[]{:S(2)}) async-start(), calls=%async_computation.10 | async-start | bytes 10027008 | tf_op jit(solution)/shard_map/all_gather | solution.py:252
  10.6 352.3 %all-gather.17.cloned.1.call-start = ((), (), s32[]{:S(2)}) async-start(), calls=%async_computation.13 | async-start | bytes 6684672 | tf_op jit(solution)/shard_map/all_gather | solution.py:254
  11.5 371.3 %all-reduce.32.cloned.1.call-start = ((), (), s32[]{:S(2)}) async-start(), calls=%async_computation.11 | async-start | bytes 1048576 | tf_op jit(solution)/shard_map/psum | solution.py:297
  277.9 321.1 %all-gather.15.cloned.1.call-start = ((), (), s32[]{:S(2)}) async-start(), calls=%async_computation.12 | async-start | bytes 20054016 | tf_op jit(solution)/shard_map/all_gather | solution.py:253
  280.9 472.0 %all-gather.19.cloned.1.call-start = ((), (), s32[]{:S(2)}) async-start(), calls=%async_computation.14 | async-start | bytes 13369344 | tf_op jit(solution)/shard_map/all_gather | solution.py:255
  283.4 560.5 %all-gather.21.cloned.1.call-start = ((), (), s32[]{:S(2)}) async-start(), calls=%async_computation.15 | async-start | bytes 4456448 | tf_op jit(solution)/shard_map/all_gather | solution.py:256
  284.3 580.0 %all-reduce.34.cloned.1.call-start = ((), (), s32[]{:S(2)}) async-start(), calls=%async_computation.16 | async-start | bytes 524288 | tf_op jit(solution)/shard_map/psum | solution.py:327
  376.7 376.1 %copy-start.124 = (f32[1,1,2048]{2,0,1:T(1,128)}, f32[1,1,2048]{2,0,1:T(1,128)S(1)}, u32[]{:S(2)}) copy-start(f32[1,1,2048]{2,0,1:T(1,128)S(1)} %get-tuple-element.258) | copy-start | bytes 24580
  377.4 375.5 %copy-start.93 = (f32[1,1,2048]{2,1,0:T(1,128)}, f32[1,1,2048]{2,1,0:T(1,128)S(1)}, u32[]{:S(2)}) copy-start(f32[1,1,2048]{2,1,0:T(1,128)S(1)} %get-tuple-element.256) | copy-start | bytes 24580
  377.4 979.0 %copy-start.67 = (f32[1,1,2048]{2,1,0:T(1,128)}, f32[1,1,2048]{2,1,0:T(1,128)S(1)}, u32[]{:S(2)}) copy-start(f32[1,1,2048]{2,1,0:T(1,128)S(1)} %get-tuple-element.255) | copy-start | bytes 24580
  384.6 231.5 %copy-start.69 = (bf16[1,8,8,1024]{3,2,1,0:T(8,128)(2,1)}, bf16[1,8,8,1024]{3,2,1,0:T(8,128)(2,1)S(1)}, u32[]{:S(2)}) copy-start(bf16[1,8,8,1024]{3,2,1,0:T(8,128)(2,1)S(1)} %slice.365) | copy-start | bytes 393220
  384.9 229.1 %copy-start.75 = (bf16[1,8,8,1024]{3,2,1,0:T(8,128)(2,1)}, bf16[1,8,8,1024]{3,2,1,0:T(8,128)(2,1)S(1)}, u32[]{:S(2)}) copy-start(bf16[1,8,8,1024]{3,2,1,0:T(8,128)(2,1)S(1)} %slice.363) | copy-start | bytes 393220
  385.2 226.7 %copy-start.77 = (bf16[1,8,8,1024]{3,2,1,0:T(8,128)(2,1)}, bf16[1,8,8,1024]{3,2,1,0:T(8,128)(2,1)S(1)}, u32[]{:S(2)}) copy-start(bf16[1,8,8,1024]{3,2,1,0:T(8,128)(2,1)S(1)} %slice.361) | copy-start | bytes 393220
  385.6 224.1 %copy-start.79 = (bf16[1,8,8,1024]{3,2,1,0:T(8,128)(2,1)}, bf16[1,8,8,1024]{3,2,1,0:T(8,128)(2,1)S(1)}, u32[]{:S(2)}) copy-start(bf16[1,8,8,1024]{3,2,1,0:T(8,128)(2,1)S(1)} %slice.359) | copy-start | bytes 393220
  385.9 221.5 %copy-start.81 = (bf16[1,8,8,1024]{3,2,1,0:T(8,128)(2,1)}, bf16[1,8,8,1024]{3,2,1,0:T(8,128)(2,1)S(1)}, u32[]{:S(2)}) copy-start(bf16[1,8,8,1024]{3,2,1,0:T(8,128)(2,1)S(1)} %slice.357) | copy-start | bytes 393220
  386.2 219.1 %copy-start.83 = (bf16[1,8,8,1024]{3,2,1,0:T(8,128)(2,1)}, bf16[1,8,8,1024]{3,2,1,0:T(8,128)(2,1)S(1)}, u32[]{:S(2)}) copy-start(bf16[1,8,8,1024]{3,2,1,0:T(8,128)(2,1)S(1)} %slice.355) | copy-start | bytes 393220
  386.6 216.6 %copy-start.85 = (bf16[1,8,8,1024]{3,2,1,0:T(8,128)(2,1)}, bf16[1,8,8,1024]{3,2,1,0:T(8,128)(2,1)S(1)}, u32[]{:S(2)}) copy-start(bf16[1,8,8,1024]{3,2,1,0:T(8,128)(2,1)S(1)} %slice.353) | copy-start | bytes 393220
  389.5 213.8 %copy-start.71 = (bf16[1,8,8,1024]{3,2,1,0:T(8,128)(2,1)}, bf16[1,8,8,1024]{3,2,1,0:T(8,128)(2,1)S(1)}, u32[]{:S(2)}) copy-start(bf16[1,8,8,1024]{3,2,1,0:T(8,128)(2,1)S(1)} %slice.349) | copy-start | bytes 393220
  389.5 211.6 %copy-start.87 = (bf16[1,8,8,1024]{3,2,1,0:T(8,128)(2,1)S(1)}, bf16[1,8,8,1024]{3,2,1,0:T(8,128)(2,1)}, u32[]{:S(2)}) copy-start(bf16[1,8,8,1024]{3,2,1,0:T(8,128)(2,1)} %slice.351) | copy-start | bytes 393220
  847.7 212.8 %all-gather.23.cloned.1.call-start = ((), (), s32[]{:S(2)}) async-start(), calls=%async_computation.17 | async-start | bytes 17825792 | tf_op jit(solution)/shard_map/all_gather | solution.py:257
  850.5 210.0 %copy-start.91 = (f32[1,1,2048]{2,0,1:T(1,128)S(1)}, f32[1,1,2048]{2,0,1:T(1,128)}, u32[]{:S(2)}) copy-start(f32[1,1,2048]{2,0,1:T(1,128)} %get-tuple-element.259) | copy-start | bytes 24580
  850.5 461.0 %all-gather.25.cloned.1.call-start = ((), (), s32[]{:S(2)}) async-start(), calls=%async_computation.18 | async-start | bytes 17825792 | tf_op jit(solution)/shard_map/all_gather | solution.py:258
  853.3 498.6 %all-reduce.36.cloned.1.call-start = ((), (), s32[]{:S(2)}) async-start(), calls=%async_computation.19 | async-start | bytes 524288 | tf_op jit(solution)/shard_map/psum | solution.py:363
  865.4 204.1 %copy-start.115 = (f32[64]{0:T(128)}, f32[64]{0:T(128)S(1)}, u32[]{:S(2)}) copy-start(f32[64]{0:T(128)S(1)} %broadcast_multiply_fusion.3) | copy-start | bytes 772
  866.7 202.9 %copy-start.130 = (f32[64]{0:T(128)}, f32[64]{0:T(128)S(1)}, u32[]{:S(2)}) copy-start(f32[64]{0:T(128)S(1)} %fusion.291) | copy-start | bytes 772
  1060.5 251.0 %copy-start.34 = (bf16[1,64,2048]{2,1,0:T(8,128)(2,1)S(1)}, bf16[1,64,2048]{2,1,0:T(8,128)(2,1)}, u32[]{:S(2)}) copy-start(bf16[1,64,2048]{2,1,0:T(8,128)(2,1)} %param.35) | copy-start | bytes 786436
  1060.5 251.0 %copy-start.97 = (f32[1,1,2048]{2,1,0:T(1,128)S(1)}, f32[1,1,2048]{2,1,0:T(1,128)}, u32[]{:S(2)}) copy-start(f32[1,1,2048]{2,1,0:T(1,128)} %get-tuple-element.254) | copy-start | bytes 24580
  1069.6 390.3 %copy-start.5 = (f32[64,4096]{1,0:T(8,128)}, f32[64,4096]{1,0:T(8,128)S(1)}, u32[]{:S(2)}) copy-start(f32[64,4096]{1,0:T(8,128)S(1)} %fusion.343) | copy-start | bytes 3145732
  1335.3 58.4 %all-reduce.38.cloned.1.call-start = ((), (), s32[]{:S(2)}) async-start(), calls=%async_computation.20 | async-start | bytes 524288 | tf_op jit(solution)/shard_map/psum | solution.py:413
  1374.1 105.6 %all-reduce.40.cloned.1.call-start = ((), (), s32[]{:S(2)}) async-start(), calls=%async_computation.21 | async-start | bytes 1048576 | tf_op jit(solution)/shard_map/psum | solution.py:449
  1459.6 76.0 %all-reduce.44.cloned.1.call-start = ((), (), s32[]{:S(2)}) async-start(), calls=%async_computation.32 | async-start | bytes 1572864 | tf_op jit(solution)/shard_map/psum | solution.py:342
  1515.0 157.6 %reduce-scatter.28.cloned.1.call-start = ((), (), s32[]{:S(2)}) async-start(), calls=%async_computation.30 | async-start | bytes 557056
  1548.1 192.6 %all-reduce.42.cloned.1.call-start = ((), (), s32[]{:S(2)}) async-start(), calls=%async_computation.31 | async-start | bytes 2097152
  1550.2 369.7 %reduce-scatter.22.cloned.1.call-start = ((), (), s32[]{:S(2)}) async-start(), calls=%async_computation.27 | async-start | bytes 8912896 | tf_op jit(solution)/shard_map/reduce_scatter | solution.py:438
  1555.0 578.5 %reduce-scatter.18.cloned.1.call-start = ((), (), s32[]{:S(2)}) async-start(), calls=%async_computation.25 | async-start | bytes 13369344 | tf_op jit(solution)/shard_map/reduce_scatter | solution.py:436
  1562.3 961.7 %reduce-scatter.12.cloned.1.call-start = ((), (), s32[]{:S(2)}) async-start(), calls=%async_computation.22 | async-start | bytes 20054016 | tf_op jit(solution)/shard_map/reduce_scatter | solution.py:468
  1573.1 1347.6 %reduce-scatter.14.cloned.1.call-start = ((), (), s32[]{:S(2)}) async-start(), calls=%async_computation.23 | async-start | bytes 20054016 | tf_op jit(solution)/shard_map/reduce_scatter | solution.py:470
  1603.3 1691.3 %reduce-scatter.20.cloned.1.call-start = ((), (), s32[]{:S(2)}) async-start(), calls=%async_computation.26 | async-start | bytes 26738688 | tf_op jit(solution)/shard_map/reduce_scatter | solution.py:437
  1614.6 2364.7 %reduce-scatter.24.cloned.1.call-start = ((), (), s32[]{:S(2)}) async-start(), calls=%async_computation.28 | async-start | bytes 35651584 | tf_op jit(solution)/shard_map/reduce_scatter | solution.py:439
  1629.0 3041.8 %reduce-scatter.26.cloned.1.call-start = ((), (), s32[]{:S(2)}) async-start(), calls=%async_computation.29 | async-start | bytes 35651584 | tf_op jit(solution)/shard_map/reduce_scatter | solution.py:440
  1643.6 3802.8 %reduce-scatter.16.cloned.1.call-start = ((), (), s32[]{:S(2)}) async-start(), calls=%async_computation.24 | async-start | bytes 40108032 | tf_op jit(solution)/shard_map/reduce_scatter | solution.py:471
  3982.1 1470.5 %copy-start.4 = (bf16[1,16,16,1024]{3,2,1,0:T(8,128)(2,1)S(1)}, bf16[1,16,16,1024]{3,2,1,0:T(8,128)(2,1)}, u32[]{:S(2)}) copy-start(bf16[1,16,16,1024]{3,2,1,0:T(8,128)(2,1)} %param.33) | copy-start | bytes 1572868
  3982.1 1470.5 %copy-start.14 = (f32[1,16,16,1024]{3,2,1,0:T(8,128)S(1)}, f32[1,16,16,1024]{3,2,1,0:T(8,128)}, u32[]{:S(2)}) copy-start(f32[1,16,16,1024]{3,2,1,0:T(8,128)} %copy-done.13) | copy-start | bytes 3145732
  3982.1 1470.5 %copy-start.96 = (f32[1024]{0:T(1024)S(1)}, f32[1024]{0:T(1024)}, u32[]{:S(2)}) copy-start(f32[1024]{0:T(1024)} %copy-done.95) | copy-start | bytes 12292
  3982.1 1470.5 %copy-start.100 = (f32[1024]{0:T(1024)S(1)}, f32[1024]{0:T(1024)}, u32[]{:S(2)}) copy-start(f32[1024]{0:T(1024)} %copy-done.99) | copy-start | bytes 12292
  3982.1 1470.5 %copy-start.102 = (f32[1,1024]{1,0:T(1,128)S(1)}, f32[1,1024]{1,0:T(1,128)}, u32[]{:S(2)}) copy-start(f32[1,1024]{1,0:T(1,128)} %copy-done.101) | copy-start | bytes 12292
  3982.1 1470.5 %copy-start.113 = (f32[1024]{0:T(1024)S(1)}, f32[1024]{0:T(1024)}, u32[]{:S(2)}) copy-start(f32[1024]{0:T(1024)} %broadcast_in_dim.94) | copy-start | bytes 12292
  (129 other events, 2393.3 us)
Sparse Core Ops, SparseCore 0:
  11.4 131.8 all-gather.10
  146.6 120.4 all-gather.12
  270.5 92.3 all-gather.16
  365.6 17.1 all-reduce.31
  386.3 212.6 all-gather.14
  602.6 150.1 all-gather.18
  756.5 87.3 all-gather.20
  847.8 16.4 all-reduce.33
  867.6 192.7 all-gather.22
  1063.6 247.8 all-gather.24
  1335.4 16.4 all-reduce.35
  1374.2 19.4 all-reduce.37
  1459.7 19.8 all-reduce.39
  1515.1 20.3 all-reduce.43
  1548.3 77.7 reduce-scatter.27
  1632.6 108.1 all-reduce.41
  1743.0 176.8 reduce-scatter.21
  1926.4 207.1 reduce-scatter.17
  2135.8 388.1 reduce-scatter.11
  2526.2 394.5 reduce-scatter.13
  2926.5 367.9 reduce-scatter.19
  3296.9 682.4 reduce-scatter.23
  3981.7 689.0 reduce-scatter.25
  4673.0 773.3 reduce-scatter.15
where the time goes:
time: 5560 us; the launch traced here: 5550 us
  waiting for transfers between devices  4930 us (89%)
  matrix products  239 us (4%)
  blocking collectives  132 us (2%)
  local copies, waits for them, and re-layouts  111 us (2%)
  other arithmetic  110 us (2%)
    reduce_scatter x1, waiting for transfers between devices, per_device(): lax.psum_scatter(grad_half, 'dp', scatter_dimension=2, tiled=True)  773 us
    reduce_scatter x1, waiting for transfers between devices, per_device(): lax.psum_scatter(grad_down, 'dp', scatter_dimension=1, tiled=True)  689 us
    reduce_scatter x1, waiting for transfers between devices, per_device(): lax.psum_scatter(grad_up, 'dp', scatter_dimension=0, tiled=True)  682 us
    reduce_scatter x1, waiting for transfers between devices, per_device(): lax.psum_scatter(grad_conv_two, 'dp', scatter_dimension=3, tiled=True)  393 us
    reduce_scatter x1, waiting for transfers between devices, per_device(): lax.psum_scatter(grad_conv_one, 'dp', scatter_dimension=2, tiled=True)  388 us
    reduce_scatter x1, waiting for transfers between devices, per_device(): lax.psum_scatter(grad_qkv_w, 'dp', scatter_dimension=0, tiled=True)  371 us
    all_gather x1, waiting for transfers between devices, per_device(): lax.all_gather(lowered[9], 'dp', axis=1, tiled=True)  242 us
    reduce_scatter x1, waiting for transfers between devices, per_device(): lax.psum_scatter(adaptive_gradient, 'dp', scatter_dimension=0, tiled=True)  212 us
  transfers between devices with their start and end apart: 24, of which 23 were waited for; matrix products, arithmetic and copies ran while one was open for 4% of the time, Pallas kernels for 0%

commit v1 on v0

--- a/solution.py
+++ b/solution.py
@@ -1,10 +1,15 @@
+import functools
+import itertools
 import math
 
 import jax
 import jax.numpy as jnp
 from jax import lax
+from jax.experimental import pallas as pl
+from jax.experimental.pallas import tpu as pltpu
 from jax.sharding import PartitionSpec as P
 
+DP, TENSOR = ("dp", "tensor")
 C = 1024
 D = 2048
 HEADS = 16
@@ -171,6 +176,45 @@
                 jnp.einsum("bhwc,bhwd->cd", window, upstream, preferred_element_type=jnp.float32)
             )
     return jnp.stack(tap_list).reshape(3, 3, inputs.shape[3], upstream.shape[3])
+
+
+def clipped_step(masters, averages, squares, combined_total, sum_all):
+    local_sq = jnp.zeros((), jnp.float32)
+    for position, reduced in enumerate(combined_total):
+        shard_sq = jnp.sum(reduced * reduced)
+        if position == 0 or position == 5:
+            shard_sq = shard_sq / lax.axis_size(TENSOR)
+        local_sq = local_sq + shard_sq
+    square_sum = sum_all(local_sq)
+    grad_norm = jnp.sqrt(square_sum)
+    factor = jnp.minimum(1.0, CLIP / (grad_norm + 1e-06))
+    conv_rate = LR_SCALE * (9 * C) ** (-0.5)
+    mod_rate = LR_SCALE * (4 * FREQ) ** (-0.5)
+    rates = (
+        LR_NORM,
+        conv_rate,
+        mod_rate,
+        conv_rate,
+        conv_rate,
+        mod_rate,
+        LR_SCALE * D ** (-0.5),
+        LR_SCALE * (HEADS * HDIM // 32) ** (-0.5),
+        LR_SCALE * D ** (-0.5),
+        LR_SCALE * FF ** (-0.5),
+    )
+    correct_one = 1.0 - BETA_ONE**STEP
+    correct_two = 1.0 - BETA_TWO**STEP
+    results = []
+    for master, average, square, reduced, learn_rate in zip(
+        masters, averages, squares, combined_total, rates
+    ):
+        clipped = reduced * factor
+        new_avg = BETA_ONE * average + (1.0 - BETA_ONE) * clipped
+        new_sq = BETA_TWO * square + (1.0 - BETA_TWO) * clipped * clipped
+        step_dir = new_avg / correct_one / (jnp.sqrt(new_sq / correct_two) + ADAM_EPS)
+        new_master = master - learn_rate * (step_dir + DECAY * master)
+        results += [new_master, new_avg, new_sq]
+    return (grad_norm.reshape(1),) + tuple(results)
 
 
 def per_device(
@@ -246,16 +290,16 @@
     )
     lowered = tuple((master.astype(jnp.bfloat16) for master in masters))
     gathered = (
-        lax.all_gather(lowered[0], "dp", axis=1, tiled=True),
-        lax.all_gather(lowered[1], "dp", axis=2, tiled=True),
-        lax.all_gather(lowered[2], "dp", axis=0, tiled=True),
-        lax.all_gather(lowered[3], "dp", axis=3, tiled=True),
-        lax.all_gather(lowered[4], "dp", axis=2, tiled=True),
-        lax.all_gather(lowered[5], "dp", axis=0, tiled=True),
-        lax.all_gather(lowered[6], "dp", axis=0, tiled=True),
-        lax.all_gather(lowered[7], "dp", axis=2, tiled=True),
-        lax.all_gather(lowered[8], "dp", axis=0, tiled=True),
-        lax.all_gather(lowered[9], "dp", axis=1, tiled=True),
+        lax.all_gather(lowered[0], DP, axis=1, tiled=True),
+        lax.all_gather(lowered[1], DP, axis=2, tiled=True),
+        lax.all_gather(lowered[2], DP, axis=0, tiled=True),
+        lax.all_gather(lowered[3], DP, axis=3, tiled=True),
+        lax.all_gather(lowered[4], DP, axis=2, tiled=True),
+        lax.all_gather(lowered[5], DP, axis=0, tiled=True),
+        lax.all_gather(lowered[6], DP, axis=0, tiled=True),
+        lax.all_gather(lowered[7], DP, axis=2, tiled=True),
+        lax.all_gather(lowered[8], DP, axis=0, tiled=True),
+        lax.all_gather(lowered[9], DP, axis=1, tiled=True),
     )
     (
         gain_bias,
@@ -275,8 +319,8 @@
     local_d = conv_half.shape[3]
     heads_here = qkv_full.shape[2]
     tokens_len = height // 2 * (breadth // 2)
-    tensor_pos = lax.axis_index("tensor")
-    n_tensor = lax.axis_size("tensor")
+    tensor_pos = lax.axis_index(TENSOR)
+    n_tensor = lax.axis_size(TENSOR)
     score_scale = HDIM ** (-0.5)
     noise_emb = embed_noise(t_index, FREQ)
     emb_low = noise_emb.astype(jnp.bfloat16)
@@ -294,13 +338,13 @@
     middle = conv_same(act_one, conv_one)
     act_two, second_back = jax.vjp(second_piece, middle, res_mods)
     act_two = act_two.astype(jnp.bfloat16)
-    branch = lax.psum(conv_same(act_two, conv_two).astype(jnp.bfloat16), "tensor").astype(
+    branch = lax.psum(conv_same(act_two, conv_two).astype(jnp.bfloat16), TENSOR).astype(
         jnp.float32
     )
     residual = image_float + branch
     resid_low = residual.astype(jnp.bfloat16)
     shrunk = conv_down(resid_low, conv_half)
-    pieces = lax.all_gather(shrunk.astype(jnp.bfloat16), "tensor", axis=3, tiled=True).astype(
+    pieces = lax.all_gather(shrunk.astype(jnp.bfloat16), TENSOR, axis=3, tiled=True).astype(
         shrunk.dtype
     )
     tokens = pieces.reshape(batch_size, tokens_len, D)
@@ -326,7 +370,7 @@
     attended = (
         lax.psum(
             jnp.dot(mixed, out_flat, preferred_element_type=jnp.float32).astype(jnp.bfloat16),
-            "tensor",
+            TENSOR,
         )
         .astype(jnp.float32)
         .reshape(batch_size, tokens_len, D)
@@ -341,7 +385,7 @@
     expanded = (
         lax.psum(
             jnp.dot(hidden_low, down_full, preferred_element_type=jnp.float32).astype(jnp.bfloat16),
-            "tensor",
+            TENSOR,
         )
         .astype(jnp.float32)
         .reshape(batch_size, tokens_len, D)
@@ -364,7 +408,7 @@
             jnp.einsum(
                 "tf,df->td", grad_pre_low, up_full, preferred_element_type=jnp.float32
             ).astype(jnp.bfloat16),
-            "tensor",
+            TENSOR,
         )
         .astype(jnp.float32)
         .reshape(batch_size, tokens_len, D)
@@ -417,7 +461,7 @@
                 qkv_full.reshape(D, 3 * heads_here * HDIM),
                 preferred_element_type=jnp.float32,
             ).astype(jnp.bfloat16),
-            "tensor",
+            TENSOR,
         )
         .astype(jnp.float32)
         .reshape(batch_size, tokens_len, D)
@@ -433,11 +477,11 @@
     grad_out_w = grad_out.reshape(heads_here, HDIM, D)
     grad_up = jnp.einsum("td,tf->df", mlp_low, grad_pre_low, preferred_element_type=jnp.float32)
     transformer_gradient_total = (
-        lax.psum_scatter(adaptive_gradient, "dp", scatter_dimension=0, tiled=True),
-        lax.psum_scatter(grad_qkv_w, "dp", scatter_dimension=0, tiled=True),
-        lax.psum_scatter(grad_out_w, "dp", scatter_dimension=2, tiled=True),
-        lax.psum_scatter(grad_up, "dp", scatter_dimension=0, tiled=True),
-        lax.psum_scatter(grad_down, "dp", scatter_dimension=1, tiled=True),
+        lax.psum_scatter(adaptive_gradient, DP, scatter_dimension=0, tiled=True),
+        lax.psum_scatter(grad_qkv_w, DP, scatter_dimension=0, tiled=True),
+        lax.psum_scatter(grad_out_w, DP, scatter_dimension=2, tiled=True),
+        lax.psum_scatter(grad_up, DP, scatter_dimension=0, tiled=True),
+        lax.psum_scatter(grad_down, DP, scatter_dimension=1, tiled=True),
     )
     grad_shrunk = lax.dynamic_slice_in_dim(
         grad_tokens.reshape(batch_size, height // 2, breadth // 2, D),
@@ -447,7 +491,7 @@
     ).astype(jnp.bfloat16)
     grad_half = conv_down_kernel(resid_low, grad_shrunk)
     grad_resid = lax.psum(
-        conv_down_input(grad_shrunk, conv_half, height, breadth).astype(jnp.bfloat16), "tensor"
+        conv_down_input(grad_shrunk, conv_half, height, breadth).astype(jnp.bfloat16), TENSOR
     ).astype(jnp.float32)
     grad_branch = grad_resid.astype(jnp.bfloat16)
     grad_conv_two = conv_same_kernel(act_two, grad_branch)
@@ -456,7 +500,7 @@
     grad_middle_low = grad_middle.astype(jnp.bfloat16)
     grad_conv_one = conv_same_kernel(act_one, grad_middle_low)
     grad_act_one = lax.psum(
-        conv_same_input(grad_middle_low, conv_one).astype(jnp.bfloat16), "tensor"
+        conv_same_input(grad_middle_low, conv_one).astype(jnp.bfloat16), TENSOR
     ).astype(jnp.float32)
     grad_image_norm, grad_gain = first_back(grad_act_one)
     images_grad = grad_resid + grad_image_norm
@@ -464,122 +508,1727 @@
         "bf,bk->fk", emb_back, grad_res_mods.reshape(batch_size, 2 * local_c), precision=HIGHEST
     ).reshape(FREQ, 2, local_c)
     resnet_gradient_total = (
-        lax.psum_scatter(grad_gain, "dp", scatter_dimension=1, tiled=True),
-        lax.psum_scatter(grad_conv_one, "dp", scatter_dimension=2, tiled=True),
-        lax.psum_scatter(grad_res_table, "dp", scatter_dimension=0, tiled=True),
-        lax.psum_scatter(grad_conv_two, "dp", scatter_dimension=3, tiled=True),
-        lax.psum_scatter(grad_half, "dp", scatter_dimension=2, tiled=True),
+        lax.psum_scatter(grad_gain, DP, scatter_dimension=1, tiled=True),
+        lax.psum_scatter(grad_conv_one, DP, scatter_dimension=2, tiled=True),
+        lax.psum_scatter(grad_res_table, DP, scatter_dimension=0, tiled=True),
+        lax.psum_scatter(grad_conv_two, DP, scatter_dimension=3, tiled=True),
+        lax.psum_scatter(grad_half, DP, scatter_dimension=2, tiled=True),
     )
     combined_total = tuple(resnet_gradient_total) + tuple(transformer_gradient_total)
-    local_sq = jnp.zeros((), jnp.float32)
-    for position, reduced in enumerate(combined_total):
-        shard_sq = jnp.sum(reduced * reduced)
-        if position == 0 or position == 5:
-            shard_sq = shard_sq / n_tensor
-        local_sq = local_sq + shard_sq
-    square_sum = lax.psum(local_sq, ("dp", "tensor"))
-    grad_norm = jnp.sqrt(square_sum)
-    factor = jnp.minimum(1.0, CLIP / (grad_norm + 1e-06))
-    conv_rate = LR_SCALE * (9 * C) ** (-0.5)
-    mod_rate = LR_SCALE * (4 * FREQ) ** (-0.5)
-    rates = (
-        LR_NORM,
-        conv_rate,
-        mod_rate,
-        conv_rate,
-        conv_rate,
-        mod_rate,
-        LR_SCALE * D ** (-0.5),
-        LR_SCALE * (HEADS * HDIM // 32) ** (-0.5),
-        LR_SCALE * D ** (-0.5),
-        LR_SCALE * FF ** (-0.5),
-    )
-    correct_one = 1.0 - BETA_ONE**STEP
-    correct_two = 1.0 - BETA_TWO**STEP
-    results = []
-    for master, average, square, reduced, learn_rate in zip(
-        masters, averages, squares, combined_total, rates
-    ):
-        clipped = reduced * factor
-        new_avg = BETA_ONE * average + (1.0 - BETA_ONE) * clipped
-        new_sq = BETA_TWO * square + (1.0 - BETA_TWO) * clipped * clipped
-        step_dir = new_avg / correct_one / (jnp.sqrt(new_sq / correct_two) + ADAM_EPS)
-        new_master = master - learn_rate * (step_dir + DECAY * master)
-        results += [new_master, new_avg, new_sq]
-    return (block_out, images_grad, grad_norm.reshape(1)) + tuple(results)
+    return (block_out, images_grad) + clipped_step(
+        masters,
+        averages,
+        squares,
+        combined_total,
+        lambda local: lax.psum(local, (DP, TENSOR)),
+    )
+
+
+MESH = pl.DeviceIdType.MESH
+ANYWHERE = pl.BlockSpec(memory_space=pl.ANY)
+IN_VMEM = pl.BlockSpec(memory_space=pltpu.VMEM)
+LAYERS = 4
+ORDER = (3, 0, 2, 1)
+VMEM_GRANT = 48 * 1024 * 1024
+
+
+class Place:
+    def __init__(self, wide):
+        self.wide = wide
+        self.dp = lax.axis_index(DP)
+        self.core = lax.axis_index(TENSOR)
+        self.z = self.dp // 4
+        x = self.dp % 2
+        y = (self.dp // 2) % 2
+        x_mate = self.dp + 1 - 2 * x
+        y_mate = self.dp + 2 - 4 * y
+        if wide:
+            self.first = x_mate * (1 - self.core) + y_mate * self.core
+            self.second = y_mate * (1 - self.core) + x_mate * self.core
+            self.stride = 4
+            self.column = self.dp % 4
+            self.first_column = self.first % 4
+            self.second_column = self.second % 4
+            self.far_column = 3 - self.column
+        else:
+            self.first = self.second = y_mate
+            self.stride = 2
+            self.column = y
+            self.second_column = 1 - y
+        self.slot = self.z * self.stride + self.column
+        self.has_below = self.z > 0
+        self.has_above = self.z < LAYERS - 1
+
+    def greet(self, with_core):
+        barrier = pltpu.get_barrier_semaphore()
+
+        def signal(dp, core):
+            pl.semaphore_signal(barrier, inc=1, device_id=(dp, core), device_id_type=MESH)
+
+        signal(self.second, self.core)
+        if self.wide:
+            signal(self.first, self.core)
+        if with_core:
+            signal(self.dp, 1 - self.core)
+        pl.when(self.has_below)(lambda: signal(self.dp - 4, self.core))
+        pl.when(self.has_above)(lambda: signal(self.dp + 4, self.core))
+        layers = (self.z + LAYERS - 1) // LAYERS + (2 * LAYERS - 2 - self.z) // LAYERS
+        pl.semaphore_wait(barrier, 1 + self.wide + with_core + layers)
+
+
+def params(number):
+    return pltpu.CompilerParams(
+        collective_id=number, has_side_effects=True, vmem_limit_bytes=VMEM_GRANT
+    )
+
+
+def gather_kernel(wide, both, block_ref, out_ref, send_sem, recv_sem, own_sem):
+    at = Place(wide)
+
+    def here(slot):
+        return out_ref.at[slot, at.core] if both else out_ref.at[slot]
+
+    def copy(sem, source, slot, mate):
+        return pltpu.make_async_remote_copy(
+            src_ref=source,
+            dst_ref=here(slot),
+            send_sem=send_sem.at[sem],
+            recv_sem=recv_sem.at[sem],
+            device_id=(mate, at.core),
+            device_id_type=MESH,
+        )
+
+    def mirror(slot, source):
+        return pltpu.make_async_remote_copy(
+            src_ref=source,
+            dst_ref=here(slot),
+            send_sem=send_sem.at[18 + slot],
+            recv_sem=recv_sem.at[18 + slot],
+            device_id=(at.dp, 1 - at.core),
+            device_id_type=MESH,
+        )
+
+    at.greet(both)
+    keep = pltpu.make_async_copy(block_ref, here(at.slot), own_sem)
+    keep.start()
+
+    def place(layer, column):
+        return layer * at.stride + column
+
+    def spread(layer, source):
+        slot = place(layer, at.column)
+        if wide:
+            copy(6 + layer, source, slot, at.first).start()
+        copy(10 + layer, source, slot, at.second).start()
+        if both:
+            mirror(slot, source).start()
+
+    def up(distance, source):
+        return copy(distance, source, place(at.z - distance, at.column), at.dp + 4)
+
+    def down(distance, source):
+        return copy(3 + distance, source, place(at.z + distance, at.column), at.dp - 4)
+
+    pl.when(at.has_above)(lambda: up(0, block_ref).start())
+    pl.when(at.has_below)(lambda: down(0, block_ref).start())
+    spread(at.z, block_ref)
+
+    def onward(layer):
+        slot = place(layer, at.first_column)
+        copy(6 + layer, here(slot), slot, at.first).wait_recv()
+        copy(14 + layer, here(slot), slot, at.second).start()
+        if both:
+            mirror(slot, here(slot)).start()
+
+    for distance in range(1, LAYERS):
+        below, above = at.z - distance, at.z + distance
+
+        @pl.when(below >= 0)
+        def _():
+            slot = place(below, at.column)
+            copy(distance - 1, here(slot), slot, at.dp).wait_recv()
+            if distance < LAYERS - 1:
+                pl.when(at.has_above)(lambda: up(distance, here(slot)).start())
+            spread(below, here(slot))
+
+        @pl.when(above < LAYERS)
+        def _():
+            slot = place(above, at.column)
+            copy(3 + distance - 1, here(slot), slot, at.dp).wait_recv()
+            if distance < LAYERS - 1:
+                pl.when(at.has_below)(lambda: down(distance, here(slot)).start())
+            spread(above, here(slot))
+
+        if not wide:
+            continue
+        if distance == 1:
+            onward(at.z)
+        else:
+            pl.when(at.z - distance + 1 >= 0)(lambda: onward(at.z - distance + 1))
+            pl.when(at.z + distance - 1 < LAYERS)(lambda: onward(at.z + distance - 1))
+    if wide:
+        pl.when(at.z == LAYERS - 1)(lambda: onward(0))
+        pl.when(at.z == 0)(lambda: onward(LAYERS - 1))
+
+    keep.wait()
+    own = here(at.slot)
+    for layer in range(LAYERS):
+        arriving = [(10, at.second_column)]
+        if wide:
+            arriving.append((14, at.far_column))
+        for sem, column in arriving:
+            slot = place(layer, column)
+            copy(sem + layer, own, slot, at.second).wait_recv()
+            if both:
+                mirror(slot, here(slot)).start()
+    if both:
+        for slot in range(at.stride * LAYERS):
+            pltpu.make_async_remote_copy(
+                src_ref=own,
+                dst_ref=out_ref.at[slot, 1 - at.core],
+                send_sem=send_sem.at[18 + slot],
+                recv_sem=recv_sem.at[18 + slot],
+                device_id=(at.dp, 1 - at.core),
+                device_id_type=MESH,
+            ).wait_recv()
+            mirror(slot, own).wait_send()
+    for sem in range(6, 18) if wide else range(10, 14):
+        copy(sem, own, at.slot, at.second).wait_send()
+    for distance in range(LAYERS - 1):
+
+        @pl.when(jnp.logical_and(at.has_above, at.z - distance >= 0))
+        def _():
+            up(distance, own).wait_send()
+
+        @pl.when(jnp.logical_and(at.has_below, at.z + distance < LAYERS))
+        def _():
+            down(distance, own).wait_send()
+
+
+def gather(number, block, wide=True, both=False):
+    chips = 16 if wide else 8
+    shape = (chips,) + ((2,) if both else ()) + block.shape
+    count = 18 + both * chips
+    return pl.pallas_call(
+        functools.partial(gather_kernel, wide, both),
+        out_shape=jax.ShapeDtypeStruct(shape, block.dtype),
+        in_specs=[ANYWHERE],
+        out_specs=ANYWHERE,
+        scratch_shapes=[
+            pltpu.SemaphoreType.DMA((count,)),
+            pltpu.SemaphoreType.DMA((count,)),
+            pltpu.SemaphoreType.DMA,
+        ],
+        compiler_params=params(number),
+        name=f"gather_{chips}" + ("_both" if both else ""),
+    )(block)
+
+
+def reduce_kernel(wide, pair, share, in_ref, out_ref, *scratch):
+    if pair:
+        *scratch, paired, pair_send, pair_recv = scratch
+    own, from_second, from_first, from_z, send_sem, recv_sem, own_sem = scratch
+    at = Place(wide)
+
+    def copy(sem, source, target, mate):
+        return pltpu.make_async_remote_copy(
+            src_ref=source,
+            dst_ref=target,
+            send_sem=send_sem.at[sem],
+            recv_sem=recv_sem.at[sem],
+            device_id=(mate, at.core),
+            device_id_type=MESH,
+        )
+
+    def place(layer, column):
+        return layer * at.stride + column
+
+    def load(slot):
+        source = in_ref.at[slot, at.core] if pair else in_ref.at[slot]
+        return pltpu.make_async_copy(source, own.at[slot], own_sem.at[slot])
+
+    def to_mate(slot):
+        return pltpu.make_async_remote_copy(
+            src_ref=in_ref.at[slot, 1 - at.core],
+            dst_ref=paired.at[slot],
+            send_sem=pair_send.at[slot],
+            recv_sem=pair_recv.at[slot],
+            device_id=(at.dp, 1 - at.core),
+            device_id_type=MESH,
+        )
+
+    def to_second(half, layer):
+        column = at.far_column if half == 0 else at.second_column
+        source = own if pair else in_ref
+        return copy(
+            4 * half + layer,
+            source.at[place(layer, column)],
+            from_second.at[4 * half + layer],
+            at.second,
+        )
+
+    def first_slot(layer):
+        return place(layer, at.first_column)
+
+    def own_slot(layer):
+        return place(layer, at.column)
+
+    def to_first(layer):
+        return copy(8 + layer, own.at[first_slot(layer)], from_first.at[layer], at.first)
+
+    def up(layer):
+        return copy(12 + layer, own.at[own_slot(layer)], from_z.at[layer], at.dp + 4)
+
+    def down(layer):
+        return copy(16 + layer, own.at[own_slot(layer)], from_z.at[4 + layer], at.dp - 4)
+
+    def value(ref, index):
+        return ref[index].astype(jnp.float32)
+
+    def join(slot):
+        load(slot).wait()
+        to_mate(slot).wait_recv()
+        own[slot] = (value(own, slot) + value(paired, slot)).astype(own.dtype)
+
+    at.greet(pair or share)
+    halves = (0, 1) if wide else (1,)
+    for half in halves:
+        for layer in ORDER:
+            away = place(layer, at.far_column if half == 0 else at.second_column)
+            keep = first_slot(layer) if half == 0 else own_slot(layer)
+            if pair:
+                for slot in (away, keep):
+                    to_mate(slot).start()
+                    load(slot).start()
+            else:
+                to_second(half, layer).start()
+                load(keep).start()
+    if pair:
+        for half in halves:
+            for layer in ORDER:
+                join(place(layer, at.far_column if half == 0 else at.second_column))
+                to_second(half, layer).start()
+        for layer in ORDER:
+            if wide:
+                join(first_slot(layer))
+            join(own_slot(layer))
+
+    if wide:
+        for layer in ORDER:
+            slot = first_slot(layer)
+            if not pair:
+                load(slot).wait()
+            to_second(0, layer).wait_recv()
+            own[slot] = (value(own, slot) + value(from_second, layer)).astype(own.dtype)
+            to_first(layer).start()
+    result = out_ref.at[at.core] if share else out_ref
+    for layer in ORDER:
+        slot = own_slot(layer)
+        if not pair:
+            load(slot).wait()
+        to_second(1, layer).wait_recv()
+        total = value(own, slot) + value(from_second, 4 + layer)
+        if wide:
+            to_first(layer).wait_recv()
+            total = total + value(from_first, layer)
+        own[slot] = total.astype(own.dtype)
+
+        @pl.when(at.z < layer)
+        def _():
+            @pl.when(at.has_below)
+            def _():
+                up(layer).wait_recv()
+                own[slot] = (value(own, slot) + value(from_z, layer)).astype(own.dtype)
+
+            up(layer).start()
+
+        @pl.when(at.z > layer)
+        def _():
+            @pl.when(at.has_above)
+            def _():
+                down(layer).wait_recv()
+                own[slot] = (value(own, slot) + value(from_z, 4 + layer)).astype(own.dtype)
+
+            down(layer).start()
+
+        @pl.when(at.z == layer)
+        def _():
+            result[...] = total.astype(out_ref.dtype)
+
+    for layer in range(LAYERS):
+
+        @pl.when(at.z == layer)
+        def _():
+            @pl.when(at.has_below)
+            def _():
+                up(layer).wait_recv()
+                result[...] = (result[...].astype(jnp.float32) + value(from_z, layer)).astype(
+                    out_ref.dtype
+                )
+
+            @pl.when(at.has_above)
+            def _():
+                down(layer).wait_recv()
+                result[...] = (result[...].astype(jnp.float32) + value(from_z, 4 + layer)).astype(
+                    out_ref.dtype
+                )
+
+    if share:
+
+        def give(core):
+            return pltpu.make_async_remote_copy(
+                src_ref=result,
+                dst_ref=out_ref.at[core],
+                send_sem=send_sem.at[20],
+                recv_sem=recv_sem.at[20],
+                device_id=(at.dp, 1 - at.core),
+                device_id_type=MESH,
+            )
+
+        give(at.core).start()
+        give(1 - at.core).wait_recv()
+        give(at.core).wait_send()
+    if pair:
+        for slot in range(at.stride * LAYERS):
+            to_mate(slot).wait_send()
+    for layer in range(LAYERS):
+        for half in halves:
+            to_second(half, layer).wait_send()
+        if wide:
+            to_first(layer).wait_send()
+        pl.when(at.z < layer)(lambda: up(layer).wait_send())
+        pl.when(at.z > layer)(lambda: down(layer).wait_send())
+
+
+def reduce(number, blocks, wide=True, pair=False, share=False):
+    chips = 16 if wide else 8
+    block = blocks.shape[-2:]
+    kind = blocks.dtype
+    scratch = [
+        pltpu.VMEM((chips,) + block, kind),
+        pltpu.VMEM((8,) + block, kind),
+        pltpu.VMEM((4,) + block, kind),
+        pltpu.VMEM((8,) + block, kind),
+        pltpu.SemaphoreType.DMA((21,)),
+        pltpu.SemaphoreType.DMA((21,)),
+        pltpu.SemaphoreType.DMA((chips,)),
+    ]
+    if pair:
+        scratch += [
+            pltpu.VMEM((chips,) + block, kind),
+            pltpu.SemaphoreType.DMA((chips,)),
+            pltpu.SemaphoreType.DMA((chips,)),
+        ]
+    return pl.pallas_call(
+        functools.partial(reduce_kernel, wide, pair, share),
+        out_shape=jax.ShapeDtypeStruct(((2,) if share else ()) + block, jnp.float32),
+        in_specs=[ANYWHERE],
+        out_specs=IN_VMEM,
+        scratch_shapes=scratch,
+        compiler_params=params(number),
+        name=f"reduce_{chips}" + ("_pair" if pair else "") + ("_share" if share else ""),
+    )(blocks)
+
+
+def trade_kernel(count, *refs):
+    in_refs, out_refs = (refs[:count], refs[count : 2 * count])
+    send_sem, recv_sem, own_sem = refs[2 * count :]
+    dp, core = (lax.axis_index(DP), lax.axis_index(TENSOR))
+    others = 4 * LAYERS - 1
+    barrier = pltpu.get_barrier_semaphore()
+
+    def peer(step):
+        return (dp + step) % (4 * LAYERS)
+
+    @pl.loop(1, others + 1)
+    def _(step):
+        pl.semaphore_signal(barrier, inc=1, device_id=(peer(step), core), device_id_type=MESH)
+
+    pl.semaphore_wait(barrier, others)
+
+    def copy(index, step):
+        return pltpu.make_async_remote_copy(
+            src_ref=in_refs[index].at[peer(step)],
+            dst_ref=out_refs[index].at[dp],
+            send_sem=send_sem.at[index, step - 1],
+            recv_sem=recv_sem.at[index, step - 1],
+            device_id=(peer(step), core),
+            device_id_type=MESH,
+        )
+
+    def keep(index):
+        return pltpu.make_async_copy(
+            in_refs[index].at[dp], out_refs[index].at[dp], own_sem.at[index]
+        )
+
+    for index in range(count):
+        keep(index).start()
+
+        @pl.loop(1, others + 1)
+        def _(step):
+            copy(index, step).start()
+
+    for index in range(count):
+        keep(index).wait()
+
+        @pl.loop(1, others + 1)
+        def _(step):
+            copy(index, step).wait()
+
+
+def trade(number, *blocks):
+    count = len(blocks)
+    return pl.pallas_call(
+        functools.partial(trade_kernel, count),
+        out_shape=[jax.ShapeDtypeStruct(b.shape, b.dtype) for b in blocks],
+        in_specs=[ANYWHERE] * count,
+        out_specs=[ANYWHERE] * count,
+        scratch_shapes=[
+            pltpu.SemaphoreType.DMA((count, 15)),
+            pltpu.SemaphoreType.DMA((count, 15)),
+            pltpu.SemaphoreType.DMA((count,)),
+        ],
+        compiler_params=params(number),
+        name="trade",
+    )(*blocks)
+
+
+def add_core_kernel(pieces, in_ref, out_ref, theirs, send_sem, recv_sem):
+    dp, core = (lax.axis_index(DP), lax.axis_index(TENSOR))
+    barrier = pltpu.get_barrier_semaphore()
+    pl.semaphore_signal(barrier, inc=1, device_id=(dp, 1 - core), device_id_type=MESH)
+    pl.semaphore_wait(barrier, 1)
+    rows = in_ref.shape[0] // pieces
+
+    def copy(piece):
+        at = pl.ds(piece * rows, rows)
+        return pltpu.make_async_remote_copy(
+            src_ref=in_ref.at[at],
+            dst_ref=theirs.at[at],
+            send_sem=send_sem.at[piece],
+            recv_sem=recv_sem.at[piece],
+            device_id=(dp, 1 - core),
+            device_id_type=MESH,
+        )
+
+    for piece in range(pieces):
+        copy(piece).start()
+    for piece in range(pieces):
+        at = pl.ds(piece * rows, rows)
+        copy(piece).wait_recv()
+        out_ref[at] = in_ref[at].astype(jnp.float32) + theirs[at].astype(jnp.float32)
+    for piece in range(pieces):
+        copy(piece).wait_send()
+
+
+def add_core(number, block):
+    pieces = 4
+    return pl.pallas_call(
+        functools.partial(add_core_kernel, pieces),
+        out_shape=jax.ShapeDtypeStruct(block.shape, jnp.float32),
+        in_specs=[IN_VMEM],
+        out_specs=IN_VMEM,
+        scratch_shapes=[
+            pltpu.VMEM(block.shape, block.dtype),
+            pltpu.SemaphoreType.DMA((pieces,)),
+            pltpu.SemaphoreType.DMA((pieces,)),
+        ],
+        compiler_params=params(number),
+        name="add_core",
+    )(block)
+
+
+def total_kernel(in_ref, out_ref, tiles, held, send_sem, recv_sem):
+    dp, core = (lax.axis_index(DP), lax.axis_index(TENSOR))
+    others = 4 * LAYERS - 1
+    barrier = pltpu.get_barrier_semaphore()
+
+    def peer(step):
+        return (dp + step) % (4 * LAYERS)
+
+    pl.semaphore_signal(barrier, inc=1, device_id=(dp, 1 - core), device_id_type=MESH)
+
+    @pl.loop(1, others + 1)
+    def _(step):
+        pl.semaphore_signal(barrier, inc=1, device_id=(peer(step), core), device_id_type=MESH)
+
+    pl.semaphore_wait(barrier, others + 1)
+    across = pltpu.make_async_remote_copy(
+        src_ref=in_ref,
+        dst_ref=tiles.at[0],
+        send_sem=send_sem.at[0],
+        recv_sem=recv_sem.at[0],
+        device_id=(dp, 1 - core),
+        device_id_type=MESH,
+    )
+    across.start()
+    across.wait()
+    held[...] = in_ref[...] + tiles[0]
+
+    def copy(step):
+        return pltpu.make_async_remote_copy(
+            src_ref=held,
+            dst_ref=tiles.at[step],
+            send_sem=send_sem.at[step],
+            recv_sem=recv_sem.at[step],
+            device_id=(peer(step), core),
+            device_id_type=MESH,
+        )
+
+    @pl.loop(1, others + 1)
+    def _(step):
+        copy(step).start()
+
+    @pl.loop(1, others + 1)
+    def _(step):
+        copy(step).wait()
+
+    total = jnp.zeros_like(held)
+    for chip in range(4 * LAYERS):
+        step = (dp - chip + 4 * LAYERS) % (4 * LAYERS)
+        part = jnp.where(step == 0, held[...], tiles[step])
+        total = total + part
+    out_ref[...] = total
+
+
+def total(number, tile):
+    return pl.pallas_call(
+        total_kernel,
+        out_shape=jax.ShapeDtypeStruct(tile.shape, tile.dtype),
+        in_specs=[IN_VMEM],
+        out_specs=IN_VMEM,
+        scratch_shapes=[
+            pltpu.VMEM((16,) + tile.shape, tile.dtype),
+            pltpu.VMEM(tile.shape, tile.dtype),
+            pltpu.SemaphoreType.DMA((16,)),
+            pltpu.SemaphoreType.DMA((16,)),
+        ],
+        compiler_params=params(number),
+        name="total",
+    )(tile)
+
+
+def layer_order(step):
+    odd = step % 2
+    return (1 - odd) * (LAYERS - 1 - step // 2) + odd * (step // 2)
+
+
+def remote(source, target, send_sem, recv_sem, device):
+    return pltpu.make_async_remote_copy(
+        src_ref=source,
+        dst_ref=target,
+        send_sem=send_sem,
+        recv_sem=recv_sem,
+        device_id=device,
+        device_id_type=MESH,
+    )
+
+
+def by_distance(at, step):
+    flip = at.z // 2
+    inner = at.z * (1 - flip) + (LAYERS - 1 - at.z) * flip
+    early = 1 - step // 2
+    base = (1 - inner) * step + inner * (early * (1 - step) + (1 - early) * step)
+    return (1 - flip) * base + flip * (LAYERS - 1 - base)
+
+
+def gather_stage(at, out, use, send_sem, recv_sem):
+    everyone = 4 * LAYERS
+
+    def send(slot, sem, mate):
+        return remote(
+            out.at[slot], out.at[slot], send_sem.at[sem], recv_sem.at[slot], (mate, at.core)
+        )
+
+    @pl.loop(0, everyone)
+    def _(step):
+        late = step // 8
+        rest = step % 8
+        last = rest // 7
+        even = 1 - rest % 2
+        is_first = (1 - late) * (last + even * ((rest + 6) // 8))
+        is_own = (1 - late) * (1 - is_first)
+        near = is_own * ((rest + 1) // 2) + is_first * ((rest - 1) // 2)
+        layer = by_distance(at, (1 - late) * near + late * (rest // 2))
+        column = (
+            is_own * at.column
+            + is_first * at.first_column
+            + late * ((1 - rest % 2) * at.second_column + rest % 2 * at.far_column)
+        )
+        slot = layer * 4 + column
+
+        @pl.when(slot != at.slot)
+        def _():
+            send(slot, 0, at.dp).wait_recv()
+
+        @pl.when(is_own == 1)
+        def _():
+            @pl.when(jnp.logical_and(layer <= at.z, at.has_above))
+            def _():
+                send(slot, layer, at.dp + 4).start()
+
+            @pl.when(jnp.logical_and(layer >= at.z, at.has_below))
+            def _():
+                send(slot, 4 + layer, at.dp - 4).start()
+
+            send(slot, 8 + layer, at.first).start()
+            send(slot, 12 + layer, at.second).start()
+
+        @pl.when(is_first == 1)
+        def _():
+            send(slot, 16 + layer, at.second).start()
+
+        use(slot)
+
+    @pl.loop(0, LAYERS)
+    def _(layer):
+        @pl.when(jnp.logical_and(layer <= at.z, at.has_above))
+        def _():
+            send(at.slot, layer, at.dp + 4).wait_send()
+
+        @pl.when(jnp.logical_and(layer >= at.z, at.has_below))
+        def _():
+            send(at.slot, 4 + layer, at.dp - 4).wait_send()
+
+        for group in (8, 12, 16):
+            send(at.slot, group + layer, at.first).wait_send()
+
+
+def reduce_stage(at, blocks, produce, pieces, result, from_second, from_first, from_z, send_sem, recv_sem, meanwhile=None):
+    rows = blocks.shape[1] // pieces
+
+    def part(ref, index, piece):
+        return ref.at[index, pl.ds(piece * rows, rows)]
+
+    def copy(sem, piece, source, target, mate):
+        return remote(
+            part(blocks, source, piece),
+            part(target[0], target[1], piece),
+            send_sem.at[sem, piece],
+            recv_sem.at[sem, piece],
+            (mate, at.core),
+        )
+
+    def to_second(half, layer, piece, slot):
+        return copy(4 * half + layer, piece, slot, (from_second, 4 * half + layer), at.second)
+
+    def to_first(layer, piece):
+        return copy(
+            8 + layer, piece, layer * 4 + at.first_column, (from_first, layer), at.first
+        )
+
+    def up(layer, piece):
+        return copy(12 + layer, piece, layer * 4 + at.column, (from_z, layer), at.dp + 4)
+
+    def down(layer, piece):
+        return copy(16 + layer, piece, layer * 4 + at.column, (from_z, 4 + layer), at.dp - 4)
+
+    def value(ref, index, piece):
+        return part(ref, index, piece)[...].astype(jnp.float32)
+
+    @pl.loop(0, 4 * LAYERS)
+    def _(step):
+        kind = step // LAYERS
+        keep, second = (kind // 2, kind % 2)
+        column = (1 - second) * ((1 - keep) * at.far_column + keep * at.first_column) + second * (
+            (1 - keep) * at.second_column + keep * at.column
+        )
+        layer = layer_order(step % LAYERS)
+        slot = layer * 4 + column
+        produce(slot)
+
+        @pl.when(keep == 0)
+        def _():
+            for piece in range(pieces):
+                to_second(second, layer, piece, slot).start()
+
+    if meanwhile is not None:
+        meanwhile()
+
+    @pl.loop(0, LAYERS * pieces)
+    def _(step):
+        layer, piece = (layer_order(step // pieces), step % pieces)
+        slot = layer * 4 + at.first_column
+        to_second(0, layer, piece, slot).wait_recv()
+        part(blocks, slot, piece)[...] = (
+            value(blocks, slot, piece) + value(from_second, layer, piece)
+        ).astype(blocks.dtype)
+        to_first(layer, piece).start()
+
+    @pl.loop(0, LAYERS * pieces)
+    def _(step):
+        layer, piece = (layer_order(step // pieces), step % pieces)
+        slot = layer * 4 + at.column
+        to_second(1, layer, piece, slot).wait_recv()
+        to_first(layer, piece).wait_recv()
+        summed = (
+            value(blocks, slot, piece)
+            + value(from_second, 4 + layer, piece)
+            + value(from_first, layer, piece)
+        )
+
+        @pl.when(at.z == layer)
+        def _():
+            result[pl.ds(piece * rows, rows)] = summed
+
+        @pl.when(at.z < layer)
+        def _():
+            part(blocks, slot, piece)[...] = summed.astype(blocks.dtype)
+
+            @pl.when(at.has_below)
+            def _():
+                up(layer, piece).wait_recv()
+                part(blocks, slot, piece)[...] = (
+                    value(blocks, slot, piece) + value(from_z, layer, piece)
+                ).astype(blocks.dtype)
+
+            up(layer, piece).start()
+
+        @pl.when(at.z > layer)
+        def _():
+            part(blocks, slot, piece)[...] = summed.astype(blocks.dtype)
+
+            @pl.when(at.has_above)
+            def _():
+                down(layer, piece).wait_recv()
+                part(blocks, slot, piece)[...] = (
+                    value(blocks, slot, piece) + value(from_z, 4 + layer, piece)
+                ).astype(blocks.dtype)
+
+            down(layer, piece).start()
+
+    @pl.loop(0, pieces)
+    def _(piece):
+        @pl.when(at.has_below)
+        def _():
+            up(at.z, piece).wait_recv()
+            result[pl.ds(piece * rows, rows)] += value(from_z, at.z, piece)
+
+        @pl.when(at.has_above)
+        def _():
+            down(at.z, piece).wait_recv()
+            result[pl.ds(piece * rows, rows)] += value(from_z, 4 + at.z, piece)
+
+    @pl.loop(0, LAYERS * pieces)
+    def _(step):
+        layer, piece = (step // pieces, step % pieces)
+        to_second(0, layer, piece, at.slot).wait_send()
+        to_second(1, layer, piece, at.slot).wait_send()
+        to_first(layer, piece).wait_send()
+        pl.when(at.z < layer)(lambda: up(layer, piece).wait_send())
+        pl.when(at.z > layer)(lambda: down(layer, piece).wait_send())
+
+
+def reduce_scratch(block, pieces):
+    kind = jnp.bfloat16
+    return [
+        pltpu.VMEM((4 * LAYERS,) + block, kind),
+        pltpu.VMEM((8,) + block, kind),
+        pltpu.VMEM((4,) + block, kind),
+        pltpu.VMEM((8,) + block, kind),
+        pltpu.SemaphoreType.DMA((20, pieces)),
+        pltpu.SemaphoreType.DMA((20, pieces)),
+    ]
+
+
+def gather_scratch():
+    return [pltpu.SemaphoreType.DMA((20,)), pltpu.SemaphoreType.DMA((16,))]
+
+
+def mean_of_groups(sums, count):
+    size = C // GROUPS
+    channels = sums.shape[-1]
+    row = lax.broadcasted_iota(jnp.int32, (channels, channels), 0) // size
+    column = lax.broadcasted_iota(jnp.int32, (channels, channels), 1) // size
+    same = jnp.where(row == column, 1.0 / (count * size), 0.0)
+    return jnp.dot(sums, same, precision=HIGHEST, preferred_element_type=jnp.float32)
+
+
+def side_by_side(maps, breadth, turned=False):
+    positions = maps.shape[0]
+    column = lax.broadcasted_iota(jnp.int32, maps.shape, 0) % breadth
+    before = jnp.where(column == 0, 0.0, pltpu.roll(maps, 1, 0))
+    after = jnp.where(column == breadth - 1, 0.0, pltpu.roll(maps, positions - 1, 0))
+    three = (after, maps, before) if turned else (before, maps, after)
+    return jnp.concatenate(three, axis=1)
+
+
+def fold_three(products, breadth, turned=False):
+    positions = products.shape[0]
+    channels = products.shape[1] // 3
+    left, middle, right = (products[:, tap * channels : (tap + 1) * channels] for tap in range(3))
+    if turned:
+        left, right = (right, left)
+    column = lax.broadcasted_iota(jnp.int32, middle.shape, 0) % breadth
+    before = jnp.where(column == 0, 0.0, pltpu.roll(left, 1, 0))
+    after = jnp.where(column == breadth - 1, 0.0, pltpu.roll(right, positions - 1, 0))
+    return before + middle + after
+
+
+def fold_rows(above, same, below, breadth):
+    edge = jnp.zeros((breadth, same.shape[1]), jnp.float32)
+    count = same.shape[0] - breadth
+    down = jnp.concatenate([edge, above[:count]], axis=0)
+    up = jnp.concatenate([below[breadth:], edge], axis=0)
+    return down + same + up
+
+
+def silu(z):
+    return z * jax.nn.sigmoid(z)
+
+
+def store_padded(ref, index, maps, breadth):
+    positions = maps.shape[0]
+    edge = jnp.zeros((breadth, maps.shape[1]), ref.dtype)
+    ref[index, pl.ds(0, breadth)] = edge
+    ref[index, pl.ds(breadth, positions)] = maps.astype(ref.dtype)
+    ref[index, pl.ds(breadth + positions, breadth)] = edge
+
+
+def res_forward_kernel(
+    breadth,
+    pictures,
+    gain_bias,
+    conv_one,
+    conv_two,
+    conv_half,
+    mods,
+    picks,
+    tokens,
+    act_out,
+    taps_one_out,
+    taps_half,
+    middle,
+    stats,
+    acts,
+    taps_one,
+    mine,
+    theirs,
+    pair_send,
+    pair_recv,
+    share_send,
+    share_recv,
+    out_sem,
+    *scratch,
+):
+    first_reduce, (act_send, act_recv), last_reduce = (scratch[:6], scratch[6:8], scratch[8:])
+    at = Place(True)
+    at.greet(True)
+    images, positions, channels = pictures.shape
+    tokens_len = positions // 4
+
+    @pl.loop(0, images)
+    def _(i):
+        x = pictures[i].astype(jnp.float32)
+        stats[0, pl.ds(i, 1)] = jnp.sum(x, axis=0, keepdims=True)
+
+    stats[0] = mean_of_groups(stats[0], positions)
+
+    @pl.loop(0, images)
+    def _(i):
+        x = pictures[i].astype(jnp.float32) - stats[0, pl.ds(i, 1)]
+        stats[1, pl.ds(i, 1)] = jnp.sum(x * x, axis=0, keepdims=True)
+
+    stats[1] = lax.rsqrt(mean_of_groups(stats[1], positions) + GN_EPS)
+
+    @pl.loop(0, images)
+    def _(i):
+        normed = (pictures[i].astype(jnp.float32) - stats[0, pl.ds(i, 1)]) * stats[1, pl.ds(i, 1)]
+        act = silu(normed * gain_bias[0:1] + gain_bias[1:2])
+        store_padded(taps_one, i, side_by_side(act, breadth), breadth)
+
+    save_taps = pltpu.make_async_copy(taps_one, taps_one_out, out_sem.at[0])
+    save_taps.start()
+
+    def first_product(slot):
+        total = jnp.zeros((positions, conv_one.shape[2]), jnp.float32)
+        for a in range(3):
+            total += dot(taps_one[slot, pl.ds(a * breadth, positions)], conv_one[a])
+        first_reduce[0][slot] = total.astype(jnp.bfloat16)
+
+    reduce_stage(at, first_reduce[0], first_product, 2, middle, *first_reduce[1:])
+
+    x = middle[...]
+    center = mean_of_groups(jnp.sum(x, axis=0, keepdims=True), positions)
+    x = x - center
+    scale = lax.rsqrt(mean_of_groups(jnp.sum(x * x, axis=0, keepdims=True), positions) + GN_EPS)
+    acts[at.slot] = silu(x * scale * (1.0 + mods[0:1]) + mods[1:2]).astype(jnp.bfloat16)
+
+    def swap(slot):
+        return remote(
+            mine.at[slot],
+            theirs.at[slot],
+            pair_send.at[slot],
+            pair_recv.at[slot],
+            (at.dp, 1 - at.core),
+        )
+
+    def second_product(slot):
+        act = acts[slot]
+        above, same, below = (dot(act, conv_two[a]) for a in range(3))
+        folded = fold_three(fold_rows(above, same, below, breadth), breadth)
+        mine[slot] = folded.astype(jnp.bfloat16)
+        swap(slot).start()
+
+    gather_stage(at, acts, second_product, act_send, act_recv)
+    save_acts = pltpu.make_async_copy(acts, act_out, out_sem.at[1])
+    save_acts.start()
+
+    def half_product(slot):
+        swap(slot).wait_recv()
+        branch = mine[slot].astype(jnp.float32) + theirs[slot].astype(jnp.float32)
+        resid = (pictures[slot].astype(jnp.float32) + branch).astype(jnp.bfloat16)
+        three = side_by_side(resid.astype(jnp.float32), breadth).astype(jnp.bfloat16)
+        picked = dot(picks[...], three).astype(jnp.bfloat16)
+        total = jnp.zeros((tokens_len, conv_half.shape[2]), jnp.float32)
+        for a in range(3):
+            part = picked[a * tokens_len : (a + 1) * tokens_len]
+            taps_half[a, slot] = part
+            total += dot(part, conv_half[a])
+        last_reduce[0][slot] = total.astype(jnp.bfloat16)
+
+    own = tokens.at[at.core]
+    reduce_stage(at, last_reduce[0], half_product, 1, own, *last_reduce[1:])
+
+    def give(core):
+        return remote(own, tokens.at[core], share_send, share_recv, (at.dp, 1 - at.core))
+
+    give(at.core).start()
+    give(1 - at.core).wait_recv()
+    give(at.core).wait_send()
+
+    @pl.loop(0, images)
+    def _(slot):
+        swap(slot).wait_send()
+
+    save_taps.wait()
+    save_acts.wait()
+
+
+def res_forward(number, breadth, pictures, gain_bias, conv_one, conv_two, conv_half, mods, picks):
+    images, positions, channels = pictures.shape
+    half_c = conv_one.shape[2]
+    half_d = conv_half.shape[2]
+    tokens_len = positions // 4
+    three = 3 * channels
+    padded = (images, positions + 2 * breadth, three)
+    low = jnp.bfloat16
+    acts = (images, positions, half_c)
+    return pl.pallas_call(
+        functools.partial(res_forward_kernel, breadth),
+        out_shape=[
+            jax.ShapeDtypeStruct((2, tokens_len, half_d), jnp.float32),
+            jax.ShapeDtypeStruct(acts, low),
+            jax.ShapeDtypeStruct(padded, low),
+            jax.ShapeDtypeStruct((3, images, tokens_len, three), low),
+            jax.ShapeDtypeStruct((positions, half_c), jnp.float32),
+            jax.ShapeDtypeStruct((2, images, channels), jnp.float32),
+        ],
+        in_specs=[IN_VMEM] * 7,
+        out_specs=[IN_VMEM, ANYWHERE, ANYWHERE, IN_VMEM, IN_VMEM, IN_VMEM],
+        scratch_shapes=[
+            pltpu.VMEM(acts, low),
+            pltpu.VMEM(padded, low),
+            pltpu.VMEM(pictures.shape, low),
+            pltpu.VMEM(pictures.shape, low),
+            pltpu.SemaphoreType.DMA((images,)),
+            pltpu.SemaphoreType.DMA((images,)),
+            pltpu.SemaphoreType.DMA,
+            pltpu.SemaphoreType.DMA,
+            pltpu.SemaphoreType.DMA((2,)),
+        ]
+        + reduce_scratch((positions, half_c), 2)
+        + gather_scratch()
+        + reduce_scratch((tokens_len, half_d), 1),
+        compiler_params=params(number),
+        name="res_forward",
+    )(pictures, gain_bias, conv_one, conv_two, conv_half, mods, picks)
+
+
+def silu_slope(z):
+    gate = jax.nn.sigmoid(z)
+    return gate * (1.0 + z * (1.0 - gate))
+
+
+def res_backward_kernel(
+    breadth,
+    shrunk,
+    pictures,
+    gain_bias,
+    conv_one,
+    conv_two,
+    conv_half,
+    mods,
+    picks,
+    taps_half,
+    middle,
+    stats,
+    acts_in,
+    taps_one_in,
+    pictures_out,
+    norm_out,
+    mods_out,
+    one_out,
+    two_out,
+    half_out,
+    gathered,
+    gathered_middle,
+    acts,
+    taps_one,
+    taps_two,
+    mine,
+    theirs,
+    back,
+    back_theirs,
+    held,
+    sums,
+    outgoing,
+    acted,
+    one_grad,
+    two_grad,
+    half_grad,
+    pair_send,
+    pair_recv,
+    back_send,
+    back_recv,
+    trade_send,
+    trade_recv,
+    io_sem,
+    *scratch,
+):
+    (shrunk_send, shrunk_recv), (middle_send, middle_recv) = (scratch[:2], scratch[2:4])
+    reducing = scratch[4:]
+    at = Place(True)
+    images, positions, channels = pictures.shape
+    others = images - 1
+    tokens_len = positions // 4
+    load_acts = pltpu.make_async_copy(acts_in, acts, io_sem.at[0])
+    load_taps = pltpu.make_async_copy(taps_one_in, taps_one, io_sem.at[1])
+    load_acts.start()
+    load_taps.start()
+    gathered[at.slot] = shrunk[...]
+
+    barrier = pltpu.get_barrier_semaphore()
+
+    def peer(step):
+        return (at.dp + step) % images
+
+    @pl.loop(1, others + 1)
+    def _(step):
+        pl.semaphore_signal(barrier, inc=1, device_id=(peer(step), at.core), device_id_type=MESH)
+
+    pl.semaphore_signal(barrier, inc=1, device_id=(at.dp, 1 - at.core), device_id_type=MESH)
+    pl.semaphore_wait(barrier, others + 1)
+
+    def swap(slot):
+        return remote(
+            mine.at[slot],
+            theirs.at[slot],
+            pair_send.at[slot],
+            pair_recv.at[slot],
+            (at.dp, 1 - at.core),
+        )
+
+    def half_back(slot):
+        products = [dot_nt(gathered[slot], conv_half[a]) for a in range(3)]
+        products = jnp.concatenate(products, axis=0)
+        coarse = products.astype(jnp.bfloat16)
+        fine = (products - coarse.astype(jnp.float32)).astype(jnp.bfloat16)
+        spread = dot_tn(picks[...], coarse) + dot_tn(picks[...], fine)
+        mine[slot] = fold_three(spread, breadth, True).astype(jnp.bfloat16)
+        swap(slot).start()
+
+    gather_stage(at, gathered, half_back, shrunk_send, shrunk_recv)
+
+    def resid(slot):
+        return mine[slot].astype(jnp.float32) + theirs[slot].astype(jnp.float32)
+
+    def second_back(slot):
+        swap(slot).wait_recv()
+        branch = resid(slot).astype(jnp.bfloat16).astype(jnp.float32)
+        store_padded(taps_two, slot, side_by_side(branch, breadth, True), breadth)
+        total = jnp.zeros((positions, conv_two.shape[1]), jnp.float32)
+        for a in range(3):
+            total += dot_nt(taps_two[slot, pl.ds((2 - a) * breadth, positions)], conv_two[a])
+        reducing[0][slot] = total.astype(jnp.bfloat16)
+
+    def weights_meanwhile():
+        half_grad[...] = jnp.zeros_like(half_grad)
+        two_grad[...] = jnp.zeros_like(two_grad)
+        load_acts.wait()
+
+        @pl.loop(0, images // 4)
+        def _(i):
+            right = gathered[pl.ds(4 * i, 4)].reshape(4 * tokens_len, -1)
+            for a in range(3):
+                left = taps_half[a, pl.ds(4 * i, 4)].reshape(4 * tokens_len, 3 * channels)
+                half_grad[a] += dot_tn(left, right)
+
+        @pl.loop(0, images)
+        def _(i):
+            right = acts[i]
+            for a in range(3):
+                left = taps_two[i, pl.ds((2 - a) * breadth, positions)]
+                two_grad[a] += dot_tn(left, right)
+
+        save(half_grad, half_out, 2).start()
+        save(two_grad, two_out, 3).start()
+
+    def save(source, target, sem):
+        return pltpu.make_async_copy(source, target, io_sem.at[sem])
+
+    reduce_stage(at, reducing[0], second_back, 2, acted, *reducing[1:], weights_meanwhile)
+
+    x = middle[...]
+    center = mean_of_groups(jnp.sum(x, axis=0, keepdims=True), positions)
+    x = x - center
+    scale = lax.rsqrt(mean_of_groups(jnp.sum(x * x, axis=0, keepdims=True), positions) + GN_EPS)
+    normed = x * scale
+    slope = 1.0 + mods[0:1]
+    grad = acted[...] * silu_slope(normed * slope + mods[1:2])
+    along = jnp.sum(grad * normed, axis=0, keepdims=True)
+    level = jnp.sum(grad, axis=0, keepdims=True)
+    mods_out[0:1] = along
+    mods_out[1:2] = level
+    along = mean_of_groups(slope * along, positions)
+    level = mean_of_groups(slope * level, positions)
+    gathered_middle[at.slot] = ((slope * grad - level - normed * along) * scale).astype(jnp.bfloat16)
+
+    def swap_back(slot):
+        return remote(
+            back.at[slot],
+            back_theirs.at[slot],
+            back_send.at[slot],
+            back_recv.at[slot],
+            (at.dp, 1 - at.core),
+        )
+
+    def first_back(slot):
+        below, same, above = (dot_nt(gathered_middle[slot], conv_one[a]) for a in range(3))
+        folded = fold_three(fold_rows(above, same, below, breadth), breadth, True)
+        back[slot] = folded.astype(jnp.bfloat16)
+        swap_back(slot).start()
+
+    gather_stage(at, gathered_middle, first_back, middle_send, middle_recv)
+
+    gain, bias = (gain_bias[0:1], gain_bias[1:2])
+
+    def normed_of(i):
+        return (pictures[i].astype(jnp.float32) - stats[0, pl.ds(i, 1)]) * stats[1, pl.ds(i, 1)]
+
+    @pl.loop(0, images)
+    def _(i):
+        swap_back(i).wait_recv()
+        grad = back[i].astype(jnp.float32) + back_theirs[i].astype(jnp.float32)
+        normed = normed_of(i)
+        grad = grad * silu_slope(normed * gain + bias)
+        held[i] = grad
+        sums[0, pl.ds(i, 1)] = jnp.sum(grad * normed, axis=0, keepdims=True)
+        sums[1, pl.ds(i, 1)] = jnp.sum(grad, axis=0, keepdims=True)
+
+    norm_out[0:1] = jnp.sum(sums[0], axis=0, keepdims=True)
+    norm_out[1:2] = jnp.sum(sums[1], axis=0, keepdims=True)
+    sums[0] = mean_of_groups(gain * sums[0], positions)
+    sums[1] = mean_of_groups(gain * sums[1], positions)
+
+    def deliver(step):
+        return remote(
+            outgoing.at[peer(step)],
+            pictures_out.at[at.dp],
+            trade_send.at[step - 1],
+            trade_recv.at[step - 1],
+            (peer(step), at.core),
+        )
+
+    keep = save(outgoing.at[at.dp], pictures_out.at[at.dp], 5)
+
+    @pl.loop(0, images)
+    def _(step):
+        i = peer(step)
+        part = gain * held[i] - sums[1, pl.ds(i, 1)] - normed_of(i) * sums[0, pl.ds(i, 1)]
+        part = resid(i) + part * stats[1, pl.ds(i, 1)]
+        half = positions // 2
+        outgoing[i] = jnp.concatenate([part[:half], part[half:]], axis=1).astype(jnp.bfloat16)
+        pl.when(step == 0)(keep.start)
+        pl.when(step > 0)(lambda: deliver(step).start())
+
+    one_grad[...] = jnp.zeros_like(one_grad)
+    load_taps.wait()
+
+    @pl.loop(0, images)
+    def _(i):
+        right = gathered_middle[i]
+        for a in range(3):
+            one_grad[a] += dot_tn(taps_one[i, pl.ds(a * breadth, positions)], right)
+
+    save(one_grad, one_out, 4).start()
+
+    @pl.loop(0, images)
+    def _(slot):
+        swap(slot).wait_send()
+        swap_back(slot).wait_send()
+
+    keep.wait()
+
+    @pl.loop(1, others + 1)
+    def _(step):
+        deliver(step).wait()
+
+    save(half_grad, half_out, 2).wait()
+    save(two_grad, two_out, 3).wait()
+    save(one_grad, one_out, 4).wait()
+
+
+def res_backward(number, breadth, *args):
+    (shrunk, pictures, gain_bias, conv_one, conv_two, conv_half, mods, picks, taps_half, middle, stats, acts, taps_one) = args
+    images, positions, channels = pictures.shape
+    half_c = conv_one.shape[2]
+    half_d = conv_half.shape[2]
+    tokens_len = positions // 4
+    three = 3 * channels
+    low, full = (jnp.bfloat16, jnp.float32)
+    grads = [(3, three, half_c), (3, three, half_c), (3, three, half_d)]
+    traded = (images, positions // 2, 2 * channels)
+    return pl.pallas_call(
+        functools.partial(res_backward_kernel, breadth),
+        out_shape=[
+            jax.ShapeDtypeStruct(traded, low),
+            jax.ShapeDtypeStruct((2, channels), full),
+            jax.ShapeDtypeStruct((2, half_c), full),
+        ]
+        + [jax.ShapeDtypeStruct(shape, full) for shape in grads],
+        in_specs=[IN_VMEM] * 11 + [ANYWHERE] * 2,
+        out_specs=[ANYWHERE, IN_VMEM, IN_VMEM] + [ANYWHERE] * 3,
+        scratch_shapes=[
+            pltpu.VMEM((images, tokens_len, half_d), low),
+            pltpu.VMEM((images, positions, half_c), low),
+            pltpu.VMEM(acts.shape, low),
+            pltpu.VMEM(taps_one.shape, low),
+            pltpu.VMEM(taps_one.shape, low),
+            pltpu.VMEM(pictures.shape, low),
+            pltpu.VMEM(pictures.shape, low),
+            pltpu.VMEM(pictures.shape, low),
+            pltpu.VMEM(pictures.shape, low),
+            pltpu.VMEM(pictures.shape, full),
+            pltpu.VMEM((2, images, channels), full),
+            pltpu.VMEM(traded, low),
+            pltpu.VMEM((positions, half_c), full),
+        ]
+        + [pltpu.VMEM(shape, full) for shape in grads]
+        + [pltpu.SemaphoreType.DMA((images,))] * 4
+        + [pltpu.SemaphoreType.DMA((images - 1,))] * 2
+        + [pltpu.SemaphoreType.DMA((6,))]
+        + gather_scratch()
+        + gather_scratch()
+        + reduce_scratch((positions, half_c), 2),
+        compiler_params=params(number),
+        name="res_backward",
+    )(*args)
+
+
+def widen(block):
+    return block.astype(jnp.float32)
+
+
+def lower(block):
+    return block.astype(jnp.bfloat16)
+
+
+def paired_lanes(block):
+    half = block.shape[-2] // 2
+    return jnp.concatenate([block[..., :half, :], block[..., half:, :]], axis=-1)
+
+
+def unpaired_lanes(block):
+    half = block.shape[-1] // 2
+    return jnp.concatenate([block[..., :half], block[..., half:]], axis=-2)
+
+
+def trade_dp(blocks):
+    return lax.all_to_all(blocks, DP, 0, 0)
+
+
+def core_rows(block, tensor_pos):
+    half = block.shape[0] // 2
+    return lax.dynamic_slice_in_dim(block, tensor_pos * half, half, axis=0)
+
+
+def layer_stats(values):
+    center = jnp.mean(values, axis=-1, keepdims=True)
+    shifted = values - center
+    spread = jnp.mean(shifted * shifted, axis=-1, keepdims=True)
+    scale = lax.rsqrt(spread + LN_EPS)
+    return shifted * scale, scale
+
+
+def layer_back(normed, scale, grad):
+    first = jnp.mean(grad, axis=-1, keepdims=True)
+    second = jnp.mean(grad * normed, axis=-1, keepdims=True)
+    return (grad - first - normed * second) * scale
+
+
+def half_picks(height, breadth):
+    outputs = height * breadth // 4
+    tap, out = (jnp.arange(3 * outputs) // outputs, jnp.arange(3 * outputs) % outputs)
+    row = 2 * (out // (breadth // 2)) + tap - 1
+    source = row * breadth + 2 * (out % (breadth // 2))
+    place = jnp.arange(height * breadth)
+    return ((place[None, :] == source[:, None]) & (row[:, None] >= 0)).astype(jnp.bfloat16)
+
+
+def dot(left, right):
+    return jnp.dot(left, right, preferred_element_type=jnp.float32)
+
+
+def dot_tn(left, right):
+    return lax.dot_general(left, right, (((0,), (0,)), ((), ())), preferred_element_type=jnp.float32)
+
+
+def dot_nt(left, right):
+    return lax.dot_general(left, right, (((1,), (1,)), ((), ())), preferred_element_type=jnp.float32)
+
+
+def stationary(
+    images,
+    t_index,
+    cotangent,
+    norm_params,
+    norm_params_avg,
+    norm_params_sq,
+    first_conv,
+    first_conv_avg,
+    first_conv_sq,
+    resnet_mod,
+    resnet_mod_avg,
+    resnet_mod_sq,
+    second_conv,
+    second_kernel_first_moment,
+    second_conv_sq,
+    down_conv,
+    down_conv_avg,
+    down_conv_sq,
+    ada_proj,
+    ada_proj_avg,
+    ada_proj_sq,
+    qkv_proj,
+    qkv_proj_avg,
+    qkv_proj_sq,
+    out_proj,
+    out_proj_avg,
+    out_proj_sq,
+    hidden_in,
+    hidden_in_avg,
+    hidden_in_sq,
+    hidden_out,
+    hidden_out_avg,
+    hidden_out_sq,
+):
+    masters = (
+        norm_params,
+        first_conv,
+        resnet_mod,
+        second_conv,
+        down_conv,
+        ada_proj,
+        qkv_proj,
+        out_proj,
+        hidden_in,
+        hidden_out,
+    )
+    averages = (
+        norm_params_avg,
+        first_conv_avg,
+        resnet_mod_avg,
+        second_kernel_first_moment,
+        down_conv_avg,
+        ada_proj_avg,
+        qkv_proj_avg,
+        out_proj_avg,
+        hidden_in_avg,
+        hidden_out_avg,
+    )
+    squares = (
+        norm_params_sq,
+        first_conv_sq,
+        resnet_mod_sq,
+        second_conv_sq,
+        down_conv_sq,
+        ada_proj_sq,
+        qkv_proj_sq,
+        out_proj_sq,
+        hidden_in_sq,
+        hidden_out_sq,
+    )
+    n_dp = lax.axis_size(DP)
+    dp_pos = lax.axis_index(DP)
+    tensor_pos = lax.axis_index(TENSOR)
+    height, breadth = (images.shape[1], images.shape[2])
+    positions = height * breadth
+    tokens_len = positions // 4
+    local_c = C // n_dp
+    half_c = first_conv.shape[3]
+    half_d = down_conv.shape[3]
+    freq_rows = resnet_mod.shape[0]
+    heads_here = out_proj.shape[0]
+    hidden_cols = hidden_in.shape[1] // n_dp
+    score_scale = HDIM ** (-0.5)
+    as_maps = (n_dp, height, breadth, local_c)
+    picks = half_picks(height, breadth)
+    numbers = itertools.count()
+
+    def gather_tokens(block, wide):
+        gathered = gather(next(numbers), core_rows(block, tensor_pos), wide, True)
+        return gathered.reshape(-1, D)
+
+    def reduce_tokens(partial, wide):
+        blocks = lower(partial).reshape(-1, 2, tokens_len // 2, D)
+        return reduce(next(numbers), blocks, wide, True, True).reshape(tokens_len, D)
+
+    def sum_cores(maps):
+        return add_core(next(numbers), lower(maps).reshape(-1, local_c)).reshape(as_maps)
+
+    def sum_all(local):
+        return total(next(numbers), jnp.full((8, 128), local))[0, 0]
+
+    gain_bias = widen(lower(norm_params))
+    conv_one = lower(first_conv).reshape(3, 3 * local_c, half_c)
+    conv_two = lower(second_conv).transpose(0, 2, 1, 3).reshape(3, half_c, 3 * local_c)
+    conv_half = lower(down_conv).reshape(3, 3 * local_c, half_d)
+    qkv_blocks = jnp.repeat(lower(qkv_proj).transpose(2, 0, 1, 3), n_dp // heads_here, axis=0)
+    qkv_head = trade_dp(qkv_blocks).reshape(D, 3 * HDIM)
+    out_blocks = jnp.repeat(lower(out_proj), n_dp // heads_here, axis=0)
+    out_head = trade_dp(out_blocks).transpose(1, 0, 2).reshape(HDIM, D)
+    up_blocks = lower(hidden_in).reshape(D // n_dp, n_dp, hidden_cols).transpose(1, 0, 2)
+    up_here = trade_dp(up_blocks).reshape(D, hidden_cols)
+    down_blocks = lower(hidden_out).reshape(n_dp, hidden_cols, D // n_dp)
+    down_here = trade_dp(down_blocks).transpose(1, 0, 2).reshape(hidden_cols, D)
+
+    emb = embed_noise(t_index, FREQ).reshape(FREQ // 128, 128)
+    emb = jnp.broadcast_to(jnp.pad(emb, ((0, 8 - FREQ // 128), (0, 0))), (n_dp, 8, 128))
+    image_blocks = images.reshape(positions, n_dp, local_c).transpose(1, 0, 2)
+    pictures, emb = trade(next(numbers), paired_lanes(image_blocks), emb)
+    pictures = unpaired_lanes(pictures)
+
+    emb_low = lower(emb[:, : FREQ // 128].reshape(n_dp, FREQ))
+    emb_rows = lax.dynamic_slice_in_dim(emb_low, dp_pos * freq_rows, freq_rows, axis=1)
+    res_partial = dot(emb_rows, lower(resnet_mod).reshape(freq_rows, 2 * half_c))
+    ada_partial = dot(emb_rows, lower(ada_proj).reshape(freq_rows, 6 * D))
+    ada_partial = lax.dynamic_slice_in_dim(ada_partial, tensor_pos * 3 * D, 3 * D, axis=1)
+    mods = jnp.concatenate([res_partial, ada_partial], axis=1).reshape(n_dp, -1, 128)
+    mods = reduce(next(numbers), mods, True, False, True).reshape(2, -1)
+    res_mods = lax.dynamic_index_in_dim(mods, tensor_pos, 0, keepdims=False)[: 2 * half_c]
+    res_mods = res_mods.reshape(2, half_c)
+    ada_mods = mods[:, 2 * half_c :].reshape(6, D)
+    shift_one, scale_one, gate_one = (ada_mods[0], 1.0 + ada_mods[1], 1.0 + ada_mods[2])
+    shift_two, scale_two, gate_two = (ada_mods[3], 1.0 + ada_mods[4], 1.0 + ada_mods[5])
+    upstream = widen(cotangent).reshape(tokens_len, D)
+    grad_expanded = gather_tokens(lower(gate_two * upstream), True)
+
+    shrunk, act_two, taps_one, taps_half, middle, stats_one = res_forward(
+        next(numbers), breadth, pictures, gain_bias, conv_one, conv_two, conv_half, res_mods, picks
+    )
+    tokens = jnp.concatenate([shrunk[0], shrunk[1]], axis=1)
+
+    token_normed, token_spread = layer_stats(tokens)
+    attn_in = gather_tokens(lower(token_normed * scale_one + shift_one), False)
+    near = n_dp // 2
+    qkv_low = lower(dot(attn_in, qkv_head)).reshape(near, tokens_len, 3, HDIM)
+    query_low, key_low, value_low = (qkv_low[:, :, 0], qkv_low[:, :, 1], qkv_low[:, :, 2])
+    scores = (
+        jnp.einsum("bqd,bkd->bqk", query_low, key_low, preferred_element_type=jnp.float32) * score_scale
+    )
+    row_max = jnp.max(scores, axis=-1, keepdims=True)
+    log_total = row_max + jnp.log(jnp.sum(jnp.exp(scores - row_max), axis=-1, keepdims=True))
+    attention = jnp.exp(scores - log_total)
+    attention_low = lower(attention)
+    mixed = lower(
+        jnp.einsum("bqk,bkd->bqd", attention_low, value_low, preferred_element_type=jnp.float32)
+    ).reshape(near * tokens_len, HDIM)
+    attended = reduce_tokens(dot(mixed, out_head), False)
+    after_attn = tokens + gate_one * attended
+    after_normed, after_spread = layer_stats(after_attn)
+    mlp_in = gather_tokens(lower(after_normed * scale_two + shift_two), True)
+    pre_act = dot(mlp_in, up_here)
+    hidden_act, gelu_back = jax.vjp(gelu_tanh, pre_act)
+    hidden_low = lower(hidden_act)
+    expanded = reduce_tokens(dot(hidden_low, down_here), True)
+    block_out = lower(after_attn + gate_two * expanded)
+
+    grad_gate_two = jnp.sum(upstream * expanded, axis=0)
+    grad_down = dot_tn(hidden_low, grad_expanded)
+    (grad_pre,) = gelu_back(dot_nt(grad_expanded, down_here))
+    grad_pre_low = lower(grad_pre)
+    grad_mlp_in = reduce_tokens(dot_nt(grad_pre_low, up_here), True)
+    grad_up = dot_tn(mlp_in, grad_pre_low)
+    grad_after = upstream + layer_back(after_normed, after_spread, scale_two * grad_mlp_in)
+    grad_attended = gather_tokens(lower(gate_one * grad_after), False)
+    grad_out = dot_tn(mixed, grad_attended)
+    grad_mixed = lower(dot_nt(grad_attended, out_head)).reshape(near, tokens_len, HDIM)
+    grad_probs = jnp.einsum(
+        "bqd,bkd->bqk", grad_mixed, value_low, preferred_element_type=jnp.float32
+    )
+    grad_values = jnp.einsum(
+        "bqk,bqd->bkd", attention_low, grad_mixed, preferred_element_type=jnp.float32
+    )
+    grad_scores = lower(
+        attention * (grad_probs - jnp.sum(grad_probs * attention, axis=-1, keepdims=True))
+    )
+    grad_query = (
+        jnp.einsum("bqk,bkd->bqd", grad_scores, key_low, preferred_element_type=jnp.float32)
+        * score_scale
+    )
+    grad_keys = (
+        jnp.einsum("bqk,bqd->bkd", grad_scores, query_low, preferred_element_type=jnp.float32)
+        * score_scale
+    )
+    grad_qkv = lower(jnp.concatenate([grad_query, grad_keys, grad_values], axis=2)).reshape(
+        near * tokens_len, 3 * HDIM
+    )
+    grad_attn_in = reduce_tokens(dot_nt(grad_qkv, qkv_head), False)
+    grad_qkv_w = dot_tn(attn_in, grad_qkv)
+    grad_tokens = grad_after + layer_back(token_normed, token_spread, scale_one * grad_attn_in)
+
+    grad_shrunk = lower(lax.dynamic_slice_in_dim(grad_tokens, tensor_pos * half_d, half_d, axis=1))
+    images_grad, grad_norm_params, grad_res_mods, grad_conv_one, grad_conv_two, grad_half = res_backward(
+        next(numbers),
+        breadth,
+        grad_shrunk,
+        pictures,
+        gain_bias,
+        conv_one,
+        conv_two,
+        conv_half,
+        res_mods,
+        picks,
+        taps_half,
+        middle,
+        stats_one,
+        act_two,
+        taps_one,
+    )
+    images_grad = widen(unpaired_lanes(images_grad))
+    images_grad = images_grad.transpose(1, 0, 2).reshape((1, height, breadth, C))
+
+    grad_ada = jnp.concatenate(
+        [
+            jnp.sum(grad_attn_in, axis=0),
+            jnp.sum(grad_attn_in * token_normed, axis=0),
+            jnp.sum(grad_after * attended, axis=0),
+            jnp.sum(grad_mlp_in, axis=0),
+            jnp.sum(grad_mlp_in * after_normed, axis=0),
+            grad_gate_two,
+        ]
+    )
+    grad_ada = lax.dynamic_slice_in_dim(grad_ada, tensor_pos * 3 * D, 3 * D, axis=0)
+    grad_mods = jnp.concatenate([grad_res_mods.reshape(-1), grad_ada]).reshape(-1, 128)
+    grad_mods = gather(next(numbers), grad_mods, True, True).reshape(n_dp, 2, -1)
+    grad_ada = grad_mods[:, :, 2 * half_c :].reshape(n_dp, 6 * D)
+    grad_mods = lax.dynamic_index_in_dim(grad_mods, tensor_pos, 1, keepdims=False)
+    emb_cols = widen(emb_rows)
+    grad_ada = jnp.einsum("bf,bk->fk", emb_cols, grad_ada, precision=HIGHEST)
+    grad_res = jnp.einsum("bf,bk->fk", emb_cols, grad_mods[:, : 2 * half_c], precision=HIGHEST)
+
+    grad_qkv_w = trade_dp(lower(grad_qkv_w).reshape(n_dp, D // n_dp, 3, HDIM))
+    grad_qkv_w = jnp.sum(
+        widen(grad_qkv_w).reshape((heads_here, n_dp // heads_here) + grad_qkv_w.shape[1:]), axis=1
+    ).transpose(1, 2, 0, 3)
+    grad_out = trade_dp(lower(grad_out).reshape(HDIM, n_dp, D // n_dp).transpose(1, 0, 2))
+    grad_out = jnp.sum(
+        widen(grad_out).reshape((heads_here, n_dp // heads_here) + grad_out.shape[1:]), axis=1
+    )
+    grad_up = widen(trade_dp(lower(grad_up).reshape(n_dp, D // n_dp, hidden_cols)))
+    grad_up = grad_up.transpose(1, 0, 2).reshape(hidden_in.shape)
+    grad_down = trade_dp(lower(grad_down).reshape(hidden_cols, n_dp, D // n_dp).transpose(1, 0, 2))
+    grad_down = widen(grad_down).reshape(hidden_out.shape)
+
+    combined_total = (
+        grad_norm_params,
+        grad_conv_one.reshape(first_conv.shape),
+        grad_res.reshape(resnet_mod.shape),
+        grad_conv_two.reshape(3, 3, local_c, half_c).transpose(0, 1, 3, 2),
+        grad_half.reshape(down_conv.shape),
+        grad_ada.reshape(ada_proj.shape),
+        grad_qkv_w,
+        grad_out,
+        grad_up,
+        grad_down,
+    )
+    results = clipped_step(masters, averages, squares, combined_total, sum_all)
+    return (block_out[None], images_grad) + results
 
 
 def solution(mesh):
     in_specs = (
-        P("dp", None, None, None),
-        P("dp"),
-        P("dp", None, None),
-        P(None, "dp"),
-        P(None, "dp"),
-        P(None, "dp"),
-        P(None, None, "dp", "tensor"),
-        P(None, None, "dp", "tensor"),
-        P(None, None, "dp", "tensor"),
-        P("dp", None, "tensor"),
-        P("dp", None, "tensor"),
-        P("dp", None, "tensor"),
-        P(None, None, "tensor", "dp"),
-        P(None, None, "tensor", "dp"),
-        P(None, None, "tensor", "dp"),
-        P(None, None, "dp", "tensor"),
-        P(None, None, "dp", "tensor"),
-        P(None, None, "dp", "tensor"),
-        P("dp", None, None),
-        P("dp", None, None),
-        P("dp", None, None),
-        P("dp", None, "tensor", None),
-        P("dp", None, "tensor", None),
-        P("dp", None, "tensor", None),
-        P("tensor", None, "dp"),
-        P("tensor", None, "dp"),
-        P("tensor", None, "dp"),
-        P("dp", "tensor"),
-        P("dp", "tensor"),
-        P("dp", "tensor"),
-        P("tensor", "dp"),
-        P("tensor", "dp"),
-        P("tensor", "dp"),
+        P(DP, None, None, None),
+        P(DP),
+        P(DP, None, None),
+        P(None, DP),
+        P(None, DP),
+        P(None, DP),
+        P(None, None, DP, TENSOR),
+        P(None, None, DP, TENSOR),
+        P(None, None, DP, TENSOR),
+        P(DP, None, TENSOR),
+        P(DP, None, TENSOR),
+        P(DP, None, TENSOR),
+        P(None, None, TENSOR, DP),
+        P(None, None, TENSOR, DP),
+        P(None, None, TENSOR, DP),
+        P(None, None, DP, TENSOR),
+        P(None, None, DP, TENSOR),
+        P(None, None, DP, TENSOR),
+        P(DP, None, None),
+        P(DP, None, None),
+        P(DP, None, None),
+        P(DP, None, TENSOR, None),
+        P(DP, None, TENSOR, None),
+        P(DP, None, TENSOR, None),
+        P(TENSOR, None, DP),
+        P(TENSOR, None, DP),
+        P(TENSOR, None, DP),
+        P(DP, TENSOR),
+        P(DP, TENSOR),
+        P(DP, TENSOR),
+        P(TENSOR, DP),
+        P(TENSOR, DP),
+        P(TENSOR, DP),
     )
     out_specs = (
-        P("dp", None, None),
-        P("dp", None, None, None),
+        P(DP, None, None),
+        P(DP, None, None, None),
         P(),
-        P(None, "dp"),
-        P(None, "dp"),
-        P(None, "dp"),
-        P(None, None, "dp", "tensor"),
-        P(None, None, "dp", "tensor"),
-        P(None, None, "dp", "tensor"),
-        P("dp", None, "tensor"),
-        P("dp", None, "tensor"),
-        P("dp", None, "tensor"),
-        P(None, None, "tensor", "dp"),
-        P(None, None, "tensor", "dp"),
-        P(None, None, "tensor", "dp"),
-        P(None, None, "dp", "tensor"),
-        P(None, None, "dp", "tensor"),
-        P(None, None, "dp", "tensor"),
-        P("dp", None, None),
-        P("dp", None, None),
-        P("dp", None, None),
-        P("dp", None, "tensor", None),
-        P("dp", None, "tensor", None),
-        P("dp", None, "tensor", None),
-        P("tensor", None, "dp"),
-        P("tensor", None, "dp"),
-        P("tensor", None, "dp"),
-        P("dp", "tensor"),
-        P("dp", "tensor"),
-        P("dp", "tensor"),
-        P("tensor", "dp"),
-        P("tensor", "dp"),
-        P("tensor", "dp"),
-    )
+        P(None, DP),
+        P(None, DP),
+        P(None, DP),
+        P(None, None, DP, TENSOR),
+        P(None, None, DP, TENSOR),
+        P(None, None, DP, TENSOR),
+        P(DP, None, TENSOR),
+        P(DP, None, TENSOR),
+        P(DP, None, TENSOR),
+        P(None, None, TENSOR, DP),
+        P(None, None, TENSOR, DP),
+        P(None, None, TENSOR, DP),
+        P(None, None, DP, TENSOR),
+        P(None, None, DP, TENSOR),
+        P(None, None, DP, TENSOR),
+        P(DP, None, None),
+        P(DP, None, None),
+        P(DP, None, None),
+        P(DP, None, TENSOR, None),
+        P(DP, None, TENSOR, None),
+        P(DP, None, TENSOR, None),
+        P(TENSOR, None, DP),
+        P(TENSOR, None, DP),
+        P(TENSOR, None, DP),
+        P(DP, TENSOR),
+        P(DP, TENSOR),
+        P(DP, TENSOR),
+        P(TENSOR, DP),
+        P(TENSOR, DP),
+        P(TENSOR, DP),
+    )
+    moves_activations = mesh.shape[DP] == 4 * LAYERS and mesh.shape[TENSOR] == 2
     return jax.shard_map(
-        per_device, mesh=mesh, in_specs=in_specs, out_specs=out_specs, check_vma=False
-    )
+        stationary if moves_activations else per_device, mesh=mesh, in_specs=in_specs, out_specs=out_specs, check_vma=False
+    )

time: 5560 us -> 888 us (0.16)
  waiting for transfers between devices: 4930 us -> 21.9 us
  Pallas kernels: 0 us -> 610 us
  matrix products: 239 us -> 33.4 us
  blocking collectives: 132 us -> 0 us
    reduce_scatter x8 -> x0, waiting for transfers between devices: 3690 us -> none  [the longest x1 773 us: per_device(): lax.psum_scatter(grad_half, 'dp', scatter_dimension=2, tiled=True)]
    all_gather x8 -> x0, waiting for transfers between devices: 1090 us -> none  [the longest x1 242 us: per_device(): lax.all_gather(lowered[9], 'dp', axis=1, tiled=True)]
    pallas_call x0 -> x14, Pallas kernels: none -> 610 us  [the longest x5 157 us: reduce(): pl.pallas_call(functools.partial(reduce_kernel, wide, pair, share), out_s...]
    dot_general x101 -> x22, matrix products: 239 us -> 33.4 us  [the longest x4 9.8 us: dot_tn(): lax.dot_general(left, right, (((0,), (0,)), ((), ())), preferred_element_...]
    all_gather x3 -> x0, blocking collectives: 86.6 us -> none  [the longest x1 42.5 us: per_device(): lax.all_gather(lowered[0], 'dp', axis=1, tiled=True)]
    psum x6 -> x0, waiting for transfers between devices: 81.9 us -> none  [the longest x1 19.9 us: per_device(): lax.psum(jnp.dot(hidden_low, down_full, preferred_element_type=jnp.float3...]
    unnamed x26 -> x0, waiting for transfers between devices: 66.5 us -> none
  transfers between devices with their start and end apart: 24 -> 8, of which waited for: 23 -> 3; matrix products, arithmetic and copies ran while one was open for 4% -> 12% of each run, Pallas kernels for 0% -> 52%
where the time goes in v1:
time: 888 us; the launch traced here: 878 us
  Pallas kernels  610 us (69%)
  local copies, waits for them, and re-layouts  83.8 us (9%)
  other arithmetic  75.7 us (9%)
  starting transfers between devices  41.8 us (5%)
  matrix products  33.4 us (4%)
  waiting for transfers between devices  21.9 us (2%)
  between operations  12.1 us (1%)
    pallas_call x5, Pallas kernels, reduce(): pl.pallas_call(functools.partial(reduce_kernel, wide, pair, share), out_s...  157 us
    pallas_call x1, Pallas kernels, res_backward(): pl.pallas_call(functools.partial(res_backward_kernel, breadth), out_shape...  146 us
    pallas_call x1, Pallas kernels, res_forward(): pl.pallas_call(functools.partial(res_forward_kernel, breadth), out_shape=...  143 us
    pallas_call x5, Pallas kernels, gather(): pl.pallas_call(functools.partial(gather_kernel, wide, both), out_shape=ja...  113 us
    all_to_all x8, starting transfers between devices, trade_dp(): return lax.all_to_all(blocks, DP, 0, 0)  41.8 us
    unnamed x281, local copies, waits for them, and re-layouts  41.1 us
    pallas_call x1, Pallas kernels, trade(): pl.pallas_call(functools.partial(trade_kernel, count), out_shape=[jax.Sha...  38.2 us
    sub x10, other arithmetic, clipped_step(): new_master = master - learn_rate * (step_dir + DECAY * master)  29 us
  transfers between devices with their start and end apart: 8, of which 3 were waited for; matrix products, arithmetic and copies ran while one was open for 12% of the time, Pallas kernels for 52%

profile of v1, /device:TPU:0, one launch (start us, length us, event | category | flops | bytes accessed | tf_op | source)
XLA Modules:
  0.0 878.3 jit_solution(6255439455536747062)
XLA Ops:
  0.7 2.7 convert_element_type.152
  3.4 8.5 all-to-all-start.3
  14.3 38.2 %trade.1 = (bf16[16,128,128]{2,1,0:T(8,128)(2,1)S(1)}, f32[16,8,128]{2,1,0:T(8,128)S(1)}) custom-call(bf16[16,128,128]{2,1,0:T(8,128)(2,1)S(1)} %pad_maximum_fusion.1.refs_0_, f32[16,8,128]{2,1,0:T(8,128)S(1)} %broadcast_in_dim.8.refs_1_), custom_call_target="tpu_custom_call" | custom-call | tf_op jit(solution)/shard_map/trade/pallas_call | solution.py:981
  54.6 4.5 all-to-all-start.2
  64.1 26.2 %reduce_16_share.1 = f32[2,56,128]{2,1,0:T(8,128)S(1)} custom-call(f32[16,56,128]{2,1,0:T(8,128)S(1)} %bitcast.247), custom_call_target="tpu_custom_call" | custom-call | tf_op jit(solution)/shard_map/reduce_16_share/pallas_call | solution.py:922
  91.2 26.1 %gather_16_both.4 = bf16[16,2,32,2048]{3,2,1,0:T(8,128)(2,1)S(1)} custom-call(bf16[32,2048]{1,0:T(8,128)(2,1)S(1)} %fusion.48.block_ref), custom_call_target="tpu_custom_call" | custom-call | tf_op jit(solution)/shard_map/gather_16_both/pallas_call | solution.py:712
  119.3 3.0 copy.140
  128.2 2.8 broadcast_in_dim.9
  131.1 5.0 all-to-all-start
  137.7 142.7 %res_forward.1 = (f32[2,64,1024]{2,1,0:T(8,128)S(1)}, bf16[16,256,512]{2,1,0:T(8,128)(2,1)}, bf16[16,288,192]{2,1,0:T(8,128)(2,1)}, bf16[3,16,64,192]{3,2,1,0:T(...) custom-call(bf16[16,256,64]{2,1,0:T(8,128)(2,1)S(1)} %pad_maximum_fusion.pictures, ...), custom_call_target="tpu_custom_call" | custom-call | tf_op jit(solution)/shard_map/res_forward/pallas_call | solution.py:1517
  283.2 21.1 %gather_8_both.2 = bf16[8,2,32,2048]{3,2,1,0:T(8,128)(2,1)S(1)} custom-call(bf16[32,2048]{1,0:T(8,128)(2,1)S(1)} %fusion.52.block_ref), custom_call_target="tpu_custom_call" | custom-call | tf_op jit(solution)/shard_map/gather_8_both/pallas_call | solution.py:712
  307.2 3.0 copy.137
  310.3 3.0 copy.138
  314.8 2.6 copy.125
  317.4 4.4 fusion.91
  323.7 4.1 all-to-all-start.1
  336.8 6.5 all-to-all-done.1
  344.1 25.9 %reduce_8_pair_share.2 = f32[2,32,2048]{2,1,0:T(8,128)S(1)} custom-call(bf16[8,2,32,2048]{3,2,1,0:T(8,128)(2,1)S(1)} %bitcast.235), custom_call_target="tpu_custom_call" | custom-call | tf_op jit(solution)/shard_map/reduce_8_pair_share/pallas_call | solution.py:922
  371.6 25.5 %gather_16_both.3 = bf16[16,2,32,2048]{3,2,1,0:T(8,128)(2,1)S(1)} custom-call(bf16[32,2048]{1,0:T(8,128)(2,1)S(1)} %fusion.50.block_ref), custom_call_target="tpu_custom_call" | custom-call | tf_op jit(solution)/shard_map/gather_16_both/pallas_call | solution.py:712
  400.6 36.4 %reduce_16_pair_share.2 = f32[2,32,2048]{2,1,0:T(8,128)S(1)} custom-call(bf16[16,2,32,2048]{3,2,1,0:T(8,128)(2,1)S(1)} %bitcast.228), custom_call_target="tpu_custom_call" | custom-call | tf_op jit(solution)/shard_map/reduce_16_pair_share/pallas_call | solution.py:922
  438.3 36.9 %reduce_16_pair_share.3 = f32[2,32,2048]{2,1,0:T(8,128)S(1)} custom-call(bf16[16,2,32,2048]{3,2,1,0:T(8,128)(2,1)S(1)} %bitcast.229), custom_call_target="tpu_custom_call" | custom-call | tf_op jit(solution)/shard_map/reduce_16_pair_share/pallas_call | solution.py:922
  478.9 19.5 %gather_8_both.3 = bf16[8,2,32,2048]{3,2,1,0:T(8,128)(2,1)S(1)} custom-call(bf16[32,2048]{1,0:T(8,128)(2,1)S(1)} %fusion.47.block_ref), custom_call_target="tpu_custom_call" | custom-call | tf_op jit(solution)/shard_map/gather_8_both/pallas_call | solution.py:712
  499.9 5.2 all-to-all-start.5
  508.4 4.5 convolution_convert_fusion.6
  512.9 7.7 all-to-all-done.5
  520.6 4.3 all-to-all-start.6
  529.6 31.7 %reduce_8_pair_share.3 = f32[2,32,2048]{2,1,0:T(8,128)S(1)} custom-call(bf16[8,2,32,2048]{3,2,1,0:T(8,128)(2,1)S(1)} %bitcast.244), custom_call_target="tpu_custom_call" | custom-call | tf_op jit(solution)/shard_map/reduce_8_pair_share/pallas_call | solution.py:922
  565.4 5.2 all-to-all-start.7
  577.7 146.1 %res_backward.1 = (bf16[16,128,128]{2,1,0:T(8,128)(2,1)S(1)}, f32[2,64]{1,0:T(2,128)S(1)}, f32[2,512]{1,0:T(2,128)S(1)}, f32[3,192,512]{2,1,0:T(8,128)S(1)}, f32...) custom-call(bf16[64,1024]{1,0:T(8,128)(2,1)S(1)} %fusion.43.shrunk, bf16[16,256,64]{2,1,0:T(8,128)(2,1)S(1)} %copy-done.2, ...), custom_call_target="tpu_custom_call" | custom-call | tf_op jit(solution)/shard_map/res_backward/pallas_call | solution.py:1792
  725.1 2.5 copy.129
  727.8 2.8 reshape.753
  731.1 21.1 %gather_16_both.5 = f32[16,2,56,128]{3,2,1,0:T(8,128)S(1)} custom-call(f32[56,128]{1,0:T(8,128)S(1)} %maximum_bitcast_fusion.1.block_ref), custom_call_target="tpu_custom_call" | custom-call | tf_op jit(solution)/shard_map/gather_16_both/pallas_call | solution.py:712
  755.7 3.5 convolution_convert_fusion.4
  759.1 3.9 reshape.760
  765.2 5.0 all-to-all-start.4
  771.5 2.6 copy.173
  775.3 3.1 multiply_reduce_fusion.4
  784.6 2.9 multiply_reduce_fusion
  796.8 7.7 all-to-all-done.4
  811.6 12.5 %total.1 = f32[8,128]{1,0:T(8,128)S(1)} custom-call(f32[8,128]{1,0:T(8,128)S(1)} %broadcast_in_dim.11.in_ref), custom_call_target="tpu_custom_call" | custom-call | tf_op jit(solution)/shard_map/total/pallas_call | solution.py:1095
  830.3 5.7 multiply_subtract_fusion.3
  836.1 3.1 copy.146
  842.6 2.6 multiply_subtract_fusion.7
  851.5 2.4 multiply_subtract_fusion.5
  855.3 2.5 multiply_subtract_fusion.4
  859.8 4.4 multiply_subtract_fusion
  867.2 4.0 multiply_subtract_fusion.2
  873.1 3.9 multiply_subtract_fusion.1
  (408 shorter events, 116.9 us)
Async XLA Ops:
  0.7 11.3 %copy-start.57 = (f32[16,6,2048]{2,0,1:T(8,128)S(1)}, f32[16,6,2048]{2,0,1:T(8,128)}, u32[]{:S(2)}) copy-start(f32[16,6,2048]{2,0,1:T(8,128)} %param.51) | copy-start | bytes 2359300
  3.4 8.6 copy-start.92
  3.4 51.1 %all-to-all-start.3 = ((bf16[16,256,128]{2,1,0:T(8,128)(2,1)}), bf16[16,256,128]{2,1,0:T(8,128)(2,1)}, u32[]{:S(2)}, u32[]{:S(2)}) async-start(bf16[16,256,128]{2,1,0:T(8,128)(2,1)} %bitcast.35), calls=%async_computation.3 | async-start | bytes 2097152 | tf_op jit(solution)/shard_map/all_to_all | solution.py:1848
  13.8 38.7 %copy-start.93 = (f32[16,2,512]{2,1,0:T(2,128)S(1)}, f32[16,2,512]{2,1,0:T(2,128)}, u32[]{:S(2)}) copy-start(f32[16,2,512]{2,1,0:T(2,128)} %param.42) | copy-start | bytes 196612
  13.9 38.8 %copy-start.27 = (f32[128,4096]{1,0:T(8,128)S(1)}, f32[128,4096]{1,0:T(8,128)}, u32[]{:S(2)}) copy-start(f32[128,4096]{1,0:T(8,128)} %param.60) | copy-start | bytes 6291460
  54.6 73.7 %all-to-all-start.2 = ((bf16[16,128,256]{1,2,0:T(8,128)(2,1)}), bf16[16,128,256]{1,2,0:T(8,128)(2,1)}, u32[]{:S(2)}, u32[]{:S(2)}) async-start(bf16[16,128,256]{1,2,0:T(8,128)(2,1)} %bitcast.257), calls=%async_computation.2 | async-start | bytes 2097152 | tf_op jit(solution)/shard_map/all_to_all | solution.py:1848
  60.0 77.7 %copy-start.5 = (bf16[3,3,64,512]{3,2,1,0:T(8,128)(2,1)}, bf16[3,3,64,512]{3,2,1,0:T(8,128)(2,1)S(1)}, u32[]{:S(2)}) copy-start(bf16[3,3,64,512]{3,2,1,0:T(8,128)(2,1)S(1)} %convert_element_type.135) | copy-start | bytes 1769476
  61.8 75.8 %copy-start.3 = (bf16[3,512,192]{2,1,0:T(8,128)(2,1)}, bf16[3,512,192]{2,1,0:T(8,128)(2,1)S(1)}, u32[]{:S(2)}) copy-start(bf16[3,512,192]{2,1,0:T(8,128)(2,1)S(1)} %copy.116.conv_two) | copy-start | bytes 1769476
  61.8 29.3 %copy-start.60 = (bf16[1,64,2048]{2,1,0:T(8,128)(2,1)S(1)}, bf16[1,64,2048]{2,1,0:T(8,128)(2,1)}, u32[]{:S(2)}) copy-start(bf16[1,64,2048]{2,1,0:T(8,128)(2,1)} %param.35) | copy-start | bytes 786436
  64.0 73.6 %copy-start = (bf16[3,3,64,1024]{3,2,1,0:T(8,128)(2,1)}, bf16[3,3,64,1024]{3,2,1,0:T(8,128)(2,1)S(1)}, u32[]{:S(2)}) copy-start(bf16[3,3,64,1024]{3,2,1,0:T(8,128)(2,1)S(1)} %convert_element_type.137) | copy-start | bytes 3538948
  91.1 26.1 %copy-start.101 = (f32[1,2048]{1,0:T(1,128)}, f32[1,2048]{1,0:T(1,128)S(1)}, u32[]{:S(2)}) copy-start(f32[1,2048]{1,0:T(1,128)S(1)} %get-tuple-element.151) | copy-start | bytes 24580
  131.1 190.8 %all-to-all-start = ((bf16[16,128,3,128]{1,3,2,0:T(8,128)(2,1)}), bf16[16,128,3,128]{1,3,2,0:T(8,128)(2,1)}, u32[]{:S(2)}, u32[]{:S(2)}) async-start(bf16[16,128,3,128]{1,3,2,0:T(8,128)(2,1)} %bitcast.252), calls=%async_computation | async-start | bytes 3145728 | tf_op jit(solution)/shard_map/all_to_all | solution.py:1848
  137.5 143.9 %copy-start.1 = (bf16[16,256,64]{2,1,0:T(8,128)(2,1)}, bf16[16,256,64]{2,1,0:T(8,128)(2,1)S(1)}, u32[]{:S(2)}) copy-start(bf16[16,256,64]{2,1,0:T(8,128)(2,1)S(1)} %pad_maximum_fusion.pictures) | copy-start | bytes 1572868
  282.3 23.4 %copy-start.122 = (f32[64]{0:T(128)}, f32[64]{0:T(128)S(1)}, u32[]{:S(2)}) copy-start(f32[64]{0:T(128)S(1)} %add_rsqrt_fusion.1) | copy-start | bytes 772
  283.1 27.2 %copy-start.70 = (f32[64,2048]{1,0:T(8,128)}, f32[64,2048]{1,0:T(8,128)S(1)}, u32[]{:S(2)}) copy-start(f32[64,2048]{1,0:T(8,128)S(1)} %subtract_multiply_fusion.2) | copy-start | bytes 1572868
  304.3 26.0 %copy-start.16 = (bf16[8,2,32,2048]{3,2,1,0:T(8,128)(2,1)}, bf16[8,2,32,2048]{3,2,1,0:T(8,128)(2,1)S(1)}, u32[]{:S(2)}) copy-start(bf16[8,2,32,2048]{3,2,1,0:T(8,128)(2,1)S(1)} %gather_8_both.2) | copy-start | bytes 6291460
  323.7 19.6 %all-to-all-start.1 = ((bf16[16,128,128]{1,2,0:T(8,128)(2,1)}), bf16[16,128,128]{1,2,0:T(8,128)(2,1)S(1)}, u32[]{:S(2)}, u32[]{:S(2)}) async-start(bf16[16,128,128]{1,2,0:T(8,128)(2,1)} %bitcast.20), calls=%async_computation.1 | async-start | bytes 1048576 | tf_op jit(solution)/shard_map/all_to_all | solution.py:1848
  343.3 26.7 %copy-start.43 = (bf16[16,128,128]{1,2,0:T(8,128)(2,1)}, bf16[16,128,128]{1,2,0:T(8,128)(2,1)S(1)}, u32[]{:S(2)}) copy-start(bf16[16,128,128]{1,2,0:T(8,128)(2,1)S(1)} %all-to-all-done.1) | copy-start | bytes 1572868
  343.3 26.7 %copy-start.49 = (f32[1,64,1024]{2,1,0:T(8,128)S(1)}, f32[1,64,1024]{2,1,0:T(8,128)}, u32[]{:S(2)}) copy-start(f32[1,64,1024]{2,1,0:T(8,128)} %get-tuple-element.145) | copy-start | bytes 786436
  343.3 26.7 %copy-start.51 = (f32[1,64,1024]{2,1,0:T(8,128)S(1)}, f32[1,64,1024]{2,1,0:T(8,128)}, u32[]{:S(2)}) copy-start(f32[1,64,1024]{2,1,0:T(8,128)} %get-tuple-element.146) | copy-start | bytes 786436
  344.0 26.5 %copy-start.48 = (f32[64,1024]{1,0:T(8,128)S(1)}, f32[64,1024]{1,0:T(8,128)}, u32[]{:S(2)}) copy-start(f32[64,1024]{1,0:T(8,128)} %copy-done.47) | copy-start | bytes 786436
  370.2 105.0 %copy-start.30 = (f32[2,32,2048]{2,1,0:T(8,128)}, f32[2,32,2048]{2,1,0:T(8,128)S(1)}, u32[]{:S(2)}) copy-start(f32[2,32,2048]{2,1,0:T(8,128)S(1)} %get-tuple-element.135) | copy-start | bytes 1572868
  371.6 25.5 %copy-start.44 = (bf16[16,128,256]{2,1,0:T(8,128)(2,1)S(1)}, bf16[16,128,256]{2,1,0:T(8,128)(2,1)}, u32[]{:S(2)}) copy-start(bf16[16,128,256]{2,1,0:T(8,128)(2,1)} %copy.125) | copy-start | bytes 3145732
  371.6 25.5 %copy-start.129 = (f32[1024,256]{1,0:T(8,128)S(1)}, f32[1024,256]{1,0:T(8,128)}, u32[]{:S(2)}) copy-start(f32[1024,256]{1,0:T(8,128)} %fusion.91) | copy-start | bytes 3145732
  399.2 37.8 %copy-start.74 = (bf16[1024,256]{1,0:T(8,128)(2,1)}, bf16[1024,256]{1,0:T(8,128)(2,1)S(1)}, u32[]{:S(2)}) copy-start(bf16[1024,256]{1,0:T(8,128)(2,1)S(1)} %get-tuple-element.159) | copy-start | bytes 1572868
  437.0 40.3 %copy-start.7 = (f32[2,32,2048]{2,1,0:T(8,128)}, f32[2,32,2048]{2,1,0:T(8,128)S(1)}, u32[]{:S(2)}) copy-start(f32[2,32,2048]{2,1,0:T(8,128)S(1)} %reduce_16_pair_share.2) | copy-start | bytes 1572868
  438.3 36.9 %copy-start.114 = (f32[2,32]{1,0:T(2,128)S(1)}, f32[2,32]{1,0:T(2,128)}, u32[]{:S(2)}) copy-start(f32[2,32]{1,0:T(2,128)} %copy-done.113) | copy-start | bytes 772
  438.3 39.0 %copy-start.54 = (f32[64,2048]{1,0:T(8,128)S(1)}, f32[64,2048]{1,0:T(8,128)}, u32[]{:S(2)}) copy-start(f32[64,2048]{1,0:T(8,128)} %copy-done.53) | copy-start | bytes 1572868
  438.3 39.0 %copy-start.61 = (bf16[1,64,2048]{2,1,0:T(8,128)(2,1)S(1)}, bf16[1,64,2048]{2,1,0:T(8,128)(2,1)}, u32[]{:S(2)}) copy-start(bf16[1,64,2048]{2,1,0:T(8,128)(2,1)} %param.35) | copy-start | bytes 786436
  438.3 38.9 %copy-start.124 = (f32[64]{0:T(128)S(1)}, f32[64]{0:T(128)}, u32[]{:S(2)}) copy-start(f32[64]{0:T(128)} %copy-done.123) | copy-start | bytes 772
  477.3 21.2 %copy-start.85 = (bf16[8,64,128]{2,1,0:T(8,128)(2,1)S(1)}, bf16[8,64,128]{2,1,0:T(8,128)(2,1)}, u32[]{:S(2)}) copy-start(bf16[8,64,128]{2,1,0:T(8,128)(2,1)} %copy-done.84) | copy-start | bytes 393220
  499.9 20.7 %all-to-all-start.5 = ((bf16[16,128,128]{2,1,0:T(8,128)(2,1)}), bf16[16,128,128]{2,1,0:T(8,128)(2,1)}, u32[]{:S(2)}, u32[]{:S(2)}) async-start(bf16[16,128,128]{2,1,0:T(8,128)(2,1)} %bitcast.272), calls=%async_computation.5 | async-start | bytes 1048576 | tf_op jit(solution)/shard_map/all_to_all | solution.py:1848
  512.9 15.2 %copy-start.83 = (bf16[512,128]{1,0:T(8,128)(2,1)S(1)}, bf16[512,128]{1,0:T(8,128)(2,1)}, u32[]{:S(2)}) copy-start(bf16[512,128]{1,0:T(8,128)(2,1)} %copy-done.82) | copy-start | bytes 393220
  512.9 15.4 %copy-start.77 = (bf16[16,128,3,128]{1,0,3,2:T(8,128)(2,1)S(1)}, bf16[16,128,3,128]{1,0,3,2:T(8,128)(2,1)}, u32[]{:S(2)}) copy-start(bf16[16,128,3,128]{1,0,3,2:T(8,128)(2,1)} %copy-done.76) | copy-start | bytes 4718596
  520.6 44.9 %all-to-all-start.6 = ((bf16[16,128,256]{2,1,0:T(8,128)(2,1)}), bf16[16,128,256]{2,1,0:T(8,128)(2,1)}, u32[]{:S(2)}, u32[]{:S(2)}) async-start(bf16[16,128,256]{2,1,0:T(8,128)(2,1)} %bitcast.280), calls=%async_computation.6 | async-start | bytes 2097152 | tf_op jit(solution)/shard_map/all_to_all | solution.py:1848
  528.3 33.1 %copy-start.14 = (bf16[16,2,32,2048]{3,2,1,0:T(8,128)(2,1)S(1)}, bf16[16,2,32,2048]{3,2,1,0:T(8,128)(2,1)}, u32[]{:S(2)}) copy-start(bf16[16,2,32,2048]{3,2,1,0:T(8,128)(2,1)} %copy-done.13) | copy-start | bytes 12582916
  529.6 31.8 %copy-start.56 = (f32[1024,256]{1,0:T(8,128)S(1)}, f32[1024,256]{1,0:T(8,128)}, u32[]{:S(2)}) copy-start(f32[1024,256]{1,0:T(8,128)} %copy-done.55) | copy-start | bytes 3145732
  564.0 10.3 %copy-start.112 = (f32[1024]{0:T(1024)S(1)}, f32[1024]{0:T(1024)}, u32[]{:S(2)}) copy-start(f32[1024]{0:T(1024)} %dynamic-slice.1) | copy-start | bytes 12292
  564.0 11.5 %copy-start.2 = (bf16[16,256,64]{2,1,0:T(8,128)(2,1)S(1)}, bf16[16,256,64]{2,1,0:T(8,128)(2,1)}, u32[]{:S(2)}) copy-start(bf16[16,256,64]{2,1,0:T(8,128)(2,1)} %copy-done.1) | copy-start | bytes 1572868
  564.0 11.5 %copy-start.4 = (bf16[3,512,192]{2,1,0:T(8,128)(2,1)S(1)}, bf16[3,512,192]{2,1,0:T(8,128)(2,1)}, u32[]{:S(2)}) copy-start(bf16[3,512,192]{2,1,0:T(8,128)(2,1)} %copy-done.3) | copy-start | bytes 1769476
  565.4 199.8 %all-to-all-start.7 = ((bf16[16,256,128]{2,1,0:T(8,128)(2,1)}), bf16[16,256,128]{2,1,0:T(8,128)(2,1)}, u32[]{:S(2)}, u32[]{:S(2)}) async-start(bf16[16,256,128]{2,1,0:T(8,128)(2,1)} %bitcast.262), calls=%async_computation.7 | async-start | bytes 2097152 | tf_op jit(solution)/shard_map/all_to_all | solution.py:1848
  731.1 24.6 %copy-start.17 = (bf16[8,2,32,2048]{3,2,1,0:T(8,128)(2,1)S(1)}, bf16[8,2,32,2048]{3,2,1,0:T(8,128)(2,1)}, u32[]{:S(2)}) copy-start(bf16[8,2,32,2048]{3,2,1,0:T(8,128)(2,1)} %copy-done.16) | copy-start | bytes 6291460
  765.2 39.2 %all-to-all-start.4 = ((bf16[16,128,3,128]{1,3,2,0:T(8,128)(2,1)}), bf16[16,128,3,128]{1,3,2,0:T(8,128)(2,1)}, u32[]{:S(2)}, u32[]{:S(2)}) async-start(bf16[16,128,3,128]{1,3,2,0:T(8,128)(2,1)} %copy.132), calls=%async_computation.4 | async-start | bytes 3145728 | tf_op jit(solution)/shard_map/all_to_all | solution.py:1848
  770.6 8.5 copy-start.12
  771.5 11.5 %copy-start.10 = (f32[3,192,512]{2,1,0:T(8,128)S(1)}, f32[3,192,512]{2,1,0:T(8,128)}, u32[]{:S(2)}) copy-start(f32[3,192,512]{2,1,0:T(8,128)} %copy-done.9) | copy-start | bytes 3538948
  780.0 8.1 copy-start.8
  780.0 8.1 copy-start.102
  791.1 15.3 %copy-start.41 = (f32[8,128,128]{2,1,0:T(8,128)}, f32[8,128,128]{2,1,0:T(8,128)S(1)}, u32[]{:S(2)}) copy-start(f32[8,128,128]{2,1,0:T(8,128)S(1)} %convert_reduce_fusion.1) | copy-start | bytes 1572868
  (90 other events, 233.5 us)

commit v2 on v1

--- a/solution.py
+++ b/solution.py
@@ -529,7 +529,7 @@
 IN_VMEM = pl.BlockSpec(memory_space=pltpu.VMEM)
 LAYERS = 4
 ORDER = (3, 0, 2, 1)
-VMEM_GRANT = 48 * 1024 * 1024
+VMEM_GRANT = 60 * 1024 * 1024
 
 
 class Place:
@@ -542,6 +542,7 @@
         y = (self.dp // 2) % 2
         x_mate = self.dp + 1 - 2 * x
         y_mate = self.dp + 2 - 4 * y
+        self.x_mate = x_mate
         if wide:
             self.first = x_mate * (1 - self.core) + y_mate * self.core
             self.second = y_mate * (1 - self.core) + x_mate * self.core
@@ -1132,73 +1133,141 @@
     return (1 - flip) * base + flip * (LAYERS - 1 - base)
 
 
-def gather_stage(at, out, use, send_sem, recv_sem):
-    everyone = 4 * LAYERS
-
-    def send(slot, sem, mate):
-        return remote(
-            out.at[slot], out.at[slot], send_sem.at[sem], recv_sem.at[slot], (mate, at.core)
-        )
-
-    @pl.loop(0, everyone)
-    def _(step):
-        late = step // 8
-        rest = step % 8
-        last = rest // 7
-        even = 1 - rest % 2
-        is_first = (1 - late) * (last + even * ((rest + 6) // 8))
-        is_own = (1 - late) * (1 - is_first)
-        near = is_own * ((rest + 1) // 2) + is_first * ((rest - 1) // 2)
-        layer = by_distance(at, (1 - late) * near + late * (rest // 2))
-        column = (
-            is_own * at.column
-            + is_first * at.first_column
-            + late * ((1 - rest % 2) * at.second_column + rest % 2 * at.far_column)
-        )
-        slot = layer * 4 + column
+def piece_of(block, index, pieces):
+    rows, lanes = block.shape
+    if rows >= 16 * pieces:
+        return block.at[pl.ds(pl.multiple_of(index * (rows // pieces), rows // pieces), rows // pieces)]
+    return block.at[:, pl.ds(pl.multiple_of(index * (lanes // pieces), lanes // pieces), lanes // pieces)]
+
+
+def gather_stage(at, outs, use, pieces, send_sem, recv_sem, mirror=None):
+    columns = at.stride
+    arrays = range(len(outs))
+
+    def here(index, slot, piece):
+        block = outs[index].at[slot, at.core] if mirror else outs[index].at[slot]
+        return piece_of(block, piece, pieces)
+
+    def each(slot, piece, sem, mate, act):
+        for index in arrays:
+            act(
+                remote(
+                    here(index, slot, piece),
+                    here(index, slot, piece),
+                    send_sem.at[index, sem * pieces + piece],
+                    recv_sem.at[index, slot * pieces + piece],
+                    (mate, at.core),
+                )
+            )
+
+    def start(copy):
+        copy.start()
+
+    def across(slot, piece, act, core):
+        for index in arrays:
+            block = piece_of(outs[index].at[slot, core], piece, pieces)
+            act(
+                remote(
+                    block,
+                    block,
+                    mirror[0].at[index, slot * pieces + piece],
+                    mirror[1].at[index, slot * pieces + piece],
+                    (at.dp, 1 - at.core),
+                )
+            )
+
+    @pl.loop(0, columns * LAYERS * pieces)
+    def _(count):
+        step, piece = (count // pieces, count % pieces)
+        if at.wide:
+            late = step // 8
+            rest = step % 8
+            last = rest // 7
+            is_first = (1 - late) * (last + (1 - rest % 2) * ((rest + 6) // 8))
+            is_own = (1 - late) * (1 - is_first)
+            near = is_own * ((rest + 1) // 2) + is_first * ((rest - 1) // 2)
+            layer = by_distance(at, (1 - late) * near + late * (rest // 2))
+            column = (
+                is_own * at.column
+                + is_first * at.first_column
+                + late * ((1 - rest % 2) * at.second_column + rest % 2 * at.far_column)
+            )
+        else:
+            is_own = 1 - step // LAYERS
+            layer = by_distance(at, step % LAYERS)
+            column = is_own * at.column + (1 - is_own) * at.second_column
+        slot = layer * columns + column
 
         @pl.when(slot != at.slot)
         def _():
-            send(slot, 0, at.dp).wait_recv()
+            each(slot, piece, 0, at.dp, lambda copy: copy.wait_recv())
 
         @pl.when(is_own == 1)
         def _():
             @pl.when(jnp.logical_and(layer <= at.z, at.has_above))
             def _():
-                send(slot, layer, at.dp + 4).start()
+                each(slot, piece, layer, at.dp + 4, start)
 
             @pl.when(jnp.logical_and(layer >= at.z, at.has_below))
             def _():
-                send(slot, 4 + layer, at.dp - 4).start()
-
-            send(slot, 8 + layer, at.first).start()
-            send(slot, 12 + layer, at.second).start()
-
-        @pl.when(is_first == 1)
-        def _():
-            send(slot, 16 + layer, at.second).start()
-
-        use(slot)
-
-    @pl.loop(0, LAYERS)
-    def _(layer):
+                each(slot, piece, 4 + layer, at.dp - 4, start)
+
+            if at.wide:
+                each(slot, piece, 8 + layer, at.first, start)
+            each(slot, piece, 12 + layer, at.second, start)
+
+        if at.wide:
+
+            @pl.when(is_first == 1)
+            def _():
+                each(slot, piece, 16 + layer, at.second, start)
+
+        if mirror:
+            across(slot, piece, start, at.core)
+        if use is not None:
+            pl.when(piece == pieces - 1)(lambda: use(slot))
+
+    def sent(copy):
+        copy.wait_send()
+
+    @pl.loop(0, LAYERS * pieces)
+    def _(count):
+        layer, piece = (count // pieces, count % pieces)
+
         @pl.when(jnp.logical_and(layer <= at.z, at.has_above))
         def _():
-            send(at.slot, layer, at.dp + 4).wait_send()
+            each(at.slot, piece, layer, at.dp + 4, sent)
 
         @pl.when(jnp.logical_and(layer >= at.z, at.has_below))
         def _():
-            send(at.slot, 4 + layer, at.dp - 4).wait_send()
-
-        for group in (8, 12, 16):
-            send(at.slot, group + layer, at.first).wait_send()
-
-
-def reduce_stage(at, blocks, produce, pieces, result, from_second, from_first, from_z, send_sem, recv_sem, meanwhile=None):
-    rows = blocks.shape[1] // pieces
+            each(at.slot, piece, 4 + layer, at.dp - 4, sent)
+
+        for group in (8, 12, 16) if at.wide else (12,):
+            each(at.slot, piece, group + layer, at.second, sent)
+
+    if mirror:
+
+        @pl.loop(0, columns * LAYERS * pieces)
+        def _(count):
+            slot, piece = (count // pieces, count % pieces)
+            across(slot, piece, lambda copy: copy.wait_recv(), 1 - at.core)
+            across(slot, piece, sent, at.core)
+
+
+def gather_scratch(pieces, arrays=1, wide=True, mirror=False):
+    chips = 16 if wide else 8
+    count = [20 * pieces, 16 * pieces] + [chips * pieces] * (2 * mirror)
+    return [pltpu.SemaphoreType.DMA((arrays, n)) for n in count]
+
+
+def reduce_stage(at, result, produce, pieces, scratch, pair=False, meanwhile=None):
+    blocks, from_second, from_first, from_z, send_sem, recv_sem, *scratch = scratch
+    columns = at.stride
+    whole = columns * LAYERS
+    lag = whole // 2 if pair else 0
 
     def part(ref, index, piece):
-        return ref.at[index, pl.ds(piece * rows, rows)]
+        return piece_of(ref.at[index], piece, pieces)
 
     def copy(sem, piece, source, target, mate):
         return remote(
@@ -1214,62 +1283,99 @@
 
     def to_first(layer, piece):
         return copy(
-            8 + layer, piece, layer * 4 + at.first_column, (from_first, layer), at.first
+            8 + layer, piece, layer * columns + at.first_column, (from_first, layer), at.first
         )
 
     def up(layer, piece):
-        return copy(12 + layer, piece, layer * 4 + at.column, (from_z, layer), at.dp + 4)
+        return copy(12 + layer, piece, layer * columns + at.column, (from_z, layer), at.dp + 4)
 
     def down(layer, piece):
-        return copy(16 + layer, piece, layer * 4 + at.column, (from_z, 4 + layer), at.dp - 4)
+        return copy(16 + layer, piece, layer * columns + at.column, (from_z, 4 + layer), at.dp - 4)
 
     def value(ref, index, piece):
         return part(ref, index, piece)[...].astype(jnp.float32)
 
-    @pl.loop(0, 4 * LAYERS)
+    def slot_of(step):
+        if at.wide:
+            keep, second, place = (step // 8, step % 2, step % 8 // 2)
+            column = (1 - second) * (
+                (1 - keep) * at.far_column + keep * at.first_column
+            ) + second * ((1 - keep) * at.second_column + keep * at.column)
+        else:
+            keep, second, place = (step // LAYERS, 1, step % LAYERS)
+            column = (1 - keep) * at.second_column + keep * at.column
+        return layer_order(place) * columns + column, keep, second, place
+
+    ahead = 2
+
+    def send_layer(place, piece):
+        layer = layer_order(place)
+        if at.wide:
+            to_second(0, layer, piece, layer * columns + at.far_column).start()
+        to_second(1, layer, piece, layer * columns + at.second_column).start()
+
+    def to_mate(slot):
+        outbound, paired, pair_send, pair_recv = scratch
+        return remote(
+            outbound.at[slot],
+            paired.at[slot],
+            pair_send.at[slot],
+            pair_recv.at[slot],
+            (at.dp, 1 - at.core),
+        )
+
+    @pl.loop(0, whole + lag)
     def _(step):
-        kind = step // LAYERS
-        keep, second = (kind // 2, kind % 2)
-        column = (1 - second) * ((1 - keep) * at.far_column + keep * at.first_column) + second * (
-            (1 - keep) * at.second_column + keep * at.column
-        )
-        layer = layer_order(step % LAYERS)
-        slot = layer * 4 + column
-        produce(slot)
-
-        @pl.when(keep == 0)
-        def _():
-            for piece in range(pieces):
-                to_second(second, layer, piece, slot).start()
+        def make():
+            slot = slot_of(step)[0]
+            produce(slot)
+            if pair:
+                to_mate(slot).start()
+
+        def pass_on():
+            slot, keep, second, place = slot_of(step - lag)
+            if pair:
+                to_mate(slot).wait_recv()
+                blocks[slot] = (
+                    blocks[slot].astype(jnp.float32) + scratch[1][slot].astype(jnp.float32)
+                ).astype(blocks.dtype)
+
+            @pl.when(jnp.logical_and(keep == 0, place < ahead))
+            def _():
+                for piece in range(pieces):
+                    to_second(second, layer_order(place), piece, slot).start()
+
+        if pair:
+            pl.when(step < whole)(make)
+            pl.when(step >= lag)(pass_on)
+        else:
+            make()
+            pass_on()
 
     if meanwhile is not None:
         meanwhile()
 
-    @pl.loop(0, LAYERS * pieces)
-    def _(step):
-        layer, piece = (layer_order(step // pieces), step % pieces)
-        slot = layer * 4 + at.first_column
+    def turn(place, piece):
+        layer = layer_order(place)
+        slot = layer * columns + at.first_column
         to_second(0, layer, piece, slot).wait_recv()
         part(blocks, slot, piece)[...] = (
             value(blocks, slot, piece) + value(from_second, layer, piece)
         ).astype(blocks.dtype)
         to_first(layer, piece).start()
 
-    @pl.loop(0, LAYERS * pieces)
-    def _(step):
-        layer, piece = (layer_order(step // pieces), step % pieces)
-        slot = layer * 4 + at.column
+    def rise(place, piece):
+        layer = layer_order(place)
+        slot = layer * columns + at.column
         to_second(1, layer, piece, slot).wait_recv()
-        to_first(layer, piece).wait_recv()
-        summed = (
-            value(blocks, slot, piece)
-            + value(from_second, 4 + layer, piece)
-            + value(from_first, layer, piece)
-        )
+        summed = value(blocks, slot, piece) + value(from_second, 4 + layer, piece)
+        if at.wide:
+            to_first(layer, piece).wait_recv()
+            summed = summed + value(from_first, layer, piece)
 
         @pl.when(at.z == layer)
         def _():
-            result[pl.ds(piece * rows, rows)] = summed
+            piece_of(result, piece, pieces)[...] = summed
 
         @pl.when(at.z < layer)
         def _():
@@ -1297,42 +1403,207 @@
 
             down(layer, piece).start()
 
+    behind = 1 if at.wide else 0
+
+    @pl.loop(0, (LAYERS + behind) * pieces)
+    def _(step):
+        place, piece = (step // pieces, step % pieces)
+        pl.when(place + ahead < LAYERS)(lambda: send_layer(place + ahead, piece))
+        if at.wide:
+            pl.when(place < LAYERS)(lambda: turn(place, piece))
+        pl.when(place >= behind)(lambda: rise(place - behind, piece))
+
     @pl.loop(0, pieces)
     def _(piece):
         @pl.when(at.has_below)
         def _():
             up(at.z, piece).wait_recv()
-            result[pl.ds(piece * rows, rows)] += value(from_z, at.z, piece)
+            piece_of(result, piece, pieces)[...] += value(from_z, at.z, piece)
 
         @pl.when(at.has_above)
         def _():
             down(at.z, piece).wait_recv()
-            result[pl.ds(piece * rows, rows)] += value(from_z, 4 + at.z, piece)
+            piece_of(result, piece, pieces)[...] += value(from_z, 4 + at.z, piece)
 
     @pl.loop(0, LAYERS * pieces)
     def _(step):
         layer, piece = (step // pieces, step % pieces)
-        to_second(0, layer, piece, at.slot).wait_send()
+        if at.wide:
+            to_second(0, layer, piece, at.slot).wait_send()
+            to_first(layer, piece).wait_send()
         to_second(1, layer, piece, at.slot).wait_send()
-        to_first(layer, piece).wait_send()
         pl.when(at.z < layer)(lambda: up(layer, piece).wait_send())
         pl.when(at.z > layer)(lambda: down(layer, piece).wait_send())
 
-
-def reduce_scratch(block, pieces):
+    if pair:
+
+        @pl.loop(0, whole)
+        def _(slot):
+            to_mate(slot).wait_send()
+
+
+def share_stage(at, result, send_sem, recv_sem):
+    def give(core):
+        return remote(result.at[core], result.at[core], send_sem, recv_sem, (at.dp, 1 - at.core))
+
+    give(at.core).start()
+    give(1 - at.core).wait_recv()
+    give(at.core).wait_send()
+
+
+def greet_all(at):
+    everyone = 4 * LAYERS
+    barrier = pltpu.get_barrier_semaphore()
+
+    @pl.loop(1, everyone)
+    def _(step):
+        pl.semaphore_signal(
+            barrier, inc=1, device_id=((at.dp + step) % everyone, at.core), device_id_type=MESH
+        )
+
+    pl.semaphore_signal(barrier, inc=1, device_id=(at.dp, 1 - at.core), device_id_type=MESH)
+    pl.semaphore_wait(barrier, everyone)
+
+
+class Ride:
+    def __init__(self, at, parts, send_sem, recv_sem, own_sem):
+        self.at, self.parts = (at, parts)
+        self.send_sem, self.recv_sem, self.own_sem = (send_sem, recv_sem, own_sem)
+
+    def copy(self, part, step):
+        source, target = self.parts[part]
+        peer = (self.at.dp + step) % (4 * LAYERS)
+        return remote(
+            source(peer),
+            target(self.at.dp),
+            self.send_sem.at[part, step - 1],
+            self.recv_sem.at[part, step - 1],
+            (peer, self.at.core),
+        )
+
+    def keep(self, part):
+        source, target = self.parts[part]
+        return pltpu.make_async_copy(
+            source(self.at.dp), target(self.at.dp), self.own_sem.at[part]
+        )
+
+    def start(self, first=0, after=None):
+        for part in range(len(self.parts))[first:after]:
+            self.keep(part).start()
+
+            @pl.loop(1, 4 * LAYERS)
+            def _(step):
+                self.copy(part, step).start()
+
+    def wait_for(self, part):
+        self.keep(part).wait()
+
+        @pl.loop(1, 4 * LAYERS)
+        def _(step):
+            self.copy(part, step).wait()
+
+    def wait(self, first=0):
+        for part in range(first, len(self.parts)):
+            self.wait_for(part)
+
+
+def ride_scratch(parts):
+    others = 4 * LAYERS - 1
+    return [
+        pltpu.SemaphoreType.DMA((parts, others)),
+        pltpu.SemaphoreType.DMA((parts, others)),
+        pltpu.SemaphoreType.DMA((parts,)),
+    ]
+
+
+class PairRide:
+    def __init__(self, at, parts, send_sem, recv_sem, own_sem):
+        self.at, self.parts = (at, parts)
+        self.send_sem, self.recv_sem, self.own_sem = (send_sem, recv_sem, own_sem)
+        self.steps = 2 * LAYERS
+
+    def copy(self, part, step):
+        source, target = self.parts[part]
+        peer = (self.at.dp + 2 * step) % (4 * LAYERS)
+        return remote(
+            source(peer),
+            target(self.at.dp),
+            self.send_sem.at[part, step],
+            self.recv_sem.at[part, step],
+            (peer, self.at.core),
+        )
+
+    def keep(self, part):
+        source, target = self.parts[part]
+        return pltpu.make_async_copy(
+            source(self.at.dp), target(self.at.dp), self.own_sem.at[part]
+        )
+
+    def onward(self, part, step):
+        target = self.parts[part][1]
+        chip = (self.at.dp + 4 * LAYERS - 2 * step) % (4 * LAYERS)
+        return remote(
+            target(chip),
+            target(chip),
+            self.send_sem.at[part, self.steps + step],
+            self.recv_sem.at[part, self.steps + step],
+            (self.at.x_mate, self.at.core),
+        )
+
+    def start(self):
+        for part in range(len(self.parts)):
+            self.keep(part).start()
+
+            @pl.loop(1, self.steps)
+            def _(step):
+                self.copy(part, step).start()
+
+    def forward(self):
+        for part in range(len(self.parts)):
+            self.keep(part).wait()
+
+            @pl.loop(0, self.steps)
+            def _(step):
+                pl.when(step > 0)(lambda: self.copy(part, step).wait_recv())
+                self.onward(part, step).start()
+
+    def wait(self):
+        for part in range(len(self.parts)):
+
+            @pl.loop(0, self.steps)
+            def _(step):
+                self.onward(part, step).wait()
+                pl.when(step > 0)(lambda: self.copy(part, step).wait_send())
+
+
+def pair_ride_scratch(parts):
+    return [
+        pltpu.SemaphoreType.DMA((parts, 4 * LAYERS)),
+        pltpu.SemaphoreType.DMA((parts, 4 * LAYERS)),
+        pltpu.SemaphoreType.DMA((parts,)),
+    ]
+
+
+def strip(ref, axis, index, size):
+    at = pl.ds(pl.multiple_of(index * size, size), size)
+    return ref.at[at] if axis == 0 else ref.at[:, at]
+
+
+def reduce_scratch(block, pieces, wide=True, pair=False):
     kind = jnp.bfloat16
-    return [
-        pltpu.VMEM((4 * LAYERS,) + block, kind),
+    chips = 16 if wide else 8
+    scratch = [
+        pltpu.VMEM((chips,) + block, kind),
         pltpu.VMEM((8,) + block, kind),
         pltpu.VMEM((4,) + block, kind),
         pltpu.VMEM((8,) + block, kind),
         pltpu.SemaphoreType.DMA((20, pieces)),
         pltpu.SemaphoreType.DMA((20, pieces)),
     ]
-
-
-def gather_scratch():
-    return [pltpu.SemaphoreType.DMA((20,)), pltpu.SemaphoreType.DMA((16,))]
+    if pair:
+        scratch += [pltpu.VMEM((chips,) + block, kind)] * 2
+        scratch += [pltpu.SemaphoreType.DMA((chips,))] * 2
+    return scratch
 
 
 def mean_of_groups(sums, count):
@@ -1387,19 +1658,35 @@
 
 def res_forward_kernel(
     breadth,
-    pictures,
     gain_bias,
     conv_one,
     conv_two,
     conv_half,
-    mods,
     picks,
+    res_table,
+    ada_table,
+    image_blocks,
+    emb_blocks,
+    qkv_blocks,
+    out_blocks,
+    up_rows,
+    down_columns,
+    pictures,
+    emb,
     tokens,
     act_out,
     taps_one_out,
     taps_half,
     middle,
     stats,
+    mods,
+    qkv_head,
+    out_head,
+    up_here,
+    down_here,
+    arrived,
+    mods_blocks,
+    mods_terms,
     acts,
     taps_one,
     mine,
@@ -1411,11 +1698,54 @@
     out_sem,
     *scratch,
 ):
-    first_reduce, (act_send, act_recv), last_reduce = (scratch[:6], scratch[6:8], scratch[8:])
+    first_reduce, (act_send, act_recv), last_reduce = (scratch[:6], scratch[6:8], scratch[8:14])
     at = Place(True)
-    at.greet(True)
+    greet_all(at)
+
+    rows, cols = (up_rows.shape[0], up_here.shape[1])
+    near = 4 * LAYERS // qkv_blocks.shape[0]
+    ride = Ride(
+        at,
+        [
+            (lambda chip: emb_blocks.at[chip], lambda chip: emb.at[chip]),
+            (lambda chip: image_blocks.at[chip], lambda chip: arrived.at[chip]),
+            (lambda chip: strip(up_rows, 1, chip, cols), lambda chip: strip(up_here, 0, chip, rows)),
+            (lambda chip: mods_blocks.at[chip], lambda chip: mods_terms.at[chip]),
+            (lambda chip: strip(down_columns, 0, chip, cols), lambda chip: strip(down_here, 1, chip, rows)),
+        ],
+        *scratch[14:17],
+    )
+    attention = PairRide(
+        at,
+        [
+            (lambda chip: qkv_blocks.at[chip // near], lambda chip: strip(qkv_head, 0, chip, rows)),
+            (lambda chip: out_blocks.at[chip // near], lambda chip: strip(out_head, 1, chip, rows)),
+        ],
+        *scratch[17:20],
+    )
+    ride.start(0, 3)
     images, positions, channels = pictures.shape
+    half_c = conv_one.shape[2]
     tokens_len = positions // 4
+
+    ride.wait_for(0)
+    emb_rows = emb[:, 0, : res_table.shape[0]].astype(jnp.bfloat16)
+    lines = 0
+    for table in (res_table, ada_table):
+        terms = dot(emb_rows, table[...])
+        for line in range(table.shape[1] // 128):
+            mods_blocks[:, lines] = terms[:, 128 * line : 128 * (line + 1)]
+            lines += 1
+    ride.start(3, 4)
+    ride.wait_for(1)
+
+    @pl.loop(0, images)
+    def _(i):
+        both = arrived[i].astype(jnp.float32)
+        sides = [both[:, :channels], both[:, channels:]]
+        pictures[i] = jnp.concatenate(sides, axis=0).astype(jnp.bfloat16)
+
+    attention.start()
 
     @pl.loop(0, images)
     def _(i):
@@ -1446,13 +1776,23 @@
             total += dot(taps_one[slot, pl.ds(a * breadth, positions)], conv_one[a])
         first_reduce[0][slot] = total.astype(jnp.bfloat16)
 
-    reduce_stage(at, first_reduce[0], first_product, 2, middle, *first_reduce[1:])
+    reduce_stage(at, middle, first_product, 4, first_reduce)
+
+    ride.start(4, 5)
+    ride.wait_for(3)
+    mods[at.core] = jnp.sum(mods_terms[...], axis=0)
+    share_stage(at, mods, share_send.at[1], share_recv.at[1])
+
+    def modulation(row):
+        lines = half_c // 128
+        parts = [mods[at.core, pl.ds(row * lines + i, 1)] for i in range(lines)]
+        return jnp.concatenate(parts, axis=1)
 
     x = middle[...]
     center = mean_of_groups(jnp.sum(x, axis=0, keepdims=True), positions)
     x = x - center
     scale = lax.rsqrt(mean_of_groups(jnp.sum(x * x, axis=0, keepdims=True), positions) + GN_EPS)
-    acts[at.slot] = silu(x * scale * (1.0 + mods[0:1]) + mods[1:2]).astype(jnp.bfloat16)
+    acts[at.slot] = silu(x * scale * (1.0 + modulation(0)) + modulation(1)).astype(jnp.bfloat16)
 
     def swap(slot):
         return remote(
@@ -1470,9 +1810,10 @@
         mine[slot] = folded.astype(jnp.bfloat16)
         swap(slot).start()
 
-    gather_stage(at, acts, second_product, act_send, act_recv)
+    gather_stage(at, [acts], second_product, 4, act_send, act_recv)
     save_acts = pltpu.make_async_copy(acts, act_out, out_sem.at[1])
     save_acts.start()
+    attention.forward()
 
     def half_product(slot):
         swap(slot).wait_recv()
@@ -1487,62 +1828,75 @@
             total += dot(part, conv_half[a])
         last_reduce[0][slot] = total.astype(jnp.bfloat16)
 
-    own = tokens.at[at.core]
-    reduce_stage(at, last_reduce[0], half_product, 1, own, *last_reduce[1:])
-
-    def give(core):
-        return remote(own, tokens.at[core], share_send, share_recv, (at.dp, 1 - at.core))
-
-    give(at.core).start()
-    give(1 - at.core).wait_recv()
-    give(at.core).wait_send()
+    reduce_stage(at, tokens.at[at.core], half_product, 4, last_reduce)
+    share_stage(at, tokens, share_send.at[0], share_recv.at[0])
 
     @pl.loop(0, images)
     def _(slot):
         swap(slot).wait_send()
 
+    ride.wait_for(2)
+    ride.wait_for(4)
+    attention.wait()
     save_taps.wait()
     save_acts.wait()
 
 
-def res_forward(number, breadth, pictures, gain_bias, conv_one, conv_two, conv_half, mods, picks):
-    images, positions, channels = pictures.shape
+def res_forward(number, height, breadth, *args):
+    (gain_bias, conv_one, conv_two, conv_half, picks, res_table, ada_table, image_blocks, emb_blocks, qkv_blocks, out_blocks, up_rows, down_columns) = args
+    images, positions, channels = (4 * LAYERS, height * breadth, gain_bias.shape[1])
     half_c = conv_one.shape[2]
     half_d = conv_half.shape[2]
     tokens_len = positions // 4
     three = 3 * channels
+    rows, cols = (up_rows.shape[0], up_rows.shape[1] // images)
+    low, full = (jnp.bfloat16, jnp.float32)
+    pictures = (images, positions, channels)
     padded = (images, positions + 2 * breadth, three)
-    low = jnp.bfloat16
     acts = (images, positions, half_c)
+    lines = (res_table.shape[1] + ada_table.shape[1]) // 128
+    outs = [
+        (pictures, low),
+        (emb_blocks.shape, full),
+        ((2, tokens_len, half_d), full),
+        (acts, low),
+        (padded, low),
+        ((3, images, tokens_len, three), low),
+        ((positions, half_c), full),
+        ((2, images, channels), full),
+        ((2, lines, 128), full),
+        ((images * rows, qkv_blocks.shape[2]), low),
+        ((out_blocks.shape[1], images * rows), low),
+        ((images * rows, cols), low),
+        ((cols, images * rows), low),
+    ]
     return pl.pallas_call(
         functools.partial(res_forward_kernel, breadth),
-        out_shape=[
-            jax.ShapeDtypeStruct((2, tokens_len, half_d), jnp.float32),
-            jax.ShapeDtypeStruct(acts, low),
-            jax.ShapeDtypeStruct(padded, low),
-            jax.ShapeDtypeStruct((3, images, tokens_len, three), low),
-            jax.ShapeDtypeStruct((positions, half_c), jnp.float32),
-            jax.ShapeDtypeStruct((2, images, channels), jnp.float32),
-        ],
-        in_specs=[IN_VMEM] * 7,
-        out_specs=[IN_VMEM, ANYWHERE, ANYWHERE, IN_VMEM, IN_VMEM, IN_VMEM],
+        out_shape=[jax.ShapeDtypeStruct(shape, kind) for shape, kind in outs],
+        in_specs=[IN_VMEM] * 7 + [ANYWHERE] * 6,
+        out_specs=[IN_VMEM] * 3 + [ANYWHERE] * 2 + [IN_VMEM] * 4 + [ANYWHERE] * 4,
         scratch_shapes=[
+            pltpu.VMEM(image_blocks.shape, low),
+            pltpu.VMEM((images, lines, 128), full),
+            pltpu.VMEM((images, lines, 128), full),
             pltpu.VMEM(acts, low),
             pltpu.VMEM(padded, low),
-            pltpu.VMEM(pictures.shape, low),
-            pltpu.VMEM(pictures.shape, low),
+            pltpu.VMEM(pictures, low),
+            pltpu.VMEM(pictures, low),
             pltpu.SemaphoreType.DMA((images,)),
             pltpu.SemaphoreType.DMA((images,)),
-            pltpu.SemaphoreType.DMA,
-            pltpu.SemaphoreType.DMA,
+            pltpu.SemaphoreType.DMA((2,)),
+            pltpu.SemaphoreType.DMA((2,)),
             pltpu.SemaphoreType.DMA((2,)),
         ]
-        + reduce_scratch((positions, half_c), 2)
-        + gather_scratch()
-        + reduce_scratch((tokens_len, half_d), 1),
+        + reduce_scratch((positions, half_c), 4)
+        + gather_scratch(4)
+        + reduce_scratch((tokens_len, half_d), 4)
+        + ride_scratch(5)
+        + pair_ride_scratch(2),
         compiler_params=params(number),
         name="res_forward",
-    )(pictures, gain_bias, conv_one, conv_two, conv_half, mods, picks)
+    )(*args)
 
 
 def silu_slope(z):
@@ -1565,12 +1919,25 @@
     stats,
     acts_in,
     taps_one_in,
+    qkv_grad,
+    out_grad,
+    up_grad,
+    ada_grad,
     pictures_out,
     norm_out,
-    mods_out,
+    mods_back,
+    ada_back,
     one_out,
     two_out,
     half_out,
+    qkv_back,
+    out_back,
+    up_back,
+    qkv_pair,
+    out_pair,
+    qkv_sums,
+    out_sums,
+    mods_block,
     gathered,
     gathered_middle,
     acts,
@@ -1594,10 +1961,13 @@
     trade_send,
     trade_recv,
     io_sem,
+    share_sem,
+    neighbour_sem,
+    store_sem,
     *scratch,
 ):
     (shrunk_send, shrunk_recv), (middle_send, middle_recv) = (scratch[:2], scratch[2:4])
-    reducing = scratch[4:]
+    reducing = scratch[4:10]
     at = Place(True)
     images, positions, channels = pictures.shape
     others = images - 1
@@ -1606,19 +1976,82 @@
     load_taps = pltpu.make_async_copy(taps_one_in, taps_one, io_sem.at[1])
     load_acts.start()
     load_taps.start()
-    gathered[at.slot] = shrunk[...]
-
-    barrier = pltpu.get_barrier_semaphore()
+    gathered[at.slot] = shrunk[at.core]
+
+    greet_all(at)
 
     def peer(step):
         return (at.dp + step) % images
 
-    @pl.loop(1, others + 1)
-    def _(step):
-        pl.semaphore_signal(barrier, inc=1, device_id=(peer(step), at.core), device_id_type=MESH)
-
-    pl.semaphore_signal(barrier, inc=1, device_id=(at.dp, 1 - at.core), device_id_type=MESH)
-    pl.semaphore_wait(barrier, others + 1)
+    rows, cols = (D // images, up_grad.shape[1])
+    half = images // 2
+    side = at.dp % 2
+
+    def to_neighbour(part, place):
+        chip = 2 * place + 1 - side
+        source, target = (
+            (strip(qkv_grad, 0, chip, rows), qkv_pair.at[place]),
+            (strip(out_grad, 1, chip, rows), out_pair.at[place]),
+        )[part]
+        return remote(
+            source,
+            target,
+            neighbour_sem.at[0, part, place],
+            neighbour_sem.at[1, part, place],
+            (at.x_mate, at.core),
+        )
+
+    def store(part, step):
+        chip = (at.dp + 2 * step) % images
+        source, target = ((qkv_sums, qkv_back), (out_sums, out_back))[part]
+        return remote(
+            source.at[chip // 2],
+            target.at[at.dp // 2],
+            store_sem.at[0, part, step],
+            store_sem.at[1, part, step],
+            (chip, at.core),
+        )
+
+    def store_own(part):
+        source, target = ((qkv_sums, qkv_back), (out_sums, out_back))[part]
+        return pltpu.make_async_copy(
+            source.at[at.dp // 2], target.at[at.dp // 2], store_sem.at[0, part, 0]
+        )
+
+    def store_sums():
+        @pl.loop(0, half)
+        def _(place):
+            chip = 2 * place + side
+            to_neighbour(0, place).wait_recv()
+            own = strip(qkv_grad, 0, chip, rows)[...].astype(jnp.float32)
+            qkv_sums[place] = (own + qkv_pair[place].astype(jnp.float32)).astype(jnp.bfloat16)
+            to_neighbour(1, place).wait_recv()
+            own = strip(out_grad, 1, chip, rows)[...].astype(jnp.float32)
+            out_sums[place] = (own + out_pair[place].astype(jnp.float32)).astype(jnp.bfloat16)
+
+        for part in range(2):
+            store_own(part).start()
+
+            @pl.loop(1, half)
+            def _(step):
+                store(part, step).start()
+
+    for part in range(2):
+
+        @pl.loop(0, half)
+        def _(place):
+            to_neighbour(part, place).start()
+
+    ride = Ride(
+        at,
+        [
+            (lambda chip: ada_grad.at[at.core], lambda chip: ada_back.at[at.core, chip]),
+            (lambda chip: mods_block, lambda chip: mods_back.at[chip]),
+            (lambda chip: strip(up_grad, 0, chip, rows), lambda chip: strip(up_back, 1, chip, cols)),
+        ],
+        *scratch[10:],
+    )
+    ride.start(0, 1)
 
     def swap(slot):
         return remote(
@@ -1638,7 +2071,9 @@
         mine[slot] = fold_three(spread, breadth, True).astype(jnp.bfloat16)
         swap(slot).start()
 
-    gather_stage(at, gathered, half_back, shrunk_send, shrunk_recv)
+    gather_stage(at, [gathered], half_back, 4, shrunk_send, shrunk_recv)
+
+    store_sums()
 
     def resid(slot):
         return mine[slot].astype(jnp.float32) + theirs[slot].astype(jnp.float32)
@@ -1677,7 +2112,7 @@
     def save(source, target, sem):
         return pltpu.make_async_copy(source, target, io_sem.at[sem])
 
-    reduce_stage(at, reducing[0], second_back, 2, acted, *reducing[1:], weights_meanwhile)
+    reduce_stage(at, acted, second_back, 4, reducing, False, weights_meanwhile)
 
     x = middle[...]
     center = mean_of_groups(jnp.sum(x, axis=0, keepdims=True), positions)
@@ -1688,8 +2123,12 @@
     grad = acted[...] * silu_slope(normed * slope + mods[1:2])
     along = jnp.sum(grad * normed, axis=0, keepdims=True)
     level = jnp.sum(grad, axis=0, keepdims=True)
-    mods_out[0:1] = along
-    mods_out[1:2] = level
+    lines = along.shape[1] // 128
+    for i in range(lines):
+        mods_block[i : i + 1] = along[:, 128 * i : 128 * (i + 1)]
+        mods_block[lines + i : lines + i + 1] = level[:, 128 * i : 128 * (i + 1)]
+    ride.start(1, 2)
+    ride.start(2, 3)
     along = mean_of_groups(slope * along, positions)
     level = mean_of_groups(slope * level, positions)
     gathered_middle[at.slot] = ((slope * grad - level - normed * along) * scale).astype(jnp.bfloat16)
@@ -1709,7 +2148,7 @@
         back[slot] = folded.astype(jnp.bfloat16)
         swap_back(slot).start()
 
-    gather_stage(at, gathered_middle, first_back, middle_send, middle_recv)
+    gather_stage(at, [gathered_middle], first_back, 4, middle_send, middle_recv)
 
     gain, bias = (gain_bias[0:1], gain_bias[1:2])
 
@@ -1770,6 +2209,17 @@
 
     keep.wait()
 
+    ride.wait()
+    for part in range(2):
+        store_own(part).wait()
+
+        @pl.loop(0, half)
+        def _(step):
+            to_neighbour(part, step).wait_send()
+            pl.when(step > 0)(lambda: store(part, step).wait())
+
+    share_stage(at, ada_back, share_sem.at[0], share_sem.at[1])
+
     @pl.loop(1, others + 1)
     def _(step):
         deliver(step).wait()
@@ -1780,13 +2230,14 @@
 
 
 def res_backward(number, breadth, *args):
-    (shrunk, pictures, gain_bias, conv_one, conv_two, conv_half, mods, picks, taps_half, middle, stats, acts, taps_one) = args
+    (shrunk, pictures, gain_bias, conv_one, conv_two, conv_half, mods, picks, taps_half, middle, stats, acts, taps_one, qkv_grad, out_grad, up_grad, ada_grad) = args
     images, positions, channels = pictures.shape
     half_c = conv_one.shape[2]
     half_d = conv_half.shape[2]
     tokens_len = positions // 4
     three = 3 * channels
     low, full = (jnp.bfloat16, jnp.float32)
+    rows = qkv_grad.shape[0] // images
     grads = [(3, three, half_c), (3, three, half_c), (3, three, half_d)]
     traded = (images, positions // 2, 2 * channels)
     return pl.pallas_call(
@@ -1794,12 +2245,23 @@
         out_shape=[
             jax.ShapeDtypeStruct(traded, low),
             jax.ShapeDtypeStruct((2, channels), full),
-            jax.ShapeDtypeStruct((2, half_c), full),
+            jax.ShapeDtypeStruct((images, 2 * half_c // 128, 128), full),
+            jax.ShapeDtypeStruct((2, images) + ada_grad.shape[1:], ada_grad.dtype),
         ]
-        + [jax.ShapeDtypeStruct(shape, full) for shape in grads],
-        in_specs=[IN_VMEM] * 11 + [ANYWHERE] * 2,
-        out_specs=[ANYWHERE, IN_VMEM, IN_VMEM] + [ANYWHERE] * 3,
+        + [jax.ShapeDtypeStruct(shape, full) for shape in grads]
+        + [
+            jax.ShapeDtypeStruct((images // 2, rows, qkv_grad.shape[1]), low),
+            jax.ShapeDtypeStruct((images // 2, out_grad.shape[0], rows), low),
+            jax.ShapeDtypeStruct((rows, images * up_grad.shape[1]), low),
+        ],
+        in_specs=[IN_VMEM] * 11 + [ANYWHERE] * 2 + [IN_VMEM] * 2 + [ANYWHERE] * 2,
+        out_specs=[ANYWHERE, IN_VMEM] + [ANYWHERE] * 8,
         scratch_shapes=[
+            pltpu.VMEM((images // 2, rows, qkv_grad.shape[1]), low),
+            pltpu.VMEM((images // 2, out_grad.shape[0], rows), low),
+            pltpu.VMEM((images // 2, rows, qkv_grad.shape[1]), low),
+            pltpu.VMEM((images // 2, out_grad.shape[0], rows), low),
+            pltpu.VMEM((2 * half_c // 128, 128), full),
             pltpu.VMEM((images, tokens_len, half_d), low),
             pltpu.VMEM((images, positions, half_c), low),
             pltpu.VMEM(acts.shape, low),
@@ -1817,40 +2279,286 @@
         + [pltpu.VMEM(shape, full) for shape in grads]
         + [pltpu.SemaphoreType.DMA((images,))] * 4
         + [pltpu.SemaphoreType.DMA((images - 1,))] * 2
-        + [pltpu.SemaphoreType.DMA((6,))]
-        + gather_scratch()
-        + gather_scratch()
-        + reduce_scratch((positions, half_c), 2),
+        + [pltpu.SemaphoreType.DMA((6,)), pltpu.SemaphoreType.DMA((2,))]
+        + [pltpu.SemaphoreType.DMA((2, 2, images // 2))] * 2
+        + gather_scratch(4)
+        + gather_scratch(4)
+        + reduce_scratch((positions, half_c), 4)
+        + ride_scratch(3),
         compiler_params=params(number),
         name="res_backward",
     )(*args)
 
 
-def widen(block):
-    return block.astype(jnp.float32)
-
-
-def lower(block):
-    return block.astype(jnp.bfloat16)
-
-
-def paired_lanes(block):
-    half = block.shape[-2] // 2
-    return jnp.concatenate([block[..., :half, :], block[..., half:, :]], axis=-1)
-
-
-def unpaired_lanes(block):
-    half = block.shape[-1] // 2
-    return jnp.concatenate([block[..., :half], block[..., half:]], axis=-2)
-
-
-def trade_dp(blocks):
-    return lax.all_to_all(blocks, DP, 0, 0)
-
-
-def core_rows(block, tensor_pos):
-    half = block.shape[0] // 2
-    return lax.dynamic_slice_in_dim(block, tensor_pos * half, half, axis=0)
+def gelu_of(z):
+    inner = jnp.tanh(math.sqrt(2.0 / math.pi) * (z + 0.044715 * z * z * z))
+    return 0.5 * z * (1.0 + inner)
+
+
+def gelu_slope(z):
+    rate = math.sqrt(2.0 / math.pi)
+    inner = jnp.tanh(rate * (z + 0.044715 * z * z * z))
+    return 0.5 * (1.0 + inner) + 0.5 * z * (1.0 - inner * inner) * rate * (1.0 + 3 * 0.044715 * z * z)
+
+
+def transformer_kernel(
+    shrunk,
+    mods,
+    cotangent,
+    qkv_head,
+    out_head,
+    up_here,
+    down_here,
+    block_out,
+    token_grad,
+    mods_grad,
+    qkv_grad,
+    out_grad,
+    up_grad,
+    down_back,
+    tokens,
+    held,
+    attn_in,
+    qkv,
+    probs,
+    mixed,
+    attended,
+    mlp_in,
+    expanded_grad,
+    pre_act,
+    hidden,
+    pre_grad,
+    expanded,
+    mlp_grad,
+    down_grad,
+    attended_grad,
+    mixed_grad,
+    qkv_back,
+    attn_grad,
+    share_send,
+    share_recv,
+    *scratch,
+):
+    scratch = list(scratch)
+
+    def take(count):
+        taken = scratch[:count]
+        del scratch[:count]
+        return taken
+
+    gather_one, gather_two, gather_three = (take(4), take(4), take(4))
+    reduce_one, reduce_two, reduce_three, reduce_four = (take(10), take(10), take(10), take(10))
+    ride_back = take(3)
+    at, near = (Place(True), Place(False))
+    greet_all(at)
+    tokens_len = cotangent.shape[0]
+    half = tokens_len // 2
+    rows, cols = (D // (4 * LAYERS), up_here.shape[1])
+    images = 4 * LAYERS
+    score_scale = HDIM ** (-0.5)
+    low, full = (jnp.bfloat16, jnp.float32)
+    mine = pl.ds(pl.multiple_of(at.core * half, half), half)
+    theirs = pl.ds(pl.multiple_of((1 - at.core) * half, half), half)
+
+    def own_rows(value, out):
+        held[...] = value.astype(low)
+        out[...] = held[mine]
+
+    def split(place, value, stage):
+        held[...] = value.astype(low)
+        stage[0][place] = held[mine]
+        stage[6][place] = held[theirs]
+
+    def image_rows(i):
+        return pl.ds(pl.multiple_of(i * tokens_len, tokens_len), tokens_len)
+
+    tokens[:, : shrunk.shape[2]] = shrunk[0]
+    tokens[:, shrunk.shape[2] :] = shrunk[1]
+    normed, _ = layer_stats(tokens[...])
+    own_rows(normed * (1.0 + mods[1:2]) + mods[0:1], attn_in.at[near.slot, near.core])
+    gather_stage(near, [attn_in], None, 4, *gather_one[:2], gather_one[2:])
+
+    @pl.loop(0, images // 2)
+    def _(i):
+        rows_in = attn_in[i].reshape(tokens_len, D)
+        low_qkv = dot(rows_in, qkv_head[...]).astype(low)
+        qkv[image_rows(i)] = low_qkv
+        query, key, value = (low_qkv[:, j * HDIM : (j + 1) * HDIM] for j in range(3))
+        scores = dot_nt(query, key) * score_scale
+        scores = scores - jnp.max(scores, axis=1, keepdims=True)
+        weight = jnp.exp(scores)
+        weight = weight / jnp.sum(weight, axis=1, keepdims=True)
+        probs[i] = weight
+        mixed[image_rows(i)] = dot(weight.astype(low), value).astype(low)
+
+    def attention_term(place):
+        split(place, dot(mixed[image_rows(place)], out_head[...]), reduce_one)
+
+    reduce_stage(near, attended.at[at.core], attention_term, 4, reduce_one, True)
+    share_stage(at, attended, share_send.at[0], share_recv.at[0])
+
+    def whole(ref):
+        return ref[...].reshape(tokens_len, D)
+
+    after = tokens[...] + (1.0 + mods[2:3]) * whole(attended)
+    normed, _ = layer_stats(after)
+    own_rows(normed * (1.0 + mods[4:5]) + mods[3:4], mlp_in.at[at.slot, at.core])
+    own_rows(
+        (1.0 + mods[5:6]) * cotangent[...].astype(full), expanded_grad.at[at.slot, at.core]
+    )
+    gather_stage(at, [mlp_in, expanded_grad], None, 4, *gather_two[:2], gather_two[2:])
+
+    @pl.loop(0, LAYERS)
+    def _(i):
+        here = pl.ds(pl.multiple_of(i * 4 * tokens_len, 4 * tokens_len), 4 * tokens_len)
+        z = dot(mlp_in[pl.ds(4 * i, 4)].reshape(4 * tokens_len, D), up_here[...])
+        pre_act[here] = z
+        hidden[here] = gelu_of(z).astype(low)
+
+    def hidden_term(place):
+        split(place, dot(hidden[image_rows(place)], down_here[...]), reduce_two)
+
+    def hidden_grads():
+        @pl.loop(0, LAYERS)
+        def _(i):
+            here = pl.ds(pl.multiple_of(i * 4 * tokens_len, 4 * tokens_len), 4 * tokens_len)
+            grad = dot_nt(expanded_grad[pl.ds(4 * i, 4)].reshape(4 * tokens_len, D), down_here[...])
+            pre_grad[here] = (grad * gelu_slope(pre_act[here])).astype(low)
+
+        @pl.loop(0, D // 512)
+        def _(i):
+            here = pl.ds(pl.multiple_of(i * 512, 512), 512)
+            left = expanded_grad[:, :, :, here].reshape(images * tokens_len, 512)
+            down_grad[:, here] = dot_tn(hidden[...], left).astype(low)
+            right = mlp_in[:, :, :, here].reshape(images * tokens_len, 512)
+            up_grad[here] = dot_tn(right, pre_grad[...]).astype(low)
+
+    reduce_stage(at, expanded.at[at.core], hidden_term, 4, reduce_two, True, hidden_grads)
+    back = Ride(
+        at,
+        [
+            (lambda chip: strip(down_grad, 1, chip, rows), lambda chip: strip(down_back, 0, chip, cols)),
+        ],
+        *ride_back,
+    )
+    back.start()
+    share_stage(at, expanded, share_send.at[1], share_recv.at[1])
+    block_out[...] = (after + (1.0 + mods[5:6]) * whole(expanded)).astype(low)
+    upstream = cotangent[...].astype(full)
+    mods_grad[5:6] = jnp.sum(upstream * whole(expanded), axis=0, keepdims=True)
+
+    def mlp_term(place):
+        split(place, dot_nt(pre_grad[image_rows(place)], up_here[...]), reduce_three)
+
+    reduce_stage(at, mlp_grad.at[at.core], mlp_term, 4, reduce_three, True)
+    share_stage(at, mlp_grad, share_send.at[2], share_recv.at[2])
+    after = tokens[...] + (1.0 + mods[2:3]) * whole(attended)
+    normed, scale = layer_stats(after)
+    grad = whole(mlp_grad)
+    mods_grad[3:4] = jnp.sum(grad, axis=0, keepdims=True)
+    mods_grad[4:5] = jnp.sum(grad * normed, axis=0, keepdims=True)
+    grad_after = cotangent[...].astype(full) + layer_back(normed, scale, (1.0 + mods[4:5]) * grad)
+    mods_grad[2:3] = jnp.sum(grad_after * whole(attended), axis=0, keepdims=True)
+
+    own_rows((1.0 + mods[2:3]) * grad_after, attended_grad.at[near.slot, near.core])
+    attended[...] = grad_after.reshape(attended.shape)
+    gather_stage(near, [attended_grad], None, 4, *gather_three[:2], gather_three[2:])
+
+    @pl.loop(0, images // 2)
+    def _(i):
+        grad = dot_nt(attended_grad[i].reshape(tokens_len, D), out_head[...]).astype(low)
+        low_qkv = qkv[image_rows(i)]
+        query, key, value = (low_qkv[:, j * HDIM : (j + 1) * HDIM] for j in range(3))
+        weight = probs[i]
+        grad_probs = dot_nt(grad, value)
+        grad_value = dot_tn(weight.astype(low), grad)
+        inner = jnp.sum(grad_probs * weight, axis=1, keepdims=True)
+        grad_scores = (weight * (grad_probs - inner)).astype(low)
+        grad_query = dot(grad_scores, key) * score_scale
+        grad_key = dot_tn(grad_scores, query) * score_scale
+        qkv_back[image_rows(i)] = jnp.concatenate(
+            [grad_query, grad_key, grad_value], axis=1
+        ).astype(low)
+
+    def qkv_term(place):
+        split(place, dot_nt(qkv_back[image_rows(place)], qkv_head[...]), reduce_four)
+
+    def attention_grads():
+        @pl.loop(0, D // 512)
+        def _(i):
+            here = pl.ds(pl.multiple_of(i * 512, 512), 512)
+            right = attended_grad[:, :, :, here].reshape(images // 2 * tokens_len, 512)
+            out_grad[:, here] = dot_tn(mixed[...], right).astype(low)
+            left = attn_in[:, :, :, here].reshape(images // 2 * tokens_len, 512)
+            qkv_grad[here] = dot_tn(left, qkv_back[...]).astype(low)
+
+    reduce_stage(near, attn_grad.at[at.core], qkv_term, 4, reduce_four, True, attention_grads)
+    share_stage(at, attn_grad, share_send.at[3], share_recv.at[3])
+    normed, scale = layer_stats(tokens[...])
+    grad = whole(attn_grad)
+    mods_grad[0:1] = jnp.sum(grad, axis=0, keepdims=True)
+    mods_grad[1:2] = jnp.sum(grad * normed, axis=0, keepdims=True)
+    grad = whole(attended) + layer_back(normed, scale, (1.0 + mods[1:2]) * grad)
+    token_grad[0] = grad[:, : shrunk.shape[2]].astype(low)
+    token_grad[1] = grad[:, shrunk.shape[2] :].astype(low)
+    back.wait()
+
+
+def transformer(number, *args):
+    shrunk, mods, cotangent, qkv_head, out_head, up_here, down_here = args
+    tokens_len = cotangent.shape[0]
+    images = 4 * LAYERS
+    half = tokens_len // 2
+    rows, cols = (D // images, up_here.shape[1])
+    low, full = (jnp.bfloat16, jnp.float32)
+    both = (2, half, D)
+    near_tokens = images // 2 * tokens_len
+    vmem = [
+        ((tokens_len, D), full),
+        ((tokens_len, D), low),
+        ((images // 2,) + both, low),
+        ((near_tokens, 3 * HDIM), low),
+        ((images // 2, tokens_len, tokens_len), full),
+        ((near_tokens, HDIM), low),
+        (both, full),
+        ((images,) + both, low),
+        ((images,) + both, low),
+        ((images * tokens_len, cols), full),
+        ((images * tokens_len, cols), low),
+        ((images * tokens_len, cols), low),
+        (both, full),
+        (both, full),
+        ((cols, D), low),
+        ((images // 2,) + both, low),
+        ((near_tokens, HDIM), low),
+        ((near_tokens, 3 * HDIM), low),
+        (both, full),
+    ]
+    return pl.pallas_call(
+        transformer_kernel,
+        out_shape=[
+            jax.ShapeDtypeStruct((tokens_len, D), low),
+            jax.ShapeDtypeStruct(shrunk.shape, low),
+            jax.ShapeDtypeStruct(mods.shape, full),
+            jax.ShapeDtypeStruct(qkv_head.shape, low),
+            jax.ShapeDtypeStruct(out_head.shape, low),
+            jax.ShapeDtypeStruct((D, cols), low),
+            jax.ShapeDtypeStruct((images * cols, rows), low),
+        ],
+        in_specs=[IN_VMEM] * 7,
+        out_specs=[IN_VMEM] * 6 + [ANYWHERE],
+        scratch_shapes=[pltpu.VMEM(shape, kind) for shape, kind in vmem]
+        + [pltpu.SemaphoreType.DMA((4,))] * 2
+        + gather_scratch(4, 1, False, True)
+        + gather_scratch(4, 2, True, True)
+        + gather_scratch(4, 1, False, True)
+        + reduce_scratch((half, D), 4, False, True)
+        + reduce_scratch((half, D), 4, True, True) * 2
+        + reduce_scratch((half, D), 4, False, True)
+        + ride_scratch(1),
+        compiler_params=params(number),
+        name="transformer",
+    )(*args)
 
 
 def layer_stats(values):
@@ -1865,6 +2573,24 @@
     first = jnp.mean(grad, axis=-1, keepdims=True)
     second = jnp.mean(grad * normed, axis=-1, keepdims=True)
     return (grad - first - normed * second) * scale
+
+
+def widen(block):
+    return block.astype(jnp.float32)
+
+
+def lower(block):
+    return block.astype(jnp.bfloat16)
+
+
+def paired_lanes(block):
+    half = block.shape[-2] // 2
+    return jnp.concatenate([block[..., :half, :], block[..., half:, :]], axis=-1)
+
+
+def unpaired_lanes(block):
+    half = block.shape[-1] // 2
+    return jnp.concatenate([block[..., :half], block[..., half:]], axis=-2)
 
 
 def half_picks(height, breadth):
@@ -1970,22 +2696,8 @@
     half_d = down_conv.shape[3]
     freq_rows = resnet_mod.shape[0]
     heads_here = out_proj.shape[0]
-    hidden_cols = hidden_in.shape[1] // n_dp
-    score_scale = HDIM ** (-0.5)
-    as_maps = (n_dp, height, breadth, local_c)
     picks = half_picks(height, breadth)
     numbers = itertools.count()
-
-    def gather_tokens(block, wide):
-        gathered = gather(next(numbers), core_rows(block, tensor_pos), wide, True)
-        return gathered.reshape(-1, D)
-
-    def reduce_tokens(partial, wide):
-        blocks = lower(partial).reshape(-1, 2, tokens_len // 2, D)
-        return reduce(next(numbers), blocks, wide, True, True).reshape(tokens_len, D)
-
-    def sum_cores(maps):
-        return add_core(next(numbers), lower(maps).reshape(-1, local_c)).reshape(as_maps)
 
     def sum_all(local):
         return total(next(numbers), jnp.full((8, 128), local))[0, 0]
@@ -1994,110 +2706,55 @@
     conv_one = lower(first_conv).reshape(3, 3 * local_c, half_c)
     conv_two = lower(second_conv).transpose(0, 2, 1, 3).reshape(3, half_c, 3 * local_c)
     conv_half = lower(down_conv).reshape(3, 3 * local_c, half_d)
-    qkv_blocks = jnp.repeat(lower(qkv_proj).transpose(2, 0, 1, 3), n_dp // heads_here, axis=0)
-    qkv_head = trade_dp(qkv_blocks).reshape(D, 3 * HDIM)
-    out_blocks = jnp.repeat(lower(out_proj), n_dp // heads_here, axis=0)
-    out_head = trade_dp(out_blocks).transpose(1, 0, 2).reshape(HDIM, D)
-    up_blocks = lower(hidden_in).reshape(D // n_dp, n_dp, hidden_cols).transpose(1, 0, 2)
-    up_here = trade_dp(up_blocks).reshape(D, hidden_cols)
-    down_blocks = lower(hidden_out).reshape(n_dp, hidden_cols, D // n_dp)
-    down_here = trade_dp(down_blocks).transpose(1, 0, 2).reshape(hidden_cols, D)
-
-    emb = embed_noise(t_index, FREQ).reshape(FREQ // 128, 128)
-    emb = jnp.broadcast_to(jnp.pad(emb, ((0, 8 - FREQ // 128), (0, 0))), (n_dp, 8, 128))
+    qkv_blocks = lower(qkv_proj).transpose(2, 0, 1, 3).reshape(heads_here, D // n_dp, 3 * HDIM)
+
+    emb = widen(lower(embed_noise(t_index, FREQ))).reshape(n_dp, 1, freq_rows)
+    emb = jnp.pad(emb, ((0, 0), (0, 7), (0, 128 - freq_rows)))
     image_blocks = images.reshape(positions, n_dp, local_c).transpose(1, 0, 2)
-    pictures, emb = trade(next(numbers), paired_lanes(image_blocks), emb)
-    pictures = unpaired_lanes(pictures)
-
-    emb_low = lower(emb[:, : FREQ // 128].reshape(n_dp, FREQ))
-    emb_rows = lax.dynamic_slice_in_dim(emb_low, dp_pos * freq_rows, freq_rows, axis=1)
-    res_partial = dot(emb_rows, lower(resnet_mod).reshape(freq_rows, 2 * half_c))
-    ada_partial = dot(emb_rows, lower(ada_proj).reshape(freq_rows, 6 * D))
-    ada_partial = lax.dynamic_slice_in_dim(ada_partial, tensor_pos * 3 * D, 3 * D, axis=1)
-    mods = jnp.concatenate([res_partial, ada_partial], axis=1).reshape(n_dp, -1, 128)
-    mods = reduce(next(numbers), mods, True, False, True).reshape(2, -1)
-    res_mods = lax.dynamic_index_in_dim(mods, tensor_pos, 0, keepdims=False)[: 2 * half_c]
+    ada_half = lax.dynamic_slice_in_dim(ada_proj, tensor_pos * 3, 3, axis=1)
+    convs = (conv_one, conv_two, conv_half)
+
+    pictures, emb, shrunk, act_two, taps_one, taps_half, middle, stats_one, mods, *heads = res_forward(
+        next(numbers),
+        height,
+        breadth,
+        gain_bias,
+        *convs,
+        picks,
+        lower(resnet_mod).reshape(freq_rows, 2 * half_c),
+        lower(ada_half).reshape(freq_rows, 3 * D),
+        paired_lanes(image_blocks),
+        emb,
+        qkv_blocks,
+        lower(out_proj),
+        lower(hidden_in),
+        lower(hidden_out),
+    )
+    qkv_head, out_head, up_here, down_here = heads
+    res_lines = 2 * half_c // 128
+    res_mods = lax.dynamic_index_in_dim(mods, tensor_pos, 0, keepdims=False)[:res_lines]
     res_mods = res_mods.reshape(2, half_c)
-    ada_mods = mods[:, 2 * half_c :].reshape(6, D)
-    shift_one, scale_one, gate_one = (ada_mods[0], 1.0 + ada_mods[1], 1.0 + ada_mods[2])
-    shift_two, scale_two, gate_two = (ada_mods[3], 1.0 + ada_mods[4], 1.0 + ada_mods[5])
-    upstream = widen(cotangent).reshape(tokens_len, D)
-    grad_expanded = gather_tokens(lower(gate_two * upstream), True)
-
-    shrunk, act_two, taps_one, taps_half, middle, stats_one = res_forward(
-        next(numbers), breadth, pictures, gain_bias, conv_one, conv_two, conv_half, res_mods, picks
-    )
-    tokens = jnp.concatenate([shrunk[0], shrunk[1]], axis=1)
-
-    token_normed, token_spread = layer_stats(tokens)
-    attn_in = gather_tokens(lower(token_normed * scale_one + shift_one), False)
-    near = n_dp // 2
-    qkv_low = lower(dot(attn_in, qkv_head)).reshape(near, tokens_len, 3, HDIM)
-    query_low, key_low, value_low = (qkv_low[:, :, 0], qkv_low[:, :, 1], qkv_low[:, :, 2])
-    scores = (
-        jnp.einsum("bqd,bkd->bqk", query_low, key_low, preferred_element_type=jnp.float32) * score_scale
-    )
-    row_max = jnp.max(scores, axis=-1, keepdims=True)
-    log_total = row_max + jnp.log(jnp.sum(jnp.exp(scores - row_max), axis=-1, keepdims=True))
-    attention = jnp.exp(scores - log_total)
-    attention_low = lower(attention)
-    mixed = lower(
-        jnp.einsum("bqk,bkd->bqd", attention_low, value_low, preferred_element_type=jnp.float32)
-    ).reshape(near * tokens_len, HDIM)
-    attended = reduce_tokens(dot(mixed, out_head), False)
-    after_attn = tokens + gate_one * attended
-    after_normed, after_spread = layer_stats(after_attn)
-    mlp_in = gather_tokens(lower(after_normed * scale_two + shift_two), True)
-    pre_act = dot(mlp_in, up_here)
-    hidden_act, gelu_back = jax.vjp(gelu_tanh, pre_act)
-    hidden_low = lower(hidden_act)
-    expanded = reduce_tokens(dot(hidden_low, down_here), True)
-    block_out = lower(after_attn + gate_two * expanded)
-
-    grad_gate_two = jnp.sum(upstream * expanded, axis=0)
-    grad_down = dot_tn(hidden_low, grad_expanded)
-    (grad_pre,) = gelu_back(dot_nt(grad_expanded, down_here))
-    grad_pre_low = lower(grad_pre)
-    grad_mlp_in = reduce_tokens(dot_nt(grad_pre_low, up_here), True)
-    grad_up = dot_tn(mlp_in, grad_pre_low)
-    grad_after = upstream + layer_back(after_normed, after_spread, scale_two * grad_mlp_in)
-    grad_attended = gather_tokens(lower(gate_one * grad_after), False)
-    grad_out = dot_tn(mixed, grad_attended)
-    grad_mixed = lower(dot_nt(grad_attended, out_head)).reshape(near, tokens_len, HDIM)
-    grad_probs = jnp.einsum(
-        "bqd,bkd->bqk", grad_mixed, value_low, preferred_element_type=jnp.float32
-    )
-    grad_values = jnp.einsum(
-        "bqk,bqd->bkd", attention_low, grad_mixed, preferred_element_type=jnp.float32
-    )
-    grad_scores = lower(
-        attention * (grad_probs - jnp.sum(grad_probs * attention, axis=-1, keepdims=True))
-    )
-    grad_query = (
-        jnp.einsum("bqk,bkd->bqd", grad_scores, key_low, preferred_element_type=jnp.float32)
-        * score_scale
-    )
-    grad_keys = (
-        jnp.einsum("bqk,bqd->bkd", grad_scores, query_low, preferred_element_type=jnp.float32)
-        * score_scale
-    )
-    grad_qkv = lower(jnp.concatenate([grad_query, grad_keys, grad_values], axis=2)).reshape(
-        near * tokens_len, 3 * HDIM
-    )
-    grad_attn_in = reduce_tokens(dot_nt(grad_qkv, qkv_head), False)
-    grad_qkv_w = dot_tn(attn_in, grad_qkv)
-    grad_tokens = grad_after + layer_back(token_normed, token_spread, scale_one * grad_attn_in)
-
-    grad_shrunk = lower(lax.dynamic_slice_in_dim(grad_tokens, tensor_pos * half_d, half_d, axis=1))
-    images_grad, grad_norm_params, grad_res_mods, grad_conv_one, grad_conv_two, grad_half = res_backward(
+    ada_mods = mods[:, res_lines:].reshape(6, D)
+
+    block_out, grad_tokens, grad_ada, grad_qkv_w, grad_out, grad_up, grad_down = transformer(
+        next(numbers),
+        shrunk,
+        ada_mods,
+        cotangent.reshape(tokens_len, D),
+        qkv_head,
+        out_head,
+        up_here,
+        down_here,
+    )
+    grad_ada = lower(grad_ada).reshape(2, 3 * D // 128, 128)
+
+    images_grad, grad_norm_params, grad_res, grad_ada, *returned = res_backward(
         next(numbers),
         breadth,
-        grad_shrunk,
+        grad_tokens,
         pictures,
         gain_bias,
-        conv_one,
-        conv_two,
-        conv_half,
+        *convs,
         res_mods,
         picks,
         taps_half,
@@ -2105,41 +2762,21 @@
         stats_one,
         act_two,
         taps_one,
-    )
+        grad_qkv_w,
+        grad_out,
+        grad_up,
+        grad_ada,
+    )
+    grad_conv_one, grad_conv_two, grad_half, grad_qkv_w, grad_out, grad_up = returned
     images_grad = widen(unpaired_lanes(images_grad))
     images_grad = images_grad.transpose(1, 0, 2).reshape((1, height, breadth, C))
 
-    grad_ada = jnp.concatenate(
-        [
-            jnp.sum(grad_attn_in, axis=0),
-            jnp.sum(grad_attn_in * token_normed, axis=0),
-            jnp.sum(grad_after * attended, axis=0),
-            jnp.sum(grad_mlp_in, axis=0),
-            jnp.sum(grad_mlp_in * after_normed, axis=0),
-            grad_gate_two,
-        ]
-    )
-    grad_ada = lax.dynamic_slice_in_dim(grad_ada, tensor_pos * 3 * D, 3 * D, axis=0)
-    grad_mods = jnp.concatenate([grad_res_mods.reshape(-1), grad_ada]).reshape(-1, 128)
-    grad_mods = gather(next(numbers), grad_mods, True, True).reshape(n_dp, 2, -1)
-    grad_ada = grad_mods[:, :, 2 * half_c :].reshape(n_dp, 6 * D)
-    grad_mods = lax.dynamic_index_in_dim(grad_mods, tensor_pos, 1, keepdims=False)
-    emb_cols = widen(emb_rows)
-    grad_ada = jnp.einsum("bf,bk->fk", emb_cols, grad_ada, precision=HIGHEST)
-    grad_res = jnp.einsum("bf,bk->fk", emb_cols, grad_mods[:, : 2 * half_c], precision=HIGHEST)
-
-    grad_qkv_w = trade_dp(lower(grad_qkv_w).reshape(n_dp, D // n_dp, 3, HDIM))
-    grad_qkv_w = jnp.sum(
-        widen(grad_qkv_w).reshape((heads_here, n_dp // heads_here) + grad_qkv_w.shape[1:]), axis=1
-    ).transpose(1, 2, 0, 3)
-    grad_out = trade_dp(lower(grad_out).reshape(HDIM, n_dp, D // n_dp).transpose(1, 0, 2))
-    grad_out = jnp.sum(
-        widen(grad_out).reshape((heads_here, n_dp // heads_here) + grad_out.shape[1:]), axis=1
-    )
-    grad_up = widen(trade_dp(lower(grad_up).reshape(n_dp, D // n_dp, hidden_cols)))
-    grad_up = grad_up.transpose(1, 0, 2).reshape(hidden_in.shape)
-    grad_down = trade_dp(lower(grad_down).reshape(hidden_cols, n_dp, D // n_dp).transpose(1, 0, 2))
-    grad_down = widen(grad_down).reshape(hidden_out.shape)
+    emb_cols = emb[:, 0, :freq_rows]
+    grad_ada = widen(grad_ada).reshape(2, n_dp, 3 * D)
+    grad_ada = jnp.einsum("bf,cbk->fck", emb_cols, grad_ada, precision=HIGHEST)
+    grad_res = jnp.einsum("bf,bk->fk", emb_cols, grad_res.reshape(n_dp, -1), precision=HIGHEST)
+
+    grad_qkv_w = widen(grad_qkv_w).reshape(heads_here, D // n_dp, 3, HDIM).transpose(1, 2, 0, 3)
 
     combined_total = (
         grad_norm_params,
@@ -2149,9 +2786,9 @@
         grad_half.reshape(down_conv.shape),
         grad_ada.reshape(ada_proj.shape),
         grad_qkv_w,
-        grad_out,
-        grad_up,
-        grad_down,
+        widen(grad_out),
+        widen(grad_up),
+        widen(grad_down),
     )
     results = clipped_step(masters, averages, squares, combined_total, sum_all)
     return (block_out[None], images_grad) + results

time: 888 us -> 762 us (0.86)
  local copies, waits for them, and re-layouts: 83.8 us -> 41.5 us
  starting transfers between devices: 41.8 us -> 0 us
  Pallas kernels: 610 us -> 641 us
  matrix products: 33.4 us -> 3.74 us
  waiting for transfers between devices: 21.9 us -> 0 us
  other arithmetic: 75.7 us -> 60.1 us
    pallas_call x11 -> x1, Pallas kernels: 308 us -> 233 us  [transformer(): pl.pallas_call(transformer_kernel, out_shape=[jax.ShapeDtypeStruct((token...]
    pallas_call x1, Pallas kernels: 143 us -> 213 us  [res_forward(): pl.pallas_call(functools.partial(res_forward_kernel, breadth), out_shape=...]
    all_to_all x8 -> x0, starting transfers between devices: 41.8 us -> none  [trade_dp(): return lax.all_to_all(blocks, DP, 0, 0)]
    pallas_call x1, Pallas kernels: 146 us -> 183 us  [res_backward(): pl.pallas_call(functools.partial(res_backward_kernel, breadth), out_shape...]
    dot_general x22 -> x2, matrix products: 33.4 us -> 3.74 us  [the longest x1 2.26 us: stationary(): grad_ada = jnp.einsum('bf,cbk->fck', emb_cols, grad_ada, precision=HIGHEST)]
    all_to_all x8 -> x0, waiting for transfers between devices: 21.9 us -> none  [trade_dp(): return lax.all_to_all(blocks, DP, 0, 0)]
    unnamed x281 -> x117, local copies, waits for them, and re-layouts: 41.1 us -> 23.1 us
  transfers between devices with their start and end apart: 8 -> 0, of which waited for: 3 -> 0; matrix products, arithmetic and copies ran while one was open for 12% -> 0% of each run, Pallas kernels for 52% -> 0%
where the time goes in v2:
time: 762 us; the launch traced here: 757 us
  Pallas kernels  641 us (84%)
  other arithmetic  60.1 us (8%)
  local copies, waits for them, and re-layouts  41.5 us (5%)
  between operations  10.5 us (1%)
    pallas_call x1, Pallas kernels, transformer(): pl.pallas_call(transformer_kernel, out_shape=[jax.ShapeDtypeStruct((token...  233 us
    pallas_call x1, Pallas kernels, res_forward(): pl.pallas_call(functools.partial(res_forward_kernel, breadth), out_shape=...  213 us
    pallas_call x1, Pallas kernels, res_backward(): pl.pallas_call(functools.partial(res_backward_kernel, breadth), out_shape...  183 us
    sub x10, other arithmetic, clipped_step(): new_master = master - learn_rate * (step_dir + DECAY * master)  29.9 us
    unnamed x117, local copies, waits for them, and re-layouts  23.1 us

profile of v2, /device:TPU:0, one launch (start us, length us, event | category | flops | bytes accessed | tf_op | source)
XLA Modules:
  0.0 756.6 jit_solution(6650672645994938088)
XLA Ops:
  1.7 1.2 convert_convert_fusion.gain_bias
  5.9 1.0 fusion.14
  7.6 1.8 convert_element_type.95.out_blocks
  10.4 1.2 copy.83.conv_two
  12.6 1.1 pad_maximum_fusion.image_blocks
  14.3 1.1 convert_element_type.96.up_rows
  16.2 1.1 convert_element_type.97.down_columns
  17.3 1.0 copy-done.1
  18.3 1.2 convert_element_type.88
  20.8 1.2 copy.84.qkv_blocks
  22.0 3.1 copy.96
  25.1 1.7 copy.98
  26.8 213.2 %res_forward.1 = (bf16[16,256,64]{2,1,0:T(8,128)(2,1)}, f32[16,8,128]{2,1,0:T(8,128)}, f32[2,64,1024]{2,1,0:T(8,128)}, bf16[16,256,512]{2,1,0:T(8,128)(2,1)}, bf...) custom-call(f32[2,64]{1,0:T(2,128)} %convert_convert_fusion.gain_bia, ...), custom_call_target="tpu_custom_call" | custom-call | tf_op jit(solution)/shard_map/res_forward/pallas_call | solution.py:1873
  243.6 232.5 %transformer.1 = (bf16[64,2048]{1,0:T(8,128)(2,1)}, bf16[2,64,1024]{2,1,0:T(8,128)(2,1)}, f32[6,2048]{1,0:T(8,128)}, bf16[2048,384]{1,0:T(8,128)(2,1)}, bf16[128...) custom-call(f32[2,64,1024]{2,1,0:T(8,128)} %get-tuple-element.63.shrunk, ...), custom_call_target="tpu_custom_call" | custom-call | tf_op jit(solution)/shard_map/transformer/pallas_call | solution.py:2537
  476.2 2.4 fusion.2
  480.0 182.6 %res_backward.1 = (bf16[16,128,128]{2,1,0:T(8,128)(2,1)}, f32[2,64]{1,0:T(2,128)}, f32[16,8,128]{2,1,0:T(8,128)}, bf16[2,16,48,128]{3,2,1,0:T(8,128)(2,1)}, f32[...) custom-call(bf16[2,64,1024]{2,1,0:T(8,128)(2,1)} %get-tuple-element., ...), custom_call_target="tpu_custom_call" | custom-call | tf_op jit(solution)/shard_map/res_backward/pallas_call | solution.py:2243
  662.7 2.4 fusion.1
  665.1 1.7 fusion.10
  666.8 1.0 fusion.5
  667.8 3.0 multiply_reduce_fusion
  670.8 0.9 multiply_reduce_fusion.1
  671.7 0.9 multiply_reduce_fusion.2
  674.5 1.5 multiply_reduce_fusion.4
  678.1 1.2 copy.138
  679.3 1.3 dot_general.18
  680.6 2.3 multiply_reduce_fusion.3
  686.7 12.4 %total.1 = f32[8,128]{1,0:T(8,128)} custom-call(f32[8,128]{1,0:T(8,128)} %broadcast_in_dim.5.in_ref), custom_call_target="tpu_custom_call" | custom-call | tf_op jit(solution)/shard_map/total/pallas_call | solution.py:1096
  699.1 1.3 slice.32
  701.1 2.4 broadcast_multiply_fusion.1
  703.6 1.6 broadcast_multiply_fusion
  705.2 1.1 broadcast_multiply_fusion.2
  709.1 1.2 fusion.38
  710.4 1.6 copy.97
  712.0 5.1 multiply_subtract_fusion.3
  717.1 1.6 copy.104
  719.0 1.2 copy.86
  720.2 1.5 reshape.264
  721.8 2.9 multiply_subtract_fusion.7
  724.7 1.6 copy.105
  726.3 1.6 copy.106
  728.0 3.4 multiply_subtract_fusion.6
  731.4 2.4 multiply_subtract_fusion.5
  735.0 2.4 multiply_subtract_fusion.4
  737.4 1.4 copy-done.3
  739.5 4.7 multiply_subtract_fusion
  745.0 4.1 multiply_subtract_fusion.1
  749.1 1.2 copy-done.29
  750.4 4.2 multiply_subtract_fusion.2
  (137 shorter events, 21.5 us)
Async XLA Ops:
  0.7 8.7 %copy-start.14 = (f32[3,3,64,512]{3,2,1,0:T(8,128)S(1)}, f32[3,3,64,512]{3,2,1,0:T(8,128)}, u32[]{:S(2)}) copy-start(f32[3,3,64,512]{3,2,1,0:T(8,128)} %param.39) | copy-start | bytes 3538948
  6.9 3.4 copy-start.16
  12.5 1.8 copy-start.6
  14.3 2.0 copy-start.4
  16.2 2.0 copy-start.1
  18.3 1.8 copy-start.32
  22.0 3.1 copy-start.33
  662.6 4.1 copy-start.20
  666.8 4.0 copy-start.11
  667.8 3.9 copy-start.10
  670.8 1.8 copy-start.51
  670.8 3.7 copy-start.45
  670.8 7.2 copy-start.41
  699.1 4.5 copy-start
  705.2 1.8 copy-start.43
  705.2 1.8 copy-start.44
  705.2 1.8 copy-start.46
  705.2 1.8 copy-start.47
  705.2 3.9 copy-start.25
  706.3 3.9 copy-start.21
  717.1 1.6 copy-start.30
  717.1 1.6 copy-start.31
  720.2 1.5 copy-start.39
  721.7 2.9 copy-start.9
  724.7 1.6 copy-start.8
  726.3 1.6 copy-start.22
  726.3 1.6 copy-start.34
  727.9 3.4 copy-start.13
  727.9 3.4 copy-start.15
  727.9 3.4 copy-start.35
  727.9 3.4 copy-start.36
  731.3 2.5 copy-start.12
  731.3 2.5 copy-start.17
  731.4 3.2 copy-start.37
  731.4 3.6 copy-start.38
  731.4 6.0 copy-start.24
  735.0 2.4 copy-start.2
  735.0 3.8 copy-start.3
  735.0 4.5 copy-start.23
  739.5 4.7 copy-start.5
  739.5 4.7 copy-start.18
  739.5 4.7 copy-start.26
  739.5 5.5 copy-start.27
  745.0 4.1 copy-start.7
  745.0 4.1 copy-start.19
  745.0 4.1 copy-start.28
  745.0 5.4 copy-start.29
  750.4 4.2 copy-start.42
  (4 other events, 4.8 us)

commit v3 on v2

--- a/solution.py
+++ b/solution.py
@@ -178,6 +178,23 @@
     return jnp.stack(tap_list).reshape(3, 3, inputs.shape[3], upstream.shape[3])
 
 
+def learn_rates():
+    conv_rate = LR_SCALE * (9 * C) ** (-0.5)
+    mod_rate = LR_SCALE * (4 * FREQ) ** (-0.5)
+    return (
+        LR_NORM,
+        conv_rate,
+        mod_rate,
+        conv_rate,
+        conv_rate,
+        mod_rate,
+        LR_SCALE * D ** (-0.5),
+        LR_SCALE * (HEADS * HDIM // 32) ** (-0.5),
+        LR_SCALE * D ** (-0.5),
+        LR_SCALE * FF ** (-0.5),
+    )
+
+
 def clipped_step(masters, averages, squares, combined_total, sum_all):
     local_sq = jnp.zeros((), jnp.float32)
     for position, reduced in enumerate(combined_total):
@@ -188,20 +205,7 @@
     square_sum = sum_all(local_sq)
     grad_norm = jnp.sqrt(square_sum)
     factor = jnp.minimum(1.0, CLIP / (grad_norm + 1e-06))
-    conv_rate = LR_SCALE * (9 * C) ** (-0.5)
-    mod_rate = LR_SCALE * (4 * FREQ) ** (-0.5)
-    rates = (
-        LR_NORM,
-        conv_rate,
-        mod_rate,
-        conv_rate,
-        conv_rate,
-        mod_rate,
-        LR_SCALE * D ** (-0.5),
-        LR_SCALE * (HEADS * HDIM // 32) ** (-0.5),
-        LR_SCALE * D ** (-0.5),
-        LR_SCALE * FF ** (-0.5),
-    )
+    rates = learn_rates()
     correct_one = 1.0 - BETA_ONE**STEP
     correct_two = 1.0 - BETA_TWO**STEP
     results = []
@@ -583,532 +587,6 @@
     )
 
 
-def gather_kernel(wide, both, block_ref, out_ref, send_sem, recv_sem, own_sem):
-    at = Place(wide)
-
-    def here(slot):
-        return out_ref.at[slot, at.core] if both else out_ref.at[slot]
-
-    def copy(sem, source, slot, mate):
-        return pltpu.make_async_remote_copy(
-            src_ref=source,
-            dst_ref=here(slot),
-            send_sem=send_sem.at[sem],
-            recv_sem=recv_sem.at[sem],
-            device_id=(mate, at.core),
-            device_id_type=MESH,
-        )
-
-    def mirror(slot, source):
-        return pltpu.make_async_remote_copy(
-            src_ref=source,
-            dst_ref=here(slot),
-            send_sem=send_sem.at[18 + slot],
-            recv_sem=recv_sem.at[18 + slot],
-            device_id=(at.dp, 1 - at.core),
-            device_id_type=MESH,
-        )
-
-    at.greet(both)
-    keep = pltpu.make_async_copy(block_ref, here(at.slot), own_sem)
-    keep.start()
-
-    def place(layer, column):
-        return layer * at.stride + column
-
-    def spread(layer, source):
-        slot = place(layer, at.column)
-        if wide:
-            copy(6 + layer, source, slot, at.first).start()
-        copy(10 + layer, source, slot, at.second).start()
-        if both:
-            mirror(slot, source).start()
-
-    def up(distance, source):
-        return copy(distance, source, place(at.z - distance, at.column), at.dp + 4)
-
-    def down(distance, source):
-        return copy(3 + distance, source, place(at.z + distance, at.column), at.dp - 4)
-
-    pl.when(at.has_above)(lambda: up(0, block_ref).start())
-    pl.when(at.has_below)(lambda: down(0, block_ref).start())
-    spread(at.z, block_ref)
-
-    def onward(layer):
-        slot = place(layer, at.first_column)
-        copy(6 + layer, here(slot), slot, at.first).wait_recv()
-        copy(14 + layer, here(slot), slot, at.second).start()
-        if both:
-            mirror(slot, here(slot)).start()
-
-    for distance in range(1, LAYERS):
-        below, above = at.z - distance, at.z + distance
-
-        @pl.when(below >= 0)
-        def _():
-            slot = place(below, at.column)
-            copy(distance - 1, here(slot), slot, at.dp).wait_recv()
-            if distance < LAYERS - 1:
-                pl.when(at.has_above)(lambda: up(distance, here(slot)).start())
-            spread(below, here(slot))
-
-        @pl.when(above < LAYERS)
-        def _():
-            slot = place(above, at.column)
-            copy(3 + distance - 1, here(slot), slot, at.dp).wait_recv()
-            if distance < LAYERS - 1:
-                pl.when(at.has_below)(lambda: down(distance, here(slot)).start())
-            spread(above, here(slot))
-
-        if not wide:
-            continue
-        if distance == 1:
-            onward(at.z)
-        else:
-            pl.when(at.z - distance + 1 >= 0)(lambda: onward(at.z - distance + 1))
-            pl.when(at.z + distance - 1 < LAYERS)(lambda: onward(at.z + distance - 1))
-    if wide:
-        pl.when(at.z == LAYERS - 1)(lambda: onward(0))
-        pl.when(at.z == 0)(lambda: onward(LAYERS - 1))
-
-    keep.wait()
-    own = here(at.slot)
-    for layer in range(LAYERS):
-        arriving = [(10, at.second_column)]
-        if wide:
-            arriving.append((14, at.far_column))
-        for sem, column in arriving:
-            slot = place(layer, column)
-            copy(sem + layer, own, slot, at.second).wait_recv()
-            if both:
-                mirror(slot, here(slot)).start()
-    if both:
-        for slot in range(at.stride * LAYERS):
-            pltpu.make_async_remote_copy(
-                src_ref=own,
-                dst_ref=out_ref.at[slot, 1 - at.core],
-                send_sem=send_sem.at[18 + slot],
-                recv_sem=recv_sem.at[18 + slot],
-                device_id=(at.dp, 1 - at.core),
-                device_id_type=MESH,
-            ).wait_recv()
-            mirror(slot, own).wait_send()
-    for sem in range(6, 18) if wide else range(10, 14):
-        copy(sem, own, at.slot, at.second).wait_send()
-    for distance in range(LAYERS - 1):
-
-        @pl.when(jnp.logical_and(at.has_above, at.z - distance >= 0))
-        def _():
-            up(distance, own).wait_send()
-
-        @pl.when(jnp.logical_and(at.has_below, at.z + distance < LAYERS))
-        def _():
-            down(distance, own).wait_send()
-
-
-def gather(number, block, wide=True, both=False):
-    chips = 16 if wide else 8
-    shape = (chips,) + ((2,) if both else ()) + block.shape
-    count = 18 + both * chips
-    return pl.pallas_call(
-        functools.partial(gather_kernel, wide, both),
-        out_shape=jax.ShapeDtypeStruct(shape, block.dtype),
-        in_specs=[ANYWHERE],
-        out_specs=ANYWHERE,
-        scratch_shapes=[
-            pltpu.SemaphoreType.DMA((count,)),
-            pltpu.SemaphoreType.DMA((count,)),
-            pltpu.SemaphoreType.DMA,
-        ],
-        compiler_params=params(number),
-        name=f"gather_{chips}" + ("_both" if both else ""),
-    )(block)
-
-
-def reduce_kernel(wide, pair, share, in_ref, out_ref, *scratch):
-    if pair:
-        *scratch, paired, pair_send, pair_recv = scratch
-    own, from_second, from_first, from_z, send_sem, recv_sem, own_sem = scratch
-    at = Place(wide)
-
-    def copy(sem, source, target, mate):
-        return pltpu.make_async_remote_copy(
-            src_ref=source,
-            dst_ref=target,
-            send_sem=send_sem.at[sem],
-            recv_sem=recv_sem.at[sem],
-            device_id=(mate, at.core),
-            device_id_type=MESH,
-        )
-
-    def place(layer, column):
-        return layer * at.stride + column
-
-    def load(slot):
-        source = in_ref.at[slot, at.core] if pair else in_ref.at[slot]
-        return pltpu.make_async_copy(source, own.at[slot], own_sem.at[slot])
-
-    def to_mate(slot):
-        return pltpu.make_async_remote_copy(
-            src_ref=in_ref.at[slot, 1 - at.core],
-            dst_ref=paired.at[slot],
-            send_sem=pair_send.at[slot],
-            recv_sem=pair_recv.at[slot],
-            device_id=(at.dp, 1 - at.core),
-            device_id_type=MESH,
-        )
-
-    def to_second(half, layer):
-        column = at.far_column if half == 0 else at.second_column
-        source = own if pair else in_ref
-        return copy(
-            4 * half + layer,
-            source.at[place(layer, column)],
-            from_second.at[4 * half + layer],
-            at.second,
-        )
-
-    def first_slot(layer):
-        return place(layer, at.first_column)
-
-    def own_slot(layer):
-        return place(layer, at.column)
-
-    def to_first(layer):
-        return copy(8 + layer, own.at[first_slot(layer)], from_first.at[layer], at.first)
-
-    def up(layer):
-        return copy(12 + layer, own.at[own_slot(layer)], from_z.at[layer], at.dp + 4)
-
-    def down(layer):
-        return copy(16 + layer, own.at[own_slot(layer)], from_z.at[4 + layer], at.dp - 4)
-
-    def value(ref, index):
-        return ref[index].astype(jnp.float32)
-
-    def join(slot):
-        load(slot).wait()
-        to_mate(slot).wait_recv()
-        own[slot] = (value(own, slot) + value(paired, slot)).astype(own.dtype)
-
-    at.greet(pair or share)
-    halves = (0, 1) if wide else (1,)
-    for half in halves:
-        for layer in ORDER:
-            away = place(layer, at.far_column if half == 0 else at.second_column)
-            keep = first_slot(layer) if half == 0 else own_slot(layer)
-            if pair:
-                for slot in (away, keep):
-                    to_mate(slot).start()
-                    load(slot).start()
-            else:
-                to_second(half, layer).start()
-                load(keep).start()
-    if pair:
-        for half in halves:
-            for layer in ORDER:
-                join(place(layer, at.far_column if half == 0 else at.second_column))
-                to_second(half, layer).start()
-        for layer in ORDER:
-            if wide:
-                join(first_slot(layer))
-            join(own_slot(layer))
-
-    if wide:
-        for layer in ORDER:
-            slot = first_slot(layer)
-            if not pair:
-                load(slot).wait()
-            to_second(0, layer).wait_recv()
-            own[slot] = (value(own, slot) + value(from_second, layer)).astype(own.dtype)
-            to_first(layer).start()
-    result = out_ref.at[at.core] if share else out_ref
-    for layer in ORDER:
-        slot = own_slot(layer)
-        if not pair:
-            load(slot).wait()
-        to_second(1, layer).wait_recv()
-        total = value(own, slot) + value(from_second, 4 + layer)
-        if wide:
-            to_first(layer).wait_recv()
-            total = total + value(from_first, layer)
-        own[slot] = total.astype(own.dtype)
-
-        @pl.when(at.z < layer)
-        def _():
-            @pl.when(at.has_below)
-            def _():
-                up(layer).wait_recv()
-                own[slot] = (value(own, slot) + value(from_z, layer)).astype(own.dtype)
-
-            up(layer).start()
-
-        @pl.when(at.z > layer)
-        def _():
-            @pl.when(at.has_above)
-            def _():
-                down(layer).wait_recv()
-                own[slot] = (value(own, slot) + value(from_z, 4 + layer)).astype(own.dtype)
-
-            down(layer).start()
-
-        @pl.when(at.z == layer)
-        def _():
-            result[...] = total.astype(out_ref.dtype)
-
-    for layer in range(LAYERS):
-
-        @pl.when(at.z == layer)
-        def _():
-            @pl.when(at.has_below)
-            def _():
-                up(layer).wait_recv()
-                result[...] = (result[...].astype(jnp.float32) + value(from_z, layer)).astype(
-                    out_ref.dtype
-                )
-
-            @pl.when(at.has_above)
-            def _():
-                down(layer).wait_recv()
-                result[...] = (result[...].astype(jnp.float32) + value(from_z, 4 + layer)).astype(
-                    out_ref.dtype
-                )
-
-    if share:
-
-        def give(core):
-            return pltpu.make_async_remote_copy(
-                src_ref=result,
-                dst_ref=out_ref.at[core],
-                send_sem=send_sem.at[20],
-                recv_sem=recv_sem.at[20],
-                device_id=(at.dp, 1 - at.core),
-                device_id_type=MESH,
-            )
-
-        give(at.core).start()
-        give(1 - at.core).wait_recv()
-        give(at.core).wait_send()
-    if pair:
-        for slot in range(at.stride * LAYERS):
-            to_mate(slot).wait_send()
-    for layer in range(LAYERS):
-        for half in halves:
-            to_second(half, layer).wait_send()
-        if wide:
-            to_first(layer).wait_send()
-        pl.when(at.z < layer)(lambda: up(layer).wait_send())
-        pl.when(at.z > layer)(lambda: down(layer).wait_send())
-
-
-def reduce(number, blocks, wide=True, pair=False, share=False):
-    chips = 16 if wide else 8
-    block = blocks.shape[-2:]
-    kind = blocks.dtype
-    scratch = [
-        pltpu.VMEM((chips,) + block, kind),
-        pltpu.VMEM((8,) + block, kind),
-        pltpu.VMEM((4,) + block, kind),
-        pltpu.VMEM((8,) + block, kind),
-        pltpu.SemaphoreType.DMA((21,)),
-        pltpu.SemaphoreType.DMA((21,)),
-        pltpu.SemaphoreType.DMA((chips,)),
-    ]
-    if pair:
-        scratch += [
-            pltpu.VMEM((chips,) + block, kind),
-            pltpu.SemaphoreType.DMA((chips,)),
-            pltpu.SemaphoreType.DMA((chips,)),
-        ]
-    return pl.pallas_call(
-        functools.partial(reduce_kernel, wide, pair, share),
-        out_shape=jax.ShapeDtypeStruct(((2,) if share else ()) + block, jnp.float32),
-        in_specs=[ANYWHERE],
-        out_specs=IN_VMEM,
-        scratch_shapes=scratch,
-        compiler_params=params(number),
-        name=f"reduce_{chips}" + ("_pair" if pair else "") + ("_share" if share else ""),
-    )(blocks)
-
-
-def trade_kernel(count, *refs):
-    in_refs, out_refs = (refs[:count], refs[count : 2 * count])
-    send_sem, recv_sem, own_sem = refs[2 * count :]
-    dp, core = (lax.axis_index(DP), lax.axis_index(TENSOR))
-    others = 4 * LAYERS - 1
-    barrier = pltpu.get_barrier_semaphore()
-
-    def peer(step):
-        return (dp + step) % (4 * LAYERS)
-
-    @pl.loop(1, others + 1)
-    def _(step):
-        pl.semaphore_signal(barrier, inc=1, device_id=(peer(step), core), device_id_type=MESH)
-
-    pl.semaphore_wait(barrier, others)
-
-    def copy(index, step):
-        return pltpu.make_async_remote_copy(
-            src_ref=in_refs[index].at[peer(step)],
-            dst_ref=out_refs[index].at[dp],
-            send_sem=send_sem.at[index, step - 1],
-            recv_sem=recv_sem.at[index, step - 1],
-            device_id=(peer(step), core),
-            device_id_type=MESH,
-        )
-
-    def keep(index):
-        return pltpu.make_async_copy(
-            in_refs[index].at[dp], out_refs[index].at[dp], own_sem.at[index]
-        )
-
-    for index in range(count):
-        keep(index).start()
-
-        @pl.loop(1, others + 1)
-        def _(step):
-            copy(index, step).start()
-
-    for index in range(count):
-        keep(index).wait()
-
-        @pl.loop(1, others + 1)
-        def _(step):
-            copy(index, step).wait()
-
-
-def trade(number, *blocks):
-    count = len(blocks)
-    return pl.pallas_call(
-        functools.partial(trade_kernel, count),
-        out_shape=[jax.ShapeDtypeStruct(b.shape, b.dtype) for b in blocks],
-        in_specs=[ANYWHERE] * count,
-        out_specs=[ANYWHERE] * count,
-        scratch_shapes=[
-            pltpu.SemaphoreType.DMA((count, 15)),
-            pltpu.SemaphoreType.DMA((count, 15)),
-            pltpu.SemaphoreType.DMA((count,)),
-        ],
-        compiler_params=params(number),
-        name="trade",
-    )(*blocks)
-
-
-def add_core_kernel(pieces, in_ref, out_ref, theirs, send_sem, recv_sem):
-    dp, core = (lax.axis_index(DP), lax.axis_index(TENSOR))
-    barrier = pltpu.get_barrier_semaphore()
-    pl.semaphore_signal(barrier, inc=1, device_id=(dp, 1 - core), device_id_type=MESH)
-    pl.semaphore_wait(barrier, 1)
-    rows = in_ref.shape[0] // pieces
-
-    def copy(piece):
-        at = pl.ds(piece * rows, rows)
-        return pltpu.make_async_remote_copy(
-            src_ref=in_ref.at[at],
-            dst_ref=theirs.at[at],
-            send_sem=send_sem.at[piece],
-            recv_sem=recv_sem.at[piece],
-            device_id=(dp, 1 - core),
-            device_id_type=MESH,
-        )
-
-    for piece in range(pieces):
-        copy(piece).start()
-    for piece in range(pieces):
-        at = pl.ds(piece * rows, rows)
-        copy(piece).wait_recv()
-        out_ref[at] = in_ref[at].astype(jnp.float32) + theirs[at].astype(jnp.float32)
-    for piece in range(pieces):
-        copy(piece).wait_send()
-
-
-def add_core(number, block):
-    pieces = 4
-    return pl.pallas_call(
-        functools.partial(add_core_kernel, pieces),
-        out_shape=jax.ShapeDtypeStruct(block.shape, jnp.float32),
-        in_specs=[IN_VMEM],
-        out_specs=IN_VMEM,
-        scratch_shapes=[
-            pltpu.VMEM(block.shape, block.dtype),
-            pltpu.SemaphoreType.DMA((pieces,)),
-            pltpu.SemaphoreType.DMA((pieces,)),
-        ],
-        compiler_params=params(number),
-        name="add_core",
-    )(block)
-
-
-def total_kernel(in_ref, out_ref, tiles, held, send_sem, recv_sem):
-    dp, core = (lax.axis_index(DP), lax.axis_index(TENSOR))
-    others = 4 * LAYERS - 1
-    barrier = pltpu.get_barrier_semaphore()
-
-    def peer(step):
-        return (dp + step) % (4 * LAYERS)
-
-    pl.semaphore_signal(barrier, inc=1, device_id=(dp, 1 - core), device_id_type=MESH)
-
-    @pl.loop(1, others + 1)
-    def _(step):
-        pl.semaphore_signal(barrier, inc=1, device_id=(peer(step), core), device_id_type=MESH)
-
-    pl.semaphore_wait(barrier, others + 1)
-    across = pltpu.make_async_remote_copy(
-        src_ref=in_ref,
-        dst_ref=tiles.at[0],
-        send_sem=send_sem.at[0],
-        recv_sem=recv_sem.at[0],
-        device_id=(dp, 1 - core),
-        device_id_type=MESH,
-    )
-    across.start()
-    across.wait()
-    held[...] = in_ref[...] + tiles[0]
-
-    def copy(step):
-        return pltpu.make_async_remote_copy(
-            src_ref=held,
-            dst_ref=tiles.at[step],
-            send_sem=send_sem.at[step],
-            recv_sem=recv_sem.at[step],
-            device_id=(peer(step), core),
-            device_id_type=MESH,
-        )
-
-    @pl.loop(1, others + 1)
-    def _(step):
-        copy(step).start()
-
-    @pl.loop(1, others + 1)
-    def _(step):
-        copy(step).wait()
-
-    total = jnp.zeros_like(held)
-    for chip in range(4 * LAYERS):
-        step = (dp - chip + 4 * LAYERS) % (4 * LAYERS)
-        part = jnp.where(step == 0, held[...], tiles[step])
-        total = total + part
-    out_ref[...] = total
-
-
-def total(number, tile):
-    return pl.pallas_call(
-        total_kernel,
-        out_shape=jax.ShapeDtypeStruct(tile.shape, tile.dtype),
-        in_specs=[IN_VMEM],
-        out_specs=IN_VMEM,
-        scratch_shapes=[
-            pltpu.VMEM((16,) + tile.shape, tile.dtype),
-            pltpu.VMEM(tile.shape, tile.dtype),
-            pltpu.SemaphoreType.DMA((16,)),
-            pltpu.SemaphoreType.DMA((16,)),
-        ],
-        compiler_params=params(number),
-        name="total",
-    )(tile)
-
-
 def layer_order(step):
     odd = step % 2
     return (1 - odd) * (LAYERS - 1 - step // 2) + odd * (step // 2)
@@ -1140,7 +618,7 @@
     return block.at[:, pl.ds(pl.multiple_of(index * (lanes // pieces), lanes // pieces), lanes // pieces)]
 
 
-def gather_stage(at, outs, use, pieces, send_sem, recv_sem, mirror=None):
+def gather_steps(at, outs, use, pieces, send_sem, recv_sem, mirror=None, tick=None):
     columns = at.stride
     arrays = range(len(outs))
 
@@ -1176,8 +654,7 @@
                 )
             )
 
-    @pl.loop(0, columns * LAYERS * pieces)
-    def _(count):
+    def turn(count):
         step, piece = (count // pieces, count % pieces)
         if at.wide:
             late = step // 8
@@ -1224,34 +701,45 @@
 
         if mirror:
             across(slot, piece, start, at.core)
+        if tick is not None:
+            tick(count)
         if use is not None:
             pl.when(piece == pieces - 1)(lambda: use(slot))
 
     def sent(copy):
         copy.wait_send()
 
-    @pl.loop(0, LAYERS * pieces)
-    def _(count):
-        layer, piece = (count // pieces, count % pieces)
-
-        @pl.when(jnp.logical_and(layer <= at.z, at.has_above))
-        def _():
-            each(at.slot, piece, layer, at.dp + 4, sent)
-
-        @pl.when(jnp.logical_and(layer >= at.z, at.has_below))
-        def _():
-            each(at.slot, piece, 4 + layer, at.dp - 4, sent)
-
-        for group in (8, 12, 16) if at.wide else (12,):
-            each(at.slot, piece, group + layer, at.second, sent)
-
-    if mirror:
-
-        @pl.loop(0, columns * LAYERS * pieces)
+    def end():
+        @pl.loop(0, LAYERS * pieces)
         def _(count):
-            slot, piece = (count // pieces, count % pieces)
-            across(slot, piece, lambda copy: copy.wait_recv(), 1 - at.core)
-            across(slot, piece, sent, at.core)
+            layer, piece = (count // pieces, count % pieces)
+
+            @pl.when(jnp.logical_and(layer <= at.z, at.has_above))
+            def _():
+                each(at.slot, piece, layer, at.dp + 4, sent)
+
+            @pl.when(jnp.logical_and(layer >= at.z, at.has_below))
+            def _():
+                each(at.slot, piece, 4 + layer, at.dp - 4, sent)
+
+            for group in (8, 12, 16) if at.wide else (12,):
+                each(at.slot, piece, group + layer, at.second, sent)
+
+        if mirror:
+
+            @pl.loop(0, columns * LAYERS * pieces)
+            def _(count):
+                slot, piece = (count // pieces, count % pieces)
+                across(slot, piece, lambda copy: copy.wait_recv(), 1 - at.core)
+                across(slot, piece, sent, at.core)
+
+    return turn, columns * LAYERS * pieces, end
+
+
+def gather_stage(*args, **options):
+    turn, turns, end = gather_steps(*args, **options)
+    pl.loop(0, turns)(turn)
+    end()
 
 
 def gather_scratch(pieces, arrays=1, wide=True, mirror=False):
@@ -1260,7 +748,7 @@
     return [pltpu.SemaphoreType.DMA((arrays, n)) for n in count]
 
 
-def reduce_stage(at, result, produce, pieces, scratch, pair=False, meanwhile=None):
+def reduce_stage(at, result, produce, pieces, scratch, pair=False, meanwhile=None, tick=None):
     blocks, from_second, from_first, from_z, send_sem, recv_sem, *scratch = scratch
     columns = at.stride
     whole = columns * LAYERS
@@ -1412,6 +900,8 @@
         if at.wide:
             pl.when(place < LAYERS)(lambda: turn(place, piece))
         pl.when(place >= behind)(lambda: rise(place - behind, piece))
+        if tick is not None:
+            tick(step)
 
     @pl.loop(0, pieces)
     def _(piece):
@@ -1684,6 +1174,7 @@
     out_head,
     up_here,
     down_here,
+    neighbour_sem,
     arrived,
     mods_blocks,
     mods_terms,
@@ -1708,7 +1199,7 @@
         at,
         [
             (lambda chip: emb_blocks.at[chip], lambda chip: emb.at[chip]),
-            (lambda chip: image_blocks.at[chip], lambda chip: arrived.at[chip]),
+            (lambda chip: image_blocks.at[chip, at.core], lambda chip: arrived.at[chip, at.core]),
             (lambda chip: strip(up_rows, 1, chip, cols), lambda chip: strip(up_here, 0, chip, rows)),
             (lambda chip: mods_blocks.at[chip], lambda chip: mods_terms.at[chip]),
             (lambda chip: strip(down_columns, 0, chip, cols), lambda chip: strip(down_here, 1, chip, rows)),
@@ -1728,20 +1219,27 @@
     half_c = conv_one.shape[2]
     tokens_len = positions // 4
 
-    ride.wait_for(0)
-    emb_rows = emb[:, 0, : res_table.shape[0]].astype(jnp.bfloat16)
-    lines = 0
-    for table in (res_table, ada_table):
-        terms = dot(emb_rows, table[...])
-        for line in range(table.shape[1] // 128):
-            mods_blocks[:, lines] = terms[:, 128 * line : 128 * (line + 1)]
-            lines += 1
-    ride.start(3, 4)
-    ride.wait_for(1)
+    def hand_over(chip, core):
+        return remote(
+            arrived.at[chip, core],
+            arrived.at[chip, core],
+            neighbour_sem.at[0, chip],
+            neighbour_sem.at[1, chip],
+            (at.dp, 1 - at.core),
+        )
+
+    ride.keep(1).wait()
+    hand_over(at.dp, at.core).start()
+
+    @pl.loop(1, images)
+    def _(step):
+        ride.copy(1, step).wait()
+        hand_over((at.dp + images - step) % images, at.core).start()
 
     @pl.loop(0, images)
     def _(i):
-        both = arrived[i].astype(jnp.float32)
+        hand_over(i, 1 - at.core).wait_recv()
+        both = arrived[i].reshape(positions // 2, 2 * channels).astype(jnp.float32)
         sides = [both[:, :channels], both[:, channels:]]
         pictures[i] = jnp.concatenate(sides, axis=0).astype(jnp.bfloat16)
 
@@ -1776,11 +1274,22 @@
             total += dot(taps_one[slot, pl.ds(a * breadth, positions)], conv_one[a])
         first_reduce[0][slot] = total.astype(jnp.bfloat16)
 
-    reduce_stage(at, middle, first_product, 4, first_reduce)
+    def modulation_terms():
+        ride.wait_for(0)
+        emb_rows = emb[:, 0, : res_table.shape[0]].astype(jnp.bfloat16)
+        lines = 0
+        for table in [res_table] + [ada_table.at[row] for row in range(ada_table.shape[0])]:
+            terms = dot(emb_rows, table[...])
+            for line in range(table.shape[1] // 128):
+                mods_blocks[:, lines] = terms[:, 128 * line : 128 * (line + 1)].astype(mods_blocks.dtype)
+                lines += 1
+        ride.start(3, 4)
+
+    reduce_stage(at, middle, first_product, 2, first_reduce, meanwhile=modulation_terms)
 
     ride.start(4, 5)
     ride.wait_for(3)
-    mods[at.core] = jnp.sum(mods_terms[...], axis=0)
+    mods[at.core] = jnp.sum(mods_terms[...].astype(jnp.float32), axis=0)
     share_stage(at, mods, share_send.at[1], share_recv.at[1])
 
     def modulation(row):
@@ -1805,12 +1314,12 @@
 
     def second_product(slot):
         act = acts[slot]
-        above, same, below = (dot(act, conv_two[a]) for a in range(3))
+        above, same, below = (dot_nt(act, conv_two[a]) for a in range(3))
         folded = fold_three(fold_rows(above, same, below, breadth), breadth)
         mine[slot] = folded.astype(jnp.bfloat16)
         swap(slot).start()
 
-    gather_stage(at, [acts], second_product, 4, act_send, act_recv)
+    gather_stage(at, [acts], second_product, 2, act_send, act_recv)
     save_acts = pltpu.make_async_copy(acts, act_out, out_sem.at[1])
     save_acts.start()
     attention.forward()
@@ -1828,12 +1337,13 @@
             total += dot(part, conv_half[a])
         last_reduce[0][slot] = total.astype(jnp.bfloat16)
 
-    reduce_stage(at, tokens.at[at.core], half_product, 4, last_reduce)
+    reduce_stage(at, tokens.at[at.core], half_product, 2, last_reduce)
     share_stage(at, tokens, share_send.at[0], share_recv.at[0])
 
     @pl.loop(0, images)
     def _(slot):
         swap(slot).wait_send()
+        hand_over(slot, at.core).wait_send()
 
     ride.wait_for(2)
     ride.wait_for(4)
@@ -1854,7 +1364,7 @@
     pictures = (images, positions, channels)
     padded = (images, positions + 2 * breadth, three)
     acts = (images, positions, half_c)
-    lines = (res_table.shape[1] + ada_table.shape[1]) // 128
+    lines = (res_table.shape[1] + ada_table.shape[0] * ada_table.shape[2]) // 128
     outs = [
         (pictures, low),
         (emb_blocks.shape, full),
@@ -1876,9 +1386,10 @@
         in_specs=[IN_VMEM] * 7 + [ANYWHERE] * 6,
         out_specs=[IN_VMEM] * 3 + [ANYWHERE] * 2 + [IN_VMEM] * 4 + [ANYWHERE] * 4,
         scratch_shapes=[
+            pltpu.SemaphoreType.DMA((2, images)),
             pltpu.VMEM(image_blocks.shape, low),
-            pltpu.VMEM((images, lines, 128), full),
-            pltpu.VMEM((images, lines, 128), full),
+            pltpu.VMEM((images, lines, 128), low),
+            pltpu.VMEM((images, lines, 128), low),
             pltpu.VMEM(acts, low),
             pltpu.VMEM(padded, low),
             pltpu.VMEM(pictures, low),
@@ -1889,9 +1400,9 @@
             pltpu.SemaphoreType.DMA((2,)),
             pltpu.SemaphoreType.DMA((2,)),
         ]
-        + reduce_scratch((positions, half_c), 4)
-        + gather_scratch(4)
-        + reduce_scratch((tokens_len, half_d), 4)
+        + reduce_scratch((positions, half_c), 2)
+        + gather_scratch(2)
+        + reduce_scratch((tokens_len, half_d), 2)
         + ride_scratch(5)
         + pair_ride_scratch(2),
         compiler_params=params(number),
@@ -1976,7 +1487,7 @@
     load_taps = pltpu.make_async_copy(taps_one_in, taps_one, io_sem.at[1])
     load_acts.start()
     load_taps.start()
-    gathered[at.slot] = shrunk[at.core]
+    gathered[at.slot] = shrunk[...]
 
     greet_all(at)
 
@@ -2071,7 +1582,7 @@
         mine[slot] = fold_three(spread, breadth, True).astype(jnp.bfloat16)
         swap(slot).start()
 
-    gather_stage(at, [gathered], half_back, 4, shrunk_send, shrunk_recv)
+    gather_stage(at, [gathered], half_back, 2, shrunk_send, shrunk_recv)
 
     store_sums()
 
@@ -2082,9 +1593,9 @@
         swap(slot).wait_recv()
         branch = resid(slot).astype(jnp.bfloat16).astype(jnp.float32)
         store_padded(taps_two, slot, side_by_side(branch, breadth, True), breadth)
-        total = jnp.zeros((positions, conv_two.shape[1]), jnp.float32)
+        total = jnp.zeros((positions, conv_two.shape[2]), jnp.float32)
         for a in range(3):
-            total += dot_nt(taps_two[slot, pl.ds((2 - a) * breadth, positions)], conv_two[a])
+            total += dot(taps_two[slot, pl.ds((2 - a) * breadth, positions)], conv_two[a])
         reducing[0][slot] = total.astype(jnp.bfloat16)
 
     def weights_meanwhile():
@@ -2112,7 +1623,7 @@
     def save(source, target, sem):
         return pltpu.make_async_copy(source, target, io_sem.at[sem])
 
-    reduce_stage(at, acted, second_back, 4, reducing, False, weights_meanwhile)
+    reduce_stage(at, acted, second_back, 2, reducing, False, weights_meanwhile)
 
     x = middle[...]
     center = mean_of_groups(jnp.sum(x, axis=0, keepdims=True), positions)
@@ -2148,7 +1659,7 @@
         back[slot] = folded.astype(jnp.bfloat16)
         swap_back(slot).start()
 
-    gather_stage(at, [gathered_middle], first_back, 4, middle_send, middle_recv)
+    gather_stage(at, [gathered_middle], first_back, 2, middle_send, middle_recv)
 
     gain, bias = (gain_bias[0:1], gain_bias[1:2])
 
@@ -2281,9 +1792,9 @@
         + [pltpu.SemaphoreType.DMA((images - 1,))] * 2
         + [pltpu.SemaphoreType.DMA((6,)), pltpu.SemaphoreType.DMA((2,))]
         + [pltpu.SemaphoreType.DMA((2, 2, images // 2))] * 2
-        + gather_scratch(4)
-        + gather_scratch(4)
-        + reduce_scratch((positions, half_c), 4)
+        + gather_scratch(2)
+        + gather_scratch(2)
+        + reduce_scratch((positions, half_c), 2)
         + ride_scratch(3),
         compiler_params=params(number),
         name="res_backward",
@@ -2317,7 +1828,10 @@
     up_grad,
     down_back,
     tokens,
-    held,
+    own_out,
+    outgoing,
+    mods_part,
+    mods_theirs,
     attn_in,
     qkv,
     probs,
@@ -2346,7 +1860,7 @@
         del scratch[:count]
         return taken
 
-    gather_one, gather_two, gather_three = (take(4), take(4), take(4))
+    gather_one, gather_two, gather_three, gather_four = (take(4), take(4), take(4), take(4))
     reduce_one, reduce_two, reduce_three, reduce_four = (take(10), take(10), take(10), take(10))
     ride_back = take(3)
     at, near = (Place(True), Place(False))
@@ -2358,25 +1872,37 @@
     score_scale = HDIM ** (-0.5)
     low, full = (jnp.bfloat16, jnp.float32)
     mine = pl.ds(pl.multiple_of(at.core * half, half), half)
-    theirs = pl.ds(pl.multiple_of((1 - at.core) * half, half), half)
-
-    def own_rows(value, out):
-        held[...] = value.astype(low)
-        out[...] = held[mine]
 
     def split(place, value, stage):
-        held[...] = value.astype(low)
-        stage[0][place] = held[mine]
-        stage[6][place] = held[theirs]
+        value = value.astype(low)
+        for core in range(2):
+
+            @pl.when(at.core == core)
+            def _():
+                stage[0][place] = value[core * half : (core + 1) * half]
+                stage[6][place] = value[(1 - core) * half : (2 - core) * half]
 
     def image_rows(i):
         return pl.ds(pl.multiple_of(i * tokens_len, tokens_len), tokens_len)
 
-    tokens[:, : shrunk.shape[2]] = shrunk[0]
-    tokens[:, shrunk.shape[2] :] = shrunk[1]
+    width = shrunk.shape[2]
+    tokens[:, :width] = shrunk[0, mine]
+    tokens[:, width:] = shrunk[1, mine]
     normed, _ = layer_stats(tokens[...])
-    own_rows(normed * (1.0 + mods[1:2]) + mods[0:1], attn_in.at[near.slot, near.core])
-    gather_stage(near, [attn_in], None, 4, *gather_one[:2], gather_one[2:])
+    attn_in[near.slot, near.core] = (normed * (1.0 + mods[1:2]) + mods[0:1]).astype(low)
+    upstream = cotangent[mine].astype(full)
+    expanded_grad[at.slot, at.core] = ((1.0 + mods[5:6]) * upstream).astype(low)
+    grad_turn, _, grad_end = gather_steps(
+        at, [expanded_grad], None, 1, *gather_four[:2], gather_four[2:]
+    )
+
+    def in_gather(count):
+        pl.when(count % 2 == 0)(lambda: grad_turn(count // 2))
+
+    def in_sum(count):
+        grad_turn(8 + count)
+
+    gather_stage(near, [attn_in], None, 2, *gather_one[:2], gather_one[2:], tick=in_gather)
 
     @pl.loop(0, images // 2)
     def _(i):
@@ -2394,19 +1920,13 @@
     def attention_term(place):
         split(place, dot(mixed[image_rows(place)], out_head[...]), reduce_one)
 
-    reduce_stage(near, attended.at[at.core], attention_term, 4, reduce_one, True)
-    share_stage(at, attended, share_send.at[0], share_recv.at[0])
-
-    def whole(ref):
-        return ref[...].reshape(tokens_len, D)
-
-    after = tokens[...] + (1.0 + mods[2:3]) * whole(attended)
+    reduce_stage(near, attended, attention_term, 2, reduce_one, True, tick=in_sum)
+    grad_end()
+
+    after = tokens[...] + (1.0 + mods[2:3]) * attended[...]
     normed, _ = layer_stats(after)
-    own_rows(normed * (1.0 + mods[4:5]) + mods[3:4], mlp_in.at[at.slot, at.core])
-    own_rows(
-        (1.0 + mods[5:6]) * cotangent[...].astype(full), expanded_grad.at[at.slot, at.core]
-    )
-    gather_stage(at, [mlp_in, expanded_grad], None, 4, *gather_two[:2], gather_two[2:])
+    mlp_in[at.slot, at.core] = (normed * (1.0 + mods[4:5]) + mods[3:4]).astype(low)
+    gather_stage(at, [mlp_in], None, 2, *gather_two[:2], gather_two[2:])
 
     @pl.loop(0, LAYERS)
     def _(i):
@@ -2433,7 +1953,7 @@
             right = mlp_in[:, :, :, here].reshape(images * tokens_len, 512)
             up_grad[here] = dot_tn(right, pre_grad[...]).astype(low)
 
-    reduce_stage(at, expanded.at[at.core], hidden_term, 4, reduce_two, True, hidden_grads)
+    reduce_stage(at, expanded, hidden_term, 2, reduce_two, True, hidden_grads)
     back = Ride(
         at,
         [
@@ -2442,27 +1962,33 @@
         *ride_back,
     )
     back.start()
-    share_stage(at, expanded, share_send.at[1], share_recv.at[1])
-    block_out[...] = (after + (1.0 + mods[5:6]) * whole(expanded)).astype(low)
-    upstream = cotangent[...].astype(full)
-    mods_grad[5:6] = jnp.sum(upstream * whole(expanded), axis=0, keepdims=True)
+    own_out[...] = (after + (1.0 + mods[5:6]) * expanded[...]).astype(low)
+    block_out[mine] = own_out[...]
+    mods_part[5:6] = jnp.sum(upstream * expanded[...], axis=0, keepdims=True)
+
+    def exchange(index, source, target):
+        return remote(
+            source, target, share_send.at[index], share_recv.at[index], (at.dp, 1 - at.core)
+        )
+
+    give_out = exchange(0, own_out, block_out.at[mine])
+    give_out.start()
 
     def mlp_term(place):
         split(place, dot_nt(pre_grad[image_rows(place)], up_here[...]), reduce_three)
 
-    reduce_stage(at, mlp_grad.at[at.core], mlp_term, 4, reduce_three, True)
-    share_stage(at, mlp_grad, share_send.at[2], share_recv.at[2])
-    after = tokens[...] + (1.0 + mods[2:3]) * whole(attended)
+    reduce_stage(at, mlp_grad, mlp_term, 2, reduce_three, True)
+    after = tokens[...] + (1.0 + mods[2:3]) * attended[...]
     normed, scale = layer_stats(after)
-    grad = whole(mlp_grad)
-    mods_grad[3:4] = jnp.sum(grad, axis=0, keepdims=True)
-    mods_grad[4:5] = jnp.sum(grad * normed, axis=0, keepdims=True)
-    grad_after = cotangent[...].astype(full) + layer_back(normed, scale, (1.0 + mods[4:5]) * grad)
-    mods_grad[2:3] = jnp.sum(grad_after * whole(attended), axis=0, keepdims=True)
-
-    own_rows((1.0 + mods[2:3]) * grad_after, attended_grad.at[near.slot, near.core])
-    attended[...] = grad_after.reshape(attended.shape)
-    gather_stage(near, [attended_grad], None, 4, *gather_three[:2], gather_three[2:])
+    grad = mlp_grad[...]
+    mods_part[3:4] = jnp.sum(grad, axis=0, keepdims=True)
+    mods_part[4:5] = jnp.sum(grad * normed, axis=0, keepdims=True)
+    grad_after = cotangent[mine].astype(full) + layer_back(normed, scale, (1.0 + mods[4:5]) * grad)
+    mods_part[2:3] = jnp.sum(grad_after * attended[...], axis=0, keepdims=True)
+
+    attended_grad[near.slot, near.core] = ((1.0 + mods[2:3]) * grad_after).astype(low)
+    attended[...] = grad_after
+    gather_stage(near, [attended_grad], None, 2, *gather_three[:2], gather_three[2:])
 
     @pl.loop(0, images // 2)
     def _(i):
@@ -2492,15 +2018,27 @@
             left = attn_in[:, :, :, here].reshape(images // 2 * tokens_len, 512)
             qkv_grad[here] = dot_tn(left, qkv_back[...]).astype(low)
 
-    reduce_stage(near, attn_grad.at[at.core], qkv_term, 4, reduce_four, True, attention_grads)
-    share_stage(at, attn_grad, share_send.at[3], share_recv.at[3])
+    reduce_stage(near, attn_grad, qkv_term, 2, reduce_four, True, attention_grads)
     normed, scale = layer_stats(tokens[...])
-    grad = whole(attn_grad)
-    mods_grad[0:1] = jnp.sum(grad, axis=0, keepdims=True)
-    mods_grad[1:2] = jnp.sum(grad * normed, axis=0, keepdims=True)
-    grad = whole(attended) + layer_back(normed, scale, (1.0 + mods[1:2]) * grad)
-    token_grad[0] = grad[:, : shrunk.shape[2]].astype(low)
-    token_grad[1] = grad[:, shrunk.shape[2] :].astype(low)
+    grad = attn_grad[...]
+    mods_part[0:1] = jnp.sum(grad, axis=0, keepdims=True)
+    mods_part[1:2] = jnp.sum(grad * normed, axis=0, keepdims=True)
+    give_mods = exchange(1, mods_part, mods_theirs)
+    give_mods.start()
+
+    grad = (attended[...] + layer_back(normed, scale, (1.0 + mods[1:2]) * grad)).astype(low)
+    for core in range(2):
+
+        @pl.when(at.core == core)
+        def _():
+            token_grad[mine] = grad[:, core * width : (core + 1) * width]
+            outgoing[...] = grad[:, (1 - core) * width : (2 - core) * width]
+
+    give_tokens = exchange(2, outgoing, token_grad.at[mine])
+    give_tokens.start()
+    for give in (give_out, give_mods, give_tokens):
+        give.wait()
+    mods_grad[...] = mods_part[...] + mods_theirs[...]
     back.wait()
 
 
@@ -2514,31 +2052,34 @@
     both = (2, half, D)
     near_tokens = images // 2 * tokens_len
     vmem = [
-        ((tokens_len, D), full),
-        ((tokens_len, D), low),
+        ((half, D), full),
+        ((half, D), low),
+        ((half, shrunk.shape[2]), low),
+        (mods.shape, full),
+        (mods.shape, full),
         ((images // 2,) + both, low),
         ((near_tokens, 3 * HDIM), low),
         ((images // 2, tokens_len, tokens_len), full),
         ((near_tokens, HDIM), low),
-        (both, full),
+        ((half, D), full),
         ((images,) + both, low),
         ((images,) + both, low),
         ((images * tokens_len, cols), full),
         ((images * tokens_len, cols), low),
         ((images * tokens_len, cols), low),
-        (both, full),
-        (both, full),
+        ((half, D), full),
+        ((half, D), full),
         ((cols, D), low),
         ((images // 2,) + both, low),
         ((near_tokens, HDIM), low),
         ((near_tokens, 3 * HDIM), low),
-        (both, full),
+        ((half, D), full),
     ]
     return pl.pallas_call(
         transformer_kernel,
         out_shape=[
             jax.ShapeDtypeStruct((tokens_len, D), low),
-            jax.ShapeDtypeStruct(shrunk.shape, low),
+            jax.ShapeDtypeStruct(shrunk.shape[1:], low),
             jax.ShapeDtypeStruct(mods.shape, full),
             jax.ShapeDtypeStruct(qkv_head.shape, low),
             jax.ShapeDtypeStruct(out_head.shape, low),
@@ -2549,16 +2090,165 @@
         out_specs=[IN_VMEM] * 6 + [ANYWHERE],
         scratch_shapes=[pltpu.VMEM(shape, kind) for shape, kind in vmem]
         + [pltpu.SemaphoreType.DMA((4,))] * 2
-        + gather_scratch(4, 1, False, True)
-        + gather_scratch(4, 2, True, True)
-        + gather_scratch(4, 1, False, True)
-        + reduce_scratch((half, D), 4, False, True)
-        + reduce_scratch((half, D), 4, True, True) * 2
-        + reduce_scratch((half, D), 4, False, True)
+        + gather_scratch(2, 1, False, True)
+        + gather_scratch(2, 1, True, True)
+        + gather_scratch(2, 1, False, True)
+        + gather_scratch(1, 1, True, True)
+        + reduce_scratch((half, D), 2, False, True)
+        + reduce_scratch((half, D), 2, True, True) * 2
+        + reduce_scratch((half, D), 2, False, True)
         + ride_scratch(1),
         compiler_params=params(number),
         name="transformer",
     )(*args)
+
+
+def rows_at_once(shape):
+    size = math.prod(shape[1:-2] + tuple(-(-n // t) * t for n, t in zip(shape[-2:], (8, 128))))
+    if len(shape) == 2:
+        size = -(-shape[1] // 128) * 128
+    step = shape[0]
+    while step % 2 == 0 and step * size > 96 * 1024:
+        step //= 2
+    return step
+
+
+def total_kernel(shared, *refs):
+    count = len(shared)
+    grads, out_ref, held = (refs[:count], refs[count], refs[count + 1 : 2 * count + 1])
+    line, mine, tiles, send_sem, recv_sem, load_sem = refs[2 * count + 1 :]
+    at = Place(True)
+
+    def load(index):
+        return pltpu.make_async_copy(grads[index], held[index], load_sem.at[index])
+
+    for index in range(count):
+        load(index).start()
+    line[...] = jnp.zeros_like(line)
+    for index in range(count):
+        load(index).wait()
+        ref = held[index]
+        step = rows_at_once(ref.shape)
+
+        @pl.loop(0, ref.shape[0] // step)
+        def _(i):
+            part = ref[pl.ds(i * step, step)].astype(jnp.float32)
+            part = jnp.sum(part * part, axis=0, keepdims=len(ref.shape) == 2)
+            if len(ref.shape) == 3:
+                part = jnp.sum(part, axis=0, keepdims=True)
+            weight = 0.5 if shared[index] else 1.0
+            line[:, : ref.shape[-1]] += weight * part
+
+    mine[...] = jnp.broadcast_to(jnp.sum(line[...], axis=1, keepdims=True), mine.shape)
+    greet_all(at)
+    across = remote(mine, tiles.at[0], send_sem.at[0], recv_sem.at[0], (at.dp, 1 - at.core))
+    across.start()
+    across.wait()
+    mine[...] = mine[...] + tiles[0]
+    others = 4 * LAYERS - 1
+
+    def copy(step):
+        peer = (at.dp + step) % (4 * LAYERS)
+        return remote(
+            mine, tiles.at[step], send_sem.at[step], recv_sem.at[step], (peer, at.core)
+        )
+
+    @pl.loop(1, others + 1)
+    def _(step):
+        copy(step).start()
+
+    @pl.loop(1, others + 1)
+    def _(step):
+        copy(step).wait()
+
+    total = jnp.zeros_like(mine)
+    for chip in range(4 * LAYERS):
+        step = (at.dp - chip + 4 * LAYERS) % (4 * LAYERS)
+        total = total + jnp.where(step == 0, mine[...], tiles[step])
+    out_ref[...] = total
+
+
+def total_of_squares(number, grads, shared):
+    tile = (8, 128)
+    count = len(grads)
+    longest = max(grad.shape[-1] for grad in grads)
+    return pl.pallas_call(
+        functools.partial(total_kernel, shared),
+        out_shape=jax.ShapeDtypeStruct(tile, jnp.float32),
+        in_specs=[ANYWHERE] * count,
+        out_specs=IN_VMEM,
+        scratch_shapes=[pltpu.VMEM(grad.shape, grad.dtype) for grad in grads]
+        + [
+            pltpu.VMEM((1, longest), jnp.float32),
+            pltpu.VMEM(tile, jnp.float32),
+            pltpu.VMEM((16,) + tile, jnp.float32),
+            pltpu.SemaphoreType.DMA((16,)),
+            pltpu.SemaphoreType.DMA((16,)),
+            pltpu.SemaphoreType.DMA((count,)),
+        ],
+        compiler_params=params(number),
+        name="total",
+    )(*grads)
+
+
+def update_kernel(rates, *refs):
+    count = len(rates)
+    total, refs = (refs[0], refs[1:])
+    ins, outs = (refs[: 4 * count], refs[4 * count : 7 * count])
+    held, (load_sem, store_sem) = (refs[7 * count : 11 * count], refs[11 * count :])
+
+    def load(index):
+        return pltpu.make_async_copy(ins[index], held[index], load_sem.at[index])
+
+    for index in range(4 * count):
+        load(index).start()
+    factor = jnp.minimum(1.0, CLIP / (jnp.sqrt(total[0:1, 0:1]) + 1e-06))
+    correct_one = 1.0 / (1.0 - BETA_ONE**STEP)
+    correct_two = 1.0 / (1.0 - BETA_TWO**STEP)
+    for index, rate in enumerate(rates):
+        master, average, square, grad = held[4 * index : 4 * index + 4]
+        for part in range(4):
+            load(4 * index + part).wait()
+        step = rows_at_once(master.shape)
+
+        @pl.loop(0, master.shape[0] // step)
+        def _(i):
+            at = pl.ds(i * step, step)
+            clipped = grad[at].astype(jnp.float32) * factor
+            new_avg = BETA_ONE * average[at] + (1.0 - BETA_ONE) * clipped
+            new_sq = BETA_TWO * square[at] + (1.0 - BETA_TWO) * clipped * clipped
+            step_dir = new_avg * correct_one / (jnp.sqrt(new_sq * correct_two) + ADAM_EPS)
+            old = master[at]
+            master[at] = old - rate * (step_dir + DECAY * old)
+            average[at] = new_avg
+            square[at] = new_sq
+
+        for part in range(3):
+            pltpu.make_async_copy(
+                held[4 * index + part], outs[3 * index + part], store_sem.at[3 * index + part]
+            ).start()
+    for index in range(count):
+        for part in range(3):
+            pltpu.make_async_copy(
+                held[4 * index + part], outs[3 * index + part], store_sem.at[3 * index + part]
+            ).wait()
+
+
+def update(total, quads, rates):
+    count = len(quads)
+    flat = [array for quad in quads for array in quad]
+    return pl.pallas_call(
+        functools.partial(update_kernel, rates),
+        out_shape=[
+            jax.ShapeDtypeStruct(array.shape, array.dtype) for quad in quads for array in quad[:3]
+        ],
+        in_specs=[IN_VMEM] + [ANYWHERE] * (4 * count),
+        out_specs=[ANYWHERE] * (3 * count),
+        scratch_shapes=[pltpu.VMEM(array.shape, array.dtype) for array in flat]
+        + [pltpu.SemaphoreType.DMA((4 * count,)), pltpu.SemaphoreType.DMA((3 * count,))],
+        compiler_params=pltpu.CompilerParams(vmem_limit_bytes=VMEM_GRANT),
+        name="update",
+    )(total, *flat)
 
 
 def layer_stats(values):
@@ -2699,19 +2389,18 @@
     picks = half_picks(height, breadth)
     numbers = itertools.count()
 
-    def sum_all(local):
-        return total(next(numbers), jnp.full((8, 128), local))[0, 0]
+    stored_order = {3: lambda array: array.transpose(0, 1, 3, 2), 5: lambda array: array.transpose(1, 0, 2)}
 
     gain_bias = widen(lower(norm_params))
     conv_one = lower(first_conv).reshape(3, 3 * local_c, half_c)
-    conv_two = lower(second_conv).transpose(0, 2, 1, 3).reshape(3, half_c, 3 * local_c)
+    conv_two = lower(stored_order[3](second_conv)).reshape(3, 3 * local_c, half_c)
     conv_half = lower(down_conv).reshape(3, 3 * local_c, half_d)
     qkv_blocks = lower(qkv_proj).transpose(2, 0, 1, 3).reshape(heads_here, D // n_dp, 3 * HDIM)
 
     emb = widen(lower(embed_noise(t_index, FREQ))).reshape(n_dp, 1, freq_rows)
     emb = jnp.pad(emb, ((0, 0), (0, 7), (0, 128 - freq_rows)))
     image_blocks = images.reshape(positions, n_dp, local_c).transpose(1, 0, 2)
-    ada_half = lax.dynamic_slice_in_dim(ada_proj, tensor_pos * 3, 3, axis=1)
+    ada_half = lax.dynamic_slice_in_dim(stored_order[5](ada_proj), tensor_pos * 3, 3, axis=0)
     convs = (conv_one, conv_two, conv_half)
 
     pictures, emb, shrunk, act_two, taps_one, taps_half, middle, stats_one, mods, *heads = res_forward(
@@ -2722,8 +2411,8 @@
         *convs,
         picks,
         lower(resnet_mod).reshape(freq_rows, 2 * half_c),
-        lower(ada_half).reshape(freq_rows, 3 * D),
-        paired_lanes(image_blocks),
+        lower(ada_half),
+        paired_lanes(image_blocks).reshape(n_dp, 2, positions // 4, 2 * local_c),
         emb,
         qkv_blocks,
         lower(out_proj),
@@ -2772,26 +2461,37 @@
     images_grad = images_grad.transpose(1, 0, 2).reshape((1, height, breadth, C))
 
     emb_cols = emb[:, 0, :freq_rows]
-    grad_ada = widen(grad_ada).reshape(2, n_dp, 3 * D)
-    grad_ada = jnp.einsum("bf,cbk->fck", emb_cols, grad_ada, precision=HIGHEST)
+    grad_ada = widen(grad_ada).reshape(2, n_dp, 3, D)
+    grad_ada = jnp.einsum("bf,cbjk->cjfk", emb_cols, grad_ada, precision=HIGHEST)
     grad_res = jnp.einsum("bf,bk->fk", emb_cols, grad_res.reshape(n_dp, -1), precision=HIGHEST)
 
-    grad_qkv_w = widen(grad_qkv_w).reshape(heads_here, D // n_dp, 3, HDIM).transpose(1, 2, 0, 3)
-
-    combined_total = (
+    grad_qkv_w = grad_qkv_w.reshape(heads_here, D // n_dp, 3, HDIM).transpose(1, 2, 0, 3)
+    gradients = (
         grad_norm_params,
-        grad_conv_one.reshape(first_conv.shape),
+        grad_conv_one.reshape(9 * local_c, half_c),
         grad_res.reshape(resnet_mod.shape),
-        grad_conv_two.reshape(3, 3, local_c, half_c).transpose(0, 1, 3, 2),
-        grad_half.reshape(down_conv.shape),
-        grad_ada.reshape(ada_proj.shape),
-        grad_qkv_w,
-        widen(grad_out),
-        widen(grad_up),
-        widen(grad_down),
-    )
-    results = clipped_step(masters, averages, squares, combined_total, sum_all)
-    return (block_out[None], images_grad) + results
+        grad_conv_two.reshape(9 * local_c, half_c),
+        grad_half.reshape(9 * local_c, half_d),
+        grad_ada.reshape((6, freq_rows, D)),
+        grad_qkv_w.reshape(-1, HDIM),
+        grad_out.reshape(heads_here * HDIM, -1),
+        grad_up,
+        grad_down,
+    )
+    shared = tuple(position in (0, 5) for position in range(len(gradients)))
+    square_sum = total_of_squares(next(numbers), gradients, shared)
+    quads = []
+    for position, grad in enumerate(gradients):
+        order = stored_order.get(position, lambda array: array)
+        three = (masters[position], averages[position], squares[position])
+        quads.append(tuple(order(array).reshape(grad.shape) for array in three) + (grad,))
+    updated = update(square_sum, quads, learn_rates())
+    results = []
+    for position, array in enumerate(updated):
+        order = stored_order.get(position // 3, lambda array: array)
+        shape = jax.eval_shape(order, masters[position // 3]).shape
+        results.append(order(array.reshape(shape)))
+    return (block_out[None], images_grad, jnp.sqrt(square_sum[0, :1])) + tuple(results)
 
 
 def solution(mesh):

time: 762 us -> 683 us (0.90)
  other arithmetic: 60.1 us -> 9.36 us
  local copies, waits for them, and re-layouts: 41.5 us -> 22.2 us
    pallas_call x1 -> x2, Pallas kernels: 12.4 us -> 42.4 us  [the longest x1 27.4 us: update(): pl.pallas_call(functools.partial(update_kernel, rates), out_shape=[jax.Sh...]
    sub x10 -> x0, other arithmetic: 29.9 us -> none  [clipped_step(): new_master = master - learn_rate * (step_dir + DECAY * master)]
    unnamed x117 -> x28, local copies, waits for them, and re-layouts: 23.1 us -> 4.13 us
    pallas_call x1, Pallas kernels: 213 us -> 199 us  [res_forward(): pl.pallas_call(functools.partial(res_forward_kernel, breadth), out_shape=...]
    reduce_sum x8 -> x0, other arithmetic: 12.9 us -> none  [clipped_step(): shard_sq = jnp.sum(reduced * reduced)]
    pallas_call x1, Pallas kernels: 233 us -> 221 us  [transformer(): pl.pallas_call(transformer_kernel, out_shape=[jax.ShapeDtypeStruct((token...]
where the time goes in v3:
time: 683 us; the launch traced here: 682 us
  Pallas kernels  645 us (94%)
  local copies, waits for them, and re-layouts  22.2 us (3%)
  other arithmetic  9.36 us (1%)
    pallas_call x1, Pallas kernels, transformer(): pl.pallas_call(transformer_kernel, out_shape=[jax.ShapeDtypeStruct((token...  221 us
    pallas_call x1, Pallas kernels, res_forward(): pl.pallas_call(functools.partial(res_forward_kernel, breadth), out_shape=...  199 us
    pallas_call x1, Pallas kernels, res_backward(): pl.pallas_call(functools.partial(res_backward_kernel, breadth), out_shape...  183 us
    pallas_call x1, Pallas kernels, update(): pl.pallas_call(functools.partial(update_kernel, rates), out_shape=[jax.Sh...  27.4 us
    pallas_call x1, Pallas kernels, total_of_squares(): pl.pallas_call(functools.partial(total_kernel, shared), out_shape=jax.Sha...  15 us

profile of v3, /device:TPU:0, one launch (start us, length us, event | category | flops | bytes accessed | tf_op | source)
XLA Modules:
  0.0 682.0 jit_solution(18425194889149060053)
XLA Ops:
  0.7 1.7 fusion.2.ada_table
  2.4 1.8 reshape.336
  4.1 0.0 copy-start
  4.2 0.2 fusion.13
  4.3 0.3 pad_maximum_fusion
  4.6 0.0 copy-start.3
  4.7 0.9 copy.74
  6.4 0.1 cosine_convert_fusion
  6.4 0.1 convert_element_type.90
  6.5 0.7 pad_convert_fusion.emb_blocks
  7.2 0.0 copy-done
  7.2 1.2 convert_element_type.78
  8.4 0.9 convert_element_type.76
  9.3 0.9 bitcast_convert_fusion
  10.2 0.8 fusion.4.picks
  11.0 0.6 convert_convert_fusion.gain_bias
  11.5 1.8 copy.76
  13.4 1.2 copy.77.qkv_blocks
  14.5 1.1 convert_element_type.87.up_rows
  15.6 0.9 copy-done.2
  16.5 1.1 convert_element_type.88.down_columns
  17.6 0.1 copy-done.5
  17.6 0.7 convert_element_type.86.out_blocks
  18.4 0.6 copy.92
  19.0 199.0 %res_forward.1 = (bf16[16,256,64]{2,1,0:T(8,128)(2,1)}, f32[16,8,128]{2,1,0:T(8,128)}, f32[2,64,1024]{2,1,0:T(8,128)}, bf16[16,256,512]{2,1,0:T(8,128)(2,1)}, bf...) custom-call(f32[2,64]{1,0:T(2,128)} %convert_convert_fusion.gain_bia, ...), custom_call_target="tpu_custom_call" | custom-call | tf_op jit(solution)/shard_map/res_forward/pallas_call | solution.py:1383
  218.0 0.8 slice.27
  218.8 0.6 reshape.339.mods
  219.5 220.7 %transformer.1 = (bf16[64,2048]{1,0:T(8,128)(2,1)}, bf16[64,1024]{1,0:T(8,128)(2,1)}, f32[6,2048]{1,0:T(8,128)}, bf16[2048,384]{1,0:T(8,128)(2,1)}, bf16[128,204...) custom-call(f32[2,64,1024]{2,1,0:T(8,128)} %get-tuple-element.93.shrunk, ...), custom_call_target="tpu_custom_call" | custom-call | tf_op jit(solution)/shard_map/transformer/pallas_call | solution.py:2078
  440.2 0.8 convert_element_type.89
  441.0 0.7 reshape.342.ada_grad
  441.7 0.7 constant_dynamic-slice_fusion
  442.3 0.6 reshape.341.mods
  442.9 183.0 %res_backward.1 = (bf16[16,128,128]{2,1,0:T(8,128)(2,1)}, f32[2,64]{1,0:T(2,128)}, f32[16,8,128]{2,1,0:T(8,128)}, bf16[2,16,48,128]{3,2,1,0:T(8,128)(2,1)}, f32[...) custom-call(bf16[64,1024]{1,0:T(8,128)(2,1)} %get-tuple-element.100., ...), custom_call_target="tpu_custom_call" | custom-call | tf_op jit(solution)/shard_map/res_backward/pallas_call | solution.py:1754
  626.0 1.5 reshape.349
  627.5 0.8 slice.31
  628.3 1.6 fusion
  629.9 0.3 fusion.5
  630.2 0.7 copy.85.refs_2_.refs_12_
  630.9 0.4 copy.83
  631.3 1.3 copy.84
  632.6 15.0 %total.1.refs_0_ = f32[8,128]{1,0:T(8,128)} custom-call(f32[2,64]{1,0:T(2,128)} %get-tuple-element.112.refs_0_.refs_4_, f32[576,512]{1,0:T(8,128)} %bitcast.114, f32[16,2,512]{2,1,0:T(2,128)} %copy.85.refs_2_.refs_12_, f32[576,512]{1,0:T(8,128)} %bitcast.116, f32[576,1024]{1,0:T(8,128)} %bitcast.101, f32[6,16,2048]{2,1,0:T(8,128)} %bitcast.103, ...), custom_call_target="tpu_custom_call" | custom-call | tf_op jit(solution)/shard_map/total/pallas_call | solution.py:2175
  647.6 27.4 %update.1 = (f32[2,64]{1,0:T(2,128)}, f32[2,64]{1,0:T(2,128)}, f32[2,64]{1,0:T(2,128)}, f32[576,512]{1,0:T(8,128)}, f32[576,512]{1,0:T(8,128)}, /*index=5*/f32[5...) custom-call(f32[8,128]{1,0:T(8,128)} %total.1.refs_0_, ...), custom_call_target="tpu_custom_call" | custom-call | tf_op jit(solution)/shard_map/update/pallas_call | solution.py:2240
  675.0 1.2 slice.32
  676.9 0.2 fusion.14
  677.1 0.2 convert_bitcast_fusion
  677.4 1.2 copy.78
  678.6 1.5 reshape.385
  680.1 0.7 copy.104
  (24 shorter events, 0.1 us)
Async XLA Ops:
  4.1 3.0 copy-start
  4.6 3.8 copy-start.3
  7.2 2.1 copy-start.4
  8.4 2.6 copy-start.11
  10.2 4.4 copy-start.1
  14.5 2.0 copy-start.2
  16.5 1.1 copy-start.5
  16.5 1.9 copy-start.8
  626.0 3.9 copy-start.10
  626.0 4.9 copy-start.7
  647.6 29.3 %copy-start.6 = (bf16[16,128,128]{2,1,0:T(8,128)(2,1)S(1)}, bf16[16,128,128]{2,1,0:T(8,128)(2,1)}, u32[]{:S(2)}) copy-start(bf16[16,128,128]{2,1,0:T(8,128)(2,1)} %get-tuple-element.111) | copy-start | bytes 1572868
  678.6 1.5 copy-start.9

commit v4 on v3

--- a/solution.py
+++ b/solution.py
@@ -1904,11 +1904,17 @@
 
     gather_stage(near, [attn_in], None, 2, *gather_one[:2], gather_one[2:], tick=in_gather)
 
+    def four_images(i):
+        return pl.ds(pl.multiple_of(i * 4 * tokens_len, 4 * tokens_len), 4 * tokens_len)
+
+    @pl.loop(0, images // 8)
+    def _(i):
+        rows_in = attn_in[pl.ds(4 * i, 4)].reshape(4 * tokens_len, D)
+        qkv[four_images(i)] = dot(rows_in, qkv_head[...]).astype(low)
+
     @pl.loop(0, images // 2)
     def _(i):
-        rows_in = attn_in[i].reshape(tokens_len, D)
-        low_qkv = dot(rows_in, qkv_head[...]).astype(low)
-        qkv[image_rows(i)] = low_qkv
+        low_qkv = qkv[image_rows(i)]
         query, key, value = (low_qkv[:, j * HDIM : (j + 1) * HDIM] for j in range(3))
         scores = dot_nt(query, key) * score_scale
         scores = scores - jnp.max(scores, axis=1, keepdims=True)
@@ -1990,9 +1996,14 @@
     attended[...] = grad_after
     gather_stage(near, [attended_grad], None, 2, *gather_three[:2], gather_three[2:])
 
+    @pl.loop(0, images // 8)
+    def _(i):
+        rows_in = attended_grad[pl.ds(4 * i, 4)].reshape(4 * tokens_len, D)
+        mixed_grad[four_images(i)] = dot_nt(rows_in, out_head[...]).astype(low)
+
     @pl.loop(0, images // 2)
     def _(i):
-        grad = dot_nt(attended_grad[i].reshape(tokens_len, D), out_head[...]).astype(low)
+        grad = mixed_grad[image_rows(i)]
         low_qkv = qkv[image_rows(i)]
         query, key, value = (low_qkv[:, j * HDIM : (j + 1) * HDIM] for j in range(3))
         weight = probs[i]

time: 683 us -> 679 us (level)
  no operation moved by 1% of the time
where the time goes in v4:
time: 679 us
  Pallas kernels  642 us (95%)
  local copies, waits for them, and re-layouts  22.2 us (3%)
  other arithmetic  9.36 us (1%)
    pallas_call x1, Pallas kernels, transformer(): pl.pallas_call(transformer_kernel, out_shape=[jax.ShapeDtypeStruct((token...  218 us
    pallas_call x1, Pallas kernels, res_forward(): pl.pallas_call(functools.partial(res_forward_kernel, breadth), out_shape=...  199 us
    pallas_call x1, Pallas kernels, res_backward(): pl.pallas_call(functools.partial(res_backward_kernel, breadth), out_shape...  183 us
    pallas_call x1, Pallas kernels, update(): pl.pallas_call(functools.partial(update_kernel, rates), out_shape=[jax.Sh...  27.4 us
    pallas_call x1, Pallas kernels, total_of_squares(): pl.pallas_call(functools.partial(total_kernel, shared), out_shape=jax.Sha...  15 us

profile of v4, /device:TPU:0, one launch (start us, length us, event | category | flops | bytes accessed | tf_op | source)
XLA Modules:
  0.0 678.7 jit_solution(11876209306970706487)
XLA Ops:
  0.7 1.7 fusion.2.ada_table
  2.4 1.8 reshape.336
  4.1 0.0 copy-start
  4.2 0.2 fusion.13
  4.3 0.3 pad_maximum_fusion
  4.6 0.0 copy-start.3
  4.7 0.9 copy.74
  6.4 0.1 cosine_convert_fusion
  6.4 0.1 convert_element_type.90
  6.5 0.7 pad_convert_fusion.emb_blocks
  7.2 1.2 convert_element_type.78
  8.4 0.9 convert_element_type.76
  9.3 0.9 bitcast_convert_fusion
  10.2 0.8 fusion.4.picks
  11.0 0.6 convert_convert_fusion.gain_bias
  11.5 1.8 copy.76
  13.4 1.2 copy.77.qkv_blocks
  14.5 1.1 convert_element_type.87.up_rows
  15.6 0.9 copy-done.2
  16.5 1.1 convert_element_type.88.down_columns
  17.6 0.1 copy-done.5
  17.6 0.7 convert_element_type.86.out_blocks
  18.4 0.6 copy.92
  19.0 199.0 %res_forward.1 = (bf16[16,256,64]{2,1,0:T(8,128)(2,1)}, f32[16,8,128]{2,1,0:T(8,128)}, f32[2,64,1024]{2,1,0:T(8,128)}, bf16[16,256,512]{2,1,0:T(8,128)(2,1)}, bf...) custom-call(f32[2,64]{1,0:T(2,128)} %convert_convert_fusion.gain_bia, ...), custom_call_target="tpu_custom_call" | custom-call | tf_op jit(solution)/shard_map/res_forward/pallas_call | solution.py:1383
  218.0 0.8 slice.27
  218.8 0.6 reshape.339.mods
  219.5 217.9 %transformer.1 = (bf16[64,2048]{1,0:T(8,128)(2,1)}, bf16[64,1024]{1,0:T(8,128)(2,1)}, f32[6,2048]{1,0:T(8,128)}, bf16[2048,384]{1,0:T(8,128)(2,1)}, bf16[128,204...) custom-call(f32[2,64,1024]{2,1,0:T(8,128)} %get-tuple-element.93.shrunk, ...), custom_call_target="tpu_custom_call" | custom-call | tf_op jit(solution)/shard_map/transformer/pallas_call | solution.py:2089
  437.3 0.8 convert_element_type.89
  438.2 0.7 reshape.342.ada_grad
  438.8 0.7 constant_dynamic-slice_fusion
  439.5 0.6 reshape.341.mods
  440.1 182.6 %res_backward.1 = (bf16[16,128,128]{2,1,0:T(8,128)(2,1)}, f32[2,64]{1,0:T(2,128)}, f32[16,8,128]{2,1,0:T(8,128)}, bf16[2,16,48,128]{3,2,1,0:T(8,128)(2,1)}, f32[...) custom-call(bf16[64,1024]{1,0:T(8,128)(2,1)} %get-tuple-element.100., ...), custom_call_target="tpu_custom_call" | custom-call | tf_op jit(solution)/shard_map/res_backward/pallas_call | solution.py:1754
  622.7 1.5 reshape.349
  624.2 0.8 slice.31
  625.1 1.6 fusion
  626.6 0.0 copy-done.10
  626.7 0.3 fusion.5
  626.9 0.7 copy.85.refs_2_.refs_12_
  627.6 0.4 copy.83
  628.0 1.3 copy.84
  629.3 15.0 %total.1.refs_0_ = f32[8,128]{1,0:T(8,128)} custom-call(f32[2,64]{1,0:T(2,128)} %get-tuple-element.112.refs_0_.refs_4_, f32[576,512]{1,0:T(8,128)} %bitcast.114, f32[16,2,512]{2,1,0:T(2,128)} %copy.85.refs_2_.refs_12_, f32[576,512]{1,0:T(8,128)} %bitcast.116, f32[576,1024]{1,0:T(8,128)} %bitcast.101, f32[6,16,2048]{2,1,0:T(8,128)} %bitcast.103, ...), custom_call_target="tpu_custom_call" | custom-call | tf_op jit(solution)/shard_map/total/pallas_call | solution.py:2186
  644.3 27.4 %update.1 = (f32[2,64]{1,0:T(2,128)}, f32[2,64]{1,0:T(2,128)}, f32[2,64]{1,0:T(2,128)}, f32[576,512]{1,0:T(8,128)}, f32[576,512]{1,0:T(8,128)}, /*index=5*/f32[5...) custom-call(f32[8,128]{1,0:T(8,128)} %total.1.refs_0_, ...), custom_call_target="tpu_custom_call" | custom-call | tf_op jit(solution)/shard_map/update/pallas_call | solution.py:2251
  671.7 1.2 slice.32
  673.6 0.2 fusion.14
  673.9 0.2 convert_bitcast_fusion
  674.1 1.2 copy.78
  675.3 1.5 reshape.385
  676.8 0.7 copy.104
  (24 shorter events, 0.1 us)
Async XLA Ops:
  4.1 3.0 copy-start
  4.6 3.8 copy-start.3
  7.2 2.1 copy-start.4
  8.4 2.6 copy-start.11
  10.2 4.4 copy-start.1
  14.5 2.0 copy-start.2
  16.5 1.1 copy-start.5
  16.5 1.9 copy-start.8
  622.7 3.9 copy-start.10
  622.7 4.9 copy-start.7
  644.3 29.3 %copy-start.6 = (bf16[16,128,128]{2,1,0:T(8,128)(2,1)S(1)}, bf16[16,128,128]{2,1,0:T(8,128)(2,1)}, u32[]{:S(2)}) copy-start(bf16[16,128,128]{2,1,0:T(8,128)(2,1)} %get-tuple-element.111) | copy-start | bytes 1572868
  675.3 1.5 copy-start.9
